TPU v7x, 32 devices: a whole 2x2x4 slice. The times are simulated.
32 devices in a mesh: tm: 4 (over y, core), height: 4 (over z), dp: 2 (over x).
Axes of the slice: x: 2, y: 2, z: 4, core: 2. Of those that a mesh axis runs over, the one named last changes fastest.
Arguments:
- queries: bfloat16 [4, 4, 4, 1, 192, 128], P('tm', 'height', 'dp'), may hold values from -4.5 to 4.5
- keys: bfloat16 [4, 4, 4, 1, 192, 128], P('tm', 'height', 'dp'), may hold values from -4.5 to 4.5
- values: bfloat16 [4, 4, 4, 1, 192, 128], P('tm', 'height', 'dp'), may hold values from -6 to 6
- grad_out: bfloat16 [4, 4, 4, 1, 192, 128], P('tm', 'height', 'dp'), may hold values from -24 to 24
- attn_out: bfloat16 [4, 4, 4, 1, 192, 128], P('tm', 'height', 'dp'), may hold values from -1.796875 to 1.796875
- window_mask: int32 [4, 4, 1, 27], P('tm', 'height'), may hold values 0 or 1
Outputs:
- grad_queries: bfloat16 [4, 4, 4, 1, 192, 128], P('tm', 'height', 'dp')
- grad_keys: bfloat16 [4, 4, 4, 1, 192, 128], P('tm', 'height', 'dp')
- grad_values: bfloat16 [4, 4, 4, 1, 192, 128], P('tm', 'height', 'dp')
All inputs are finite; a program needn't handle non-finite values. No bound on the sum of `window_mask` on one device may be relied on, other than what follows from the above.
Results may differ from a plain program's by a relative error of at most 0.009.
Values may be sent and summed in bfloat16 or wider, within the bound.
No kernel may reach another device: no remote copies, remote signals or barrier semaphores. Data moves between devices by JAX's collectives and lax.ppermute only.
A program may use at most 64 MiB of HBM per device.

v0:
```python
import functools

import jax
import jax.numpy as jnp
from jax import lax
from jax.experimental import pallas as pl
from jax.experimental.pallas import tpu as pltpu
from jax.sharding import PartitionSpec as P

VMEM = pl.BlockSpec(memory_space=pltpu.VMEM)
HBM = pl.BlockSpec(memory_space=pltpu.HBM)
LIMIT = pltpu.CompilerParams(vmem_limit_bytes=32 * 1024 * 1024)
ROWS_T = (((1,), (1,)), ((), ()))
COLS_T = (((0,), (0,)), ((), ()))


def dot(a, b, dims=(((1,), (0,)), ((), ()))):
    return lax.dot_general(a, b, dims, preferred_element_type=jnp.float32)


LATE, EARLY = 0, 1


def place():
    t = lax.axis_index("tm")
    return t // 2, t % 2, lax.axis_index("height")


def head_at():
    y, c, z = place()
    return (c + y + z) % 2


def pair(index, which):
    rising = (index % 2) == (0 if which == 0 else 1)
    return rising, jnp.where(rising, index + 1, index - 1)


def within(index, size):
    return (index >= 0) & (index < size)


def pack_kernel(tok, k_ref, v_ref, q_ref, g_ref, o_ref, mask_ref, kv_ref, rest_ref, other_ref, flags, sems):
    head = head_at()
    copies = [pltpu.make_async_copy(mask_ref, flags, sems.at[10])]
    for i, ref in enumerate((k_ref, v_ref, q_ref, g_ref, o_ref)):
        own = (kv_ref if i < 2 else rest_ref).at[pl.ds((i if i < 2 else i - 2) * tok, tok), :]
        copies.append(pltpu.make_async_copy(ref.at[0, 0, head, 0], own, sems.at[2 * i + 1]))
        copies.append(
            pltpu.make_async_copy(ref.at[0, 0, 1 - head, 0], other_ref.at[pl.ds(i * tok, tok), :], sems.at[2 * i])
        )
    for copy in copies:
        copy.start()
    copies[0].wait()
    row = lax.broadcasted_iota(jnp.int32, (16, rest_ref.shape[1]), 0)
    spread = jnp.zeros(row.shape, jnp.float32)
    for i in range(9):
        on = (flags[0, 0, 0, 9 * (i // 3) + 3 * (i % 3) + 1] != 0).astype(jnp.float32)
        spread = jnp.where(row == i, on, spread)
    rest_ref[pl.ds(3 * tok, 16), :] = spread.astype(jnp.bfloat16)
    other_ref[pl.ds(5 * tok, 16), :] = spread.astype(jnp.bfloat16)
    for copy in copies[1:]:
        copy.wait()


def rows_at(index, tok):
    return pl.ds(index * tok, tok)


def border_is_own(y, c):
    rising, _ = pair(y, 0)
    return (c == 1) == rising


def pick(near, which, own, par):
    return jnp.where(near, own, par) if which == 0 else jnp.where(near, par, own)


def three_terms(row):
    terms = []
    for _ in range(3):
        terms.append(row.astype(jnp.bfloat16).astype(jnp.float32))
        row = row - terms[-1]
    return terms


def line_kernel(tok, rest_ref, par_ref, par_kv_ref, *border_refs):
    y, c, _ = place()
    near = border_is_own(y, c)
    for i in range(2):
        par_kv_ref[rows_at(i, tok), :] = par_ref[rows_at(i, tok), :]
    width = par_ref.shape[1]
    f32 = jnp.float32
    q, g, o = (
        [pick(near, which, rest_ref[rows_at(i, tok), :], par_ref[rows_at(i + 2, tok), :]) for which in range(2)]
        for i in range(3)
    )
    own_flags, par_flags = rest_ref[pl.ds(3 * tok, 16), :].astype(f32), par_ref[pl.ds(5 * tok, 16), :].astype(f32)
    flags = [pick(near, which, own_flags, par_flags)[0:9] for which in range(2)]
    product = jnp.concatenate(g, axis=0).astype(f32) * jnp.concatenate(o, axis=0).astype(f32)
    terms = [
        [term[:, start : start + width] for start in range(0, 2 * tok, width)]
        for term in three_terms(jnp.sum(product.T, axis=0, keepdims=True))
    ]
    for which, ref in enumerate(border_refs):
        ref[rows_at(0, tok), :], ref[rows_at(1, tok), :] = q[which], g[which]
        part = slice(0, 2) if which == 0 else slice(len(terms[0]) - 2, None)
        lines = [flags[which]] + [row for term in terms for row in term[part]] + [jnp.zeros((1, width), f32)]
        ref[pl.ds(2 * tok, 16), :] = jnp.concatenate(lines, axis=0).astype(jnp.bfloat16)
    lines = flags + [row for term in terms for row in term] + [jnp.zeros((5, width), f32)]
    par_kv_ref[pl.ds(2 * tok, 32), :] = jnp.concatenate(lines, axis=0).astype(jnp.bfloat16)


def foreign_delta(ref, tok):
    terms = ref[pl.ds(2 * tok, 16), :].astype(jnp.float32)
    return jnp.concatenate(
        [sum(terms[9 + 2 * i + half : 10 + 2 * i + half] for i in range(3)) for half in range(2)], axis=1
    )


def line_place(z, line, heights):
    if line == 0:
        return True, lambda flags, dt: flags[3 * dt + 1 : 3 * dt + 2]
    rising, at = pair(z, line - 1)
    return within(at, heights), lambda flags, dt: jnp.where(
        rising, flags[3 * dt + 2 : 3 * dt + 3], flags[3 * dt : 3 * dt + 1]
    )


def lanes_of(tok, border, other):
    width = border.shape[1]
    lane = lax.broadcasted_iota(jnp.int32, (1, width), 1)
    return jnp.concatenate(
        [jnp.where(lane + start < tok, border, other) for start in range(0, 2 * tok, width)], axis=1
    )


def flag_row(tok, slot, at, own_flags, par_flags, own_query):
    y, c, _ = place()
    first, near = c == 0, border_is_own(y, c)
    if slot == 0:
        own, par = at(own_flags, 1), jnp.where(first, at(par_flags, 0), at(par_flags, 2))
    else:
        own, par = jnp.where(first, at(own_flags, 2), at(own_flags, 0)), at(par_flags, 1)
    if own_query:
        centre = jnp.ones_like(own)
        own, par = (centre, par) if slot == 0 else (own, centre)
    return lanes_of(tok, pick(near, 0, own, par), pick(near, 1, own, par))


def first_kernel(tok, heights, scale, kv_ref, par_kv_ref, rest_ref, par_ref, q_all, g_all, table, s_ref, d_ref):
    qg = (q_all, g_all)
    y, c, z = place()
    two = 2 * tok
    width = rest_ref.shape[1]
    f32 = jnp.float32
    near = border_is_own(y, c)
    out = []
    for part in range(3):
        own, par = rest_ref[rows_at(part, tok), :], par_ref[rows_at(part + 2, tok), :]
        tiles = [pick(near, which, own, par) for which in range(2)]
        if part == 2:
            out = jnp.concatenate(tiles, axis=0)
        else:
            for which in range(2):
                qg[part][rows_at(which, tok), :] = tiles[which]
    delta = jnp.sum((qg[1][...].astype(f32) * out.astype(f32)).T, axis=0, keepdims=True)

    own_flags = rest_ref[pl.ds(3 * tok, 16), :].astype(f32)
    par_flags = par_ref[pl.ds(5 * tok, 16), :].astype(f32)
    lines = []
    for line in range(3):
        inside, at = line_place(z, line, heights)
        for slot in range(2):
            row = flag_row(tok, slot, at, own_flags, par_flags, line == 0)
            lines.append(jnp.where(inside, (row - 1.0) * 1e30, -1e30))
    table[...] = jnp.concatenate(lines + [delta, jnp.zeros((1, two), f32)], axis=0)
    for i, source in enumerate((kv_ref, par_kv_ref)):
        rows = rows_at(i, tok)
        s_ref[rows, :] = dot(source[rows_at(0, tok), :], qg[0][...], ROWS_T) * scale + table[i : i + 1, :]
        d_ref[rows, :] = dot(source[rows_at(1, tok), :], qg[1][...], ROWS_T) - table[6:7, :]


def largest(tok, blocks):
    lanes = blocks[0][0].shape[1]
    top = jnp.full((8, lanes), -1e30, jnp.float32)
    for ref, i in blocks:
        top = jnp.maximum(top, jnp.max(ref[rows_at(i, tok), :].reshape(tok // 8, 8, lanes), axis=0))
    return jnp.max(top, axis=0, keepdims=True)


def summed(tok, blocks, top):
    lanes = blocks[0][0].shape[1]
    total = jnp.zeros((8, lanes), jnp.float32)
    for ref, i in blocks:
        weights = jnp.exp(ref[rows_at(i, tok), :] - top)
        total = total + jnp.sum(weights.reshape(tok // 8, 8, lanes), axis=0)
    return jnp.sum(total, axis=0, keepdims=True)


def early_kernel(tok, scale, q_all, g_all, table, s_own, one_ref, two_ref, s_ref, d_ref, part_ref):
    qg = (q_all, g_all)
    for i, source in enumerate((one_ref, two_ref)):
        rows = rows_at(i, tok)
        s_ref[rows, :] = dot(source[rows_at(0, tok), :], qg[0][...], ROWS_T) * scale + table[2 + 2 * i + EARLY : 3 + 2 * i + EARLY, :]
        d_ref[rows, :] = dot(source[rows_at(1, tok), :], qg[1][...], ROWS_T) - table[6:7, :]
    blocks = [(ref, i) for ref in (s_own, s_ref) for i in range(2)]
    top = largest(tok, blocks)
    total = summed(tok, blocks, top)
    part_ref[...] = jnp.concatenate([top, total, jnp.zeros((6, 2 * tok), jnp.float32)], axis=0)


def foreign_rows(ref, part, which, tok):
    block = ref[rows_at(part, tok), :]
    gap = jnp.zeros((2 * block.shape[1] - tok, block.shape[1]), block.dtype)
    return jnp.concatenate([block, gap] if which == 0 else [gap, block], axis=0)


def foreign_lanes(which, tok, width):
    return slice(0, 2 * width) if which == 0 else slice(2 * tok - 2 * width, 2 * tok)


def far_row(tok, which, row):
    lane, width = lax.broadcasted_iota(jnp.int32, row.shape, 1), row.shape[1]
    return jnp.concatenate(
        [
            jnp.where(lane + start < tok if which == 0 else lane + start >= 2 * width - tok, row, 0.0)
            for start in (0, width)
        ],
        axis=1,
    )


def to_lanes(which, tok, row, fill):
    gap = jnp.full((1, 2 * tok - row.shape[1]), fill, jnp.float32)
    return jnp.concatenate([row, gap] if which == 0 else [gap, row], axis=1)


def score_kernel(tok, chips, heights, sides, scale, q_all, g_all, table, part, *refs):
    qg = (q_all, g_all)
    keys, foreign, refs = refs[:6], refs[6 : 6 + sides], refs[6 + sides :]
    s_late, s_far, *notes = refs
    y, c, z = place()
    near = border_is_own(y, c)
    two = 2 * tok
    f32 = jnp.float32
    far = []
    for which in range(sides):
        rising, y_at = pair(y, which)
        flags = foreign[which][pl.ds(2 * tok, 16), :].astype(f32)
        queries = foreign_rows(foreign[which], 0, which, tok)
        for line in range(3):
            inside, at = line_place(z, line, heights)
            row = far_row(tok, which, jnp.where(rising, at(flags, 0), at(flags, 2)))
            bias = jnp.where(inside & within(y_at, chips), (row - 1.0) * 1e30, -1e30)
            border = pick(near, which, keys[2 * line][rows_at(0, tok), :], keys[2 * line + 1][rows_at(0, tok), :])
            s_far[rows_at(3 * which + line, tok), :] = dot(border, queries, ROWS_T) * scale + bias
        blocks = [(s_far, 3 * which + line) for line in range(3)]
        top = largest(tok, blocks)
        far.append([to_lanes(which, tok, top, -1e30), to_lanes(which, tok, summed(tok, blocks, top), 0.0)])
    for i in range(2):
        at = 2 + 2 * i + LATE
        scores = dot(keys[at][rows_at(0, tok), :], qg[0][...], ROWS_T) * scale
        s_late[rows_at(i, tok), :] = scores + table[at : at + 1, :]
    blocks = [(s_late, i) for i in range(2)]
    top = jnp.maximum(part[0:1, :], largest(tok, blocks))
    total = part[1:2, :] * jnp.exp(part[0:1, :] - top) + summed(tok, blocks, top)
    for which in range(sides):
        notes[which][...] = jnp.concatenate([top, total] + far[which] + [jnp.zeros((4, two), f32)], axis=0)


def middle_kernel(tok, sides, scale, q_all, g_all, table, s_own, d_own, s_early, d_early, s_late, s_far, *refs):
    qg = (q_all, g_all)
    tiles, foreign, sent = refs[:6], refs[6 : 6 + sides], refs[6 + sides : 6 + 2 * sides]
    e_ref, ds_ref, e_far, ds_far, dq_ref, *far_dq = refs[6 + 2 * sides :]
    y, c, _ = place()
    near = border_is_own(y, c)
    f32, bf16 = jnp.float32, jnp.bfloat16
    dq = jnp.zeros(dq_ref.shape, f32)
    for line in range(3):
        for slot in range(2):
            i, at = 2 * line + slot, rows_at(line - 1 if line else slot, tok)
            scores = s_own if line == 0 else s_early if slot == EARLY else s_late
            weights = jnp.exp(scores[at, :] - sent[0][0:1, :])
            if line and slot == LATE:
                grads = dot(tiles[i][rows_at(1, tok), :], qg[1][...], ROWS_T) - table[6:7, :]
            else:
                grads = (d_early if line else d_own)[at, :]
            low = (weights * grads * scale).astype(bf16)
            if line == 0:
                e_ref[rows_at(i, tok), :] = weights.astype(bf16)
                ds_ref[rows_at(i, tok), :] = low
            dq = dq + dot(tiles[i][rows_at(0, tok), :], low, COLS_T)
    dq_ref[...] = dq
    for which in range(sides):
        far_g = foreign_rows(foreign[which], 1, which, tok)
        delta = foreign_delta(foreign[which], tok)
        lanes = foreign_lanes(which, tok, qg[0].shape[1])
        dq = jnp.zeros(far_dq[which].shape, f32)
        for line in range(3):
            rows = rows_at(3 * which + line, tok)
            own, par = tiles[2 * line], tiles[2 * line + 1]
            key, value = (pick(near, which, own[rows_at(i, tok), :], par[rows_at(i, tok), :]) for i in range(2))
            weights = jnp.exp(s_far[rows, :] - sent[which][2:3, lanes])
            low = (weights * (dot(value, far_g, ROWS_T) - delta) * scale).astype(bf16)
            if line == 0:
                e_far[rows_at(which, tok), :] = weights.astype(bf16)
                ds_far[rows_at(which, tok), :] = low
            dq = dq + dot(key, low, COLS_T)
        far_dq[which][...] = dq


def total_kernel(tok, chips, sides, *refs):
    far_dq, sent, came = (refs[i * sides : (i + 1) * sides] for i in range(3))
    note_ref, *shares = refs[3 * sides :]
    y, _, _ = place()
    width = far_dq[0].shape[0]

    def log_total(top, total, other_top, other_total):
        both = jnp.maximum(top, other_top)
        return both + jnp.log(total * jnp.exp(top - both) + other_total * jnp.exp(other_top - both))

    lse, far_rows = None, []
    for which in range(sides):
        _, y_at = pair(y, which)
        inside = within(y_at, chips)
        note = came[which]
        far_lse = log_total(note[0:1, :], note[1:2, :], sent[which][2:3, :], sent[which][3:4, :])
        far_lse = jnp.where(inside, far_lse, 0.0)
        far_rows.append(far_lse)
        lanes = foreign_lanes(which, tok, width)
        factor = jnp.where(inside, jnp.exp(sent[which][2:3, lanes] - far_lse[:, lanes]), 0.0)
        share = (far_dq[which][...] * factor).T
        shares[which][...] = (share[:tok] if which == 0 else share[2 * width - tok :]).astype(jnp.bfloat16)
        other = jnp.where(inside, note[2:3, :], -1e30), jnp.where(inside, note[3:4, :], 0.0)
        if which == 0:
            lse = log_total(sent[0][0:1, :], sent[0][1:2, :], *other)
        else:
            lse = log_total(lse, jnp.ones_like(lse), *other)
    rows = [lse] + far_rows
    note_ref[...] = jnp.concatenate(rows + [jnp.zeros((8 - len(rows), 2 * tok), jnp.float32)], axis=0)


def line_query_kernel(tok, chips, heights, sides, scale, kv_ref, par_kv_ref, *refs):
    queries, grads_in, extras = refs[:2], refs[2:4], refs[4:6]
    foreign, outs = refs[6 : 6 + 2 * sides], refs[6 + 2 * sides :]
    e_ref, ds_ref, e_far, ds_far, top_ref = outs
    y, c, z = place()
    near = border_is_own(y, c)
    two = 2 * tok
    width = kv_ref.shape[1]
    f32, bf16 = jnp.float32, jnp.bfloat16
    tops, far_tops = [], []
    tiles = (kv_ref, par_kv_ref)
    for line in (1, 2):
        rising, z_at = pair(z, line - 1)
        inside = within(z_at, heights)

        def at(flags, dt):
            return jnp.where(rising, flags[3 * dt : 3 * dt + 1], flags[3 * dt + 2 : 3 * dt + 3])

        rows = extras[line - 1][pl.ds(2 * tok, 32), :].astype(f32)
        own_flags, par_flags = (pick(near, which, rows[0:9], rows[9:18]) for which in range(2))
        delta = [sum(rows[18 + 3 * i + part : 19 + 3 * i + part] for i in range(3)) for part in range(two // width)]
        delta = jnp.concatenate(delta, axis=1)
        line_q, line_g = queries[line - 1][...], grads_in[line - 1][...]
        scores = []
        for slot in range(2):
            row = flag_row(tok, slot, at, own_flags, par_flags, False)
            bias = jnp.where(inside, (row - 1.0) * 1e30, -1e30)
            scores.append(dot(tiles[slot][rows_at(0, tok), :], line_q, ROWS_T) * scale + bias)
        top = jnp.maximum(*(jnp.max(block, axis=0, keepdims=True) for block in scores))
        tops.append(top)
        for slot in range(2):
            weights = jnp.exp(scores[slot] - top)
            grads = dot(tiles[slot][rows_at(1, tok), :], line_g, ROWS_T) - delta
            kept = rows_at(2 * (line - 1) + slot, tok)
            e_ref[kept, :] = weights.astype(bf16)
            ds_ref[kept, :] = (weights * grads * scale).astype(bf16)
        for which in range(sides):
            ref = foreign[2 * which + line - 1]
            y_rising, y_at = pair(y, which)
            flags = ref[pl.ds(2 * tok, 16), :].astype(f32)
            row = far_row(tok, which, jnp.where(y_rising, at(flags, 0), at(flags, 2)))
            bias = jnp.where(inside & within(y_at, chips), (row - 1.0) * 1e30, -1e30)
            key, value = (pick(near, which, *(tile[rows_at(i, tok), :] for tile in tiles)) for i in range(2))
            far_q, far_g = (foreign_rows(ref, part, which, tok) for part in range(2))
            block = dot(key, far_q, ROWS_T) * scale + bias
            top = jnp.max(block, axis=0, keepdims=True)
            far_tops.append(to_lanes(which, tok, top, -1e30))
            weights = jnp.exp(block - top)
            grads = dot(value, far_g, ROWS_T) - foreign_delta(ref, tok)
            kept = rows_at(2 * which + line - 1, tok)
            e_far[kept, :] = weights.astype(bf16)
            ds_far[kept, :] = (weights * grads * scale).astype(bf16)
    top_ref[...] = jnp.concatenate(tops + far_tops + [jnp.zeros((6 - 2 * sides, two), f32)], axis=0)


def times(block, factor):
    column = jnp.broadcast_to(factor, (block.shape[1], factor.shape[1])).T
    return (block.astype(jnp.float32) * column).astype(jnp.bfloat16)


def key_sums(tok, near, line, e_ref, ds_ref, scaled, far):
    rows = [rows_at(2 * line + slot, tok) for slot in range(2)]
    sums = [[dot(ref[at, :], scaled[i]) for i, ref in enumerate((ds_ref, e_ref))] for at in rows]
    for which, (e_far, ds_far, at, far_scaled) in enumerate(far):
        for i, ref in enumerate((ds_far, e_far)):
            block = dot(ref[at, :], far_scaled[i])
            for slot in range(2):
                sums[slot][i] = sums[slot][i] + jnp.where(near == ((slot == 0) == (which == 0)), block, 0.0)
    return sums


def stay_kernel(tok, chips, sides, q_all, g_all, e_ref, ds_ref, e_far, ds_far, raw_dq, note, *refs):
    qg = (q_all, g_all)
    sent, foreign, (own_ref, dq_ref) = refs[:sides], refs[sides : 2 * sides], refs[2 * sides :]
    y, c, _ = place()
    near = border_is_own(y, c)
    width = qg[0].shape[1]
    factor = jnp.exp(sent[0][0:1, :] - note[0:1, :])
    dq_ref[...] = (raw_dq[...] * factor).T
    far = []
    for which in range(sides):
        _, y_at = pair(y, which)
        lanes = foreign_lanes(which, tok, width)
        far_factor = jnp.exp(sent[which][2:3, lanes] - note[1 + which : 2 + which, lanes])
        far_factor = jnp.where(within(y_at, chips), far_factor, 0.0)
        scaled = [times(foreign_rows(foreign[which], part, which, tok), far_factor) for part in range(2)]
        far.append((e_far, ds_far, rows_at(which, tok), scaled))
    sums = key_sums(tok, near, 0, e_ref, ds_ref, [times(qg[part][...], factor) for part in range(2)], far)
    for slot in range(2):
        for i in range(2):
            own_ref[i, rows_at(slot, tok), :] = sums[slot][i]


def leave_kernel(tok, chips, sides, own_ref, dq_ref, e_ref, ds_ref, e_far, ds_far, top_ref, *refs):
    queries, refs = (refs[0:2], refs[2:4]), refs[4:]
    foreign, notes, backs = refs[: 2 * sides], refs[2 * sides : 2 + 2 * sides], refs[2 + 2 * sides : 2 + 3 * sides]
    mine_ref, mine_q_ref, swap_ref = refs[2 + 3 * sides :]
    y, c, _ = place()
    near = border_is_own(y, c)
    f32, bf16 = jnp.float32, jnp.bfloat16
    width = dq_ref.shape[1]
    sums = [[own_ref[i, rows_at(slot, tok), :] for i in range(2)] for slot in range(2)]
    for line in (1, 2):
        note = notes[line - 1]
        factor = jnp.exp(top_ref[line - 1 : line, :] - note[0:1, :])
        scaled = [times(queries[part][line - 1][...], factor) for part in range(2)]
        far = []
        for which in range(sides):
            lanes = foreign_lanes(which, tok, width)
            at = 2 + sides * (line - 1) + which
            far_factor = jnp.exp(top_ref[at : at + 1, lanes] - note[1 + which : 2 + which, lanes])
            rows = [foreign_rows(foreign[2 * which + line - 1], part, which, tok) for part in range(2)]
            far.append(
                (e_far, ds_far, rows_at(2 * which + line - 1, tok), [times(block, far_factor) for block in rows])
            )
        more = key_sums(tok, near, line - 1, e_ref, ds_ref, scaled, far)
        sums = [[sums[slot][i] + more[slot][i] for i in range(2)] for slot in range(2)]
    for i in range(2):
        mine_ref[i], swap_ref[i] = sums[0][i].astype(bf16), sums[1][i].astype(bf16)
    tiles = []
    for tile in range(2):
        value = dq_ref[rows_at(tile, tok), :]
        if tile < sides:
            _, y_at = pair(y, tile)
            value = value + jnp.where(within(y_at, chips), backs[tile][...].astype(f32), 0.0)
        tiles.append(value.astype(bf16))
    mine_q_ref[...] = jnp.where(near, tiles[0], tiles[1])
    swap_ref[2] = jnp.where(near, tiles[1], tiles[0])


def final_kernel(mine_ref, swap_ref, mine_q_ref, gq_ref, gk_ref, gv_ref):
    head = head_at()
    gq_ref[0, 0, head, 0] = mine_q_ref[...]
    gq_ref[0, 0, 1 - head, 0] = swap_ref[2]
    for i, ref in enumerate((gk_ref, gv_ref)):
        ref[0, 0, head, 0] = mine_ref[i]
        ref[0, 0, 1 - head, 0] = swap_ref[i]


def body(queries, keys, values, grad_out, attn_out, window_mask):
    tok, width = queries.shape[-2:]
    scale = width ** -0.5
    times, heights = lax.axis_size("tm"), lax.axis_size("height")
    chips = times // 2
    sides = 1 if chips == 2 else 2
    bf16, f32 = jnp.bfloat16, jnp.float32

    def call(kernel, shapes, specs, scratch=()):
        return pl.pallas_call(
            kernel,
            out_shape=[jax.ShapeDtypeStruct(*shape) for shape in shapes],
            in_specs=list(specs),
            out_specs=[VMEM] * len(shapes),
            scratch_shapes=list(scratch),
            compiler_params=LIMIT,
        )

    def partner(index, which, size):
        if which is None:
            return index
        at = index + 1 if index % 2 == which else index - 1
        return at if 0 <= at < size else None

    def exchange(block, y_which, z_which):
        pairs = []
        for t in range(times):
            for z in range(heights):
                y_at, z_at = partner(t // 2, y_which, chips), partner(z, z_which, heights)
                at = t * heights + z
                alone = y_at is None or z_at is None
                pairs.append((at, (t ^ 1) * heights + z if alone else (2 * y_at + 1 - t % 2) * heights + z_at))
        return lax.ppermute(block, ("tm", "height"), pairs)

    def swap_cores(block):
        return lax.ppermute(block, "tm", [(t, t ^ 1) for t in range(times)])

    line_shape, tile_shape = ((2, 2 * tok, width), bf16), ((2, tok, width), bf16)
    extra = 48
    arguments = (keys, values, queries, grad_out, attn_out, window_mask)
    kv, rest, other = call(
        functools.partial(pack_kernel, tok),
        [((2 * tok + extra, width), bf16), ((3 * tok + 16, width), bf16), ((5 * tok + 16, width), bf16)],
        [HBM] * 6,
        [pltpu.SMEM(window_mask.shape, jnp.int32), pltpu.SemaphoreType.DMA((11,))],
    )(*(pltpu.with_memory_space_constraint(x, pltpu.HBM) for x in arguments))
    early = [exchange(kv, None, which) for which in range(2)]
    par = swap_cores(other)
    border_shape, two = ((2 * tok + 16, width), bf16), 2 * tok
    par_kv, *borders = call(
        functools.partial(line_kernel, tok), [((2 * tok + 32, width), bf16)] + [border_shape] * sides, [VMEM] * 2
    )(rest, par)
    foreign = [exchange(borders[which], which, None) for which in range(sides)]
    late = [exchange(par_kv, None, which) for which in range(2)]
    tiles = (kv, par_kv, late[0], early[0], late[1], early[1])
    note_shape, raw_shape = ((8, two), f32), ((width, two), f32)

    def square(count, kind=f32):
        return ((count * tok, two), kind)

    def far_square(kind=f32):
        return ((3 * sides * tok, 2 * width), kind)

    q_all, g_all, table, s_own, d_own = call(
        functools.partial(first_kernel, tok, heights, scale),
        [((two, width), bf16)] * 2 + [note_shape, square(2), square(2)],
        [VMEM] * 4,
    )(kv, par_kv, rest, par)
    qg = (q_all, g_all)
    queries_in = [exchange(block, None, which) for block in qg for which in range(2)]
    foreign_in = [exchange(block, None, which) for block in foreign for which in range(2)]
    s_early, d_early, part = call(
        functools.partial(early_kernel, tok, scale), [square(2), square(2), note_shape], [VMEM] * 6
    )(*qg, table, s_own, *early)
    s_late, s_far, *sent = call(
        functools.partial(score_kernel, tok, chips, heights, sides, scale),
        [square(2), far_square()] + [note_shape] * sides,
        [VMEM] * (10 + sides),
    )(*qg, table, part, *tiles, *foreign)
    came = [exchange(sent[which], which, None) for which in range(sides)]
    far_tile = ((sides * tok, 2 * width), bf16)
    e, ds, e_far, ds_far, raw_dq, *far_dq = call(
        functools.partial(middle_kernel, tok, sides, scale),
        [square(2, bf16)] * 2 + [far_tile] * 2 + [raw_shape] + [((width, 2 * width), f32)] * sides,
        [VMEM] * (15 + 2 * sides),
    )(*qg, table, s_own, d_own, s_early, d_early, s_late, s_far, *tiles, *foreign, *sent)
    note, *shares = call(
        functools.partial(total_kernel, tok, chips, sides),
        [note_shape] + [((tok, width), bf16)] * sides,
        [VMEM] * (3 * sides),
    )(*far_dq, *sent, *came)
    notes = [exchange(note, None, which) for which in range(2)]
    shares = [exchange(share, which, None) for which, share in enumerate(shares)]
    far_pair = ((2 * sides * tok, 2 * width), bf16)
    line_terms = call(
        functools.partial(line_query_kernel, tok, chips, heights, sides, scale),
        [square(4, bf16)] * 2 + [far_pair] * 2 + [note_shape],
        [VMEM] * (8 + 2 * sides),
    )(kv, par_kv, *queries_in, *late, *foreign_in)
    own, dq = call(
        functools.partial(stay_kernel, tok, chips, sides),
        [((2, two, width), f32), ((two, width), f32)],
        [VMEM] * (8 + 2 * sides),
    )(*qg, e, ds, e_far, ds_far, raw_dq, note, *sent, *foreign)
    mine, mine_q, leaving = call(
        functools.partial(leave_kernel, tok, chips, sides),
        [tile_shape, ((tok, width), bf16), ((3, tok, width), bf16)],
        [VMEM] * (13 + 3 * sides),
    )(own, dq, *line_terms, *queries_in, *foreign_in, *notes, *shares)
    return call(final_kernel, [(queries.shape, bf16)] * 3, [VMEM] * 3)(mine, swap_cores(leaving), mine_q)


def solution(mesh):
    placed = P("tm", "height", "dp", None, None, None)
    return jax.shard_map(
        body,
        mesh=mesh,
        in_specs=(placed,) * 5 + (P("tm", "height", None, None),),
        out_specs=(placed,) * 3,
        check_vma=False,
    )
```

profile of v0, /device:TPU:0, one launch (start us, length us, event | category | flops | bytes accessed | tf_op | source)
XLA Modules:
  0.0 26.6 jit_solution(6762718543808948761)
XLA Ops:
  0.6 1.1 %shard_map.85 = (bf16[432,128]{1,0:T(8,128)(2,1)S(1)}, bf16[592,128]{1,0:T(8,128)(2,1)S(1)}, bf16[976,128]{1,0:T(8,128)(2,1)S(1)}) custom-call(bf16[1,1,2,1,192,128]{5,4,3,2,1,0:T(8,128)(2,1)} %k_ref.1, bf16[1,1,2,1,192,128]{5,4,3,2,1,0:T(8,128)(2,1)} %v_ref.1, bf16[1,1,2,1,192,128]{5,4,3,2,1,0:T(8,128)(2,1)} %q_ref.1, ...), custom_call_target="tpu_custom_call" | custom-call | tf_op jit(solution)/shard_map/pallas_call | solution.py:523
  1.8 0.5 %collective-permute-start = (bf16[976,128]{1,0:T(8,128)(2,1)S(1)}, bf16[976,128]{1,0:T(8,128)(2,1)S(1)}, u32[]{:S(2)}, u32[]{:S(2)}) collective-permute-start(bf16[976,128]{1,0:T(8,128)(2,1)S(1)} %get-tuple-element.39), channel_id=1, source_target_pairs={{0,8},{8,0},{16,24},{24,16},{1,9},{9,1},{17,25},{25,17},{2,10},{10... | collective-permute-start | bytes 749576 | tf_op jit(solution)/shard_map/ppermute | solution.py:518
  2.3 2.7 %collective-permute-start.1 = (bf16[432,128]{1,0:T(8,128)(2,1)S(1)}, bf16[432,128]{1,0:T(8,128)(2,1)S(1)}, u32[]{:S(2)}, u32[]{:S(2)}) collective-permute-start(bf16[432,128]{1,0:T(8,128)(2,1)S(1)} %get-tuple-element.37.kv_ref.refs_0_), channel_id=1, source_target_pairs={{0,10},{2,8},{4,14},{6,12},{8,2},{10,0},{12,6},{14,4},{16,26},{18,... | collective-permute-start | bytes 331784 | tf_op jit(solution)/shard_map/ppermute | solution.py:515
  5.2 2.9 %collective-permute-start.3 = (bf16[416,128]{1,0:T(8,128)(2,1)S(1)}, bf16[416,128]{1,0:T(8,128)(2,1)S(1)}, u32[]{:S(2)}, u32[]{:S(2)}) collective-permute-start(bf16[416,128]{1,0:T(8,128)(2,1)S(1)} %get-tuple-element.40.par_kv_ref.refs_1_), channel_id=1, source_target_pairs={{0,10},{2,8},{4,14},{6,12},{8,2},{10,0},{12,6},{14,4},{16,26},{18,... | collective-permute-start | bytes 319496 | tf_op jit(solution)/shard_map/ppermute | solution.py:515
  8.2 1.6 %collective-permute-start.5 = (bf16[400,128]{1,0:T(8,128)(2,1)S(1)}, bf16[400,128]{1,0:T(8,128)(2,1)S(1)}, u32[]{:S(2)}, u32[]{:S(2)}) collective-permute-start(bf16[400,128]{1,0:T(8,128)(2,1)S(1)} %get-tuple-element.49), channel_id=1, source_target_pairs={{0,24},{2,26},{4,28},{6,30},{8,16},{10,18},{12,20},{14,22},{16,8},... | collective-permute-start | bytes 307208 | tf_op jit(solution)/shard_map/ppermute | solution.py:515
  9.7 0.4 %shard_map.87 = (bf16[384,128]{1,0:T(8,128)(2,1)S(1)}, bf16[384,128]{1,0:T(8,128)(2,1)S(1)}, f32[8,384]{1,0:T(8,128)S(1)}, f32[384,384]{1,0:T(8,128)S(1)}, f32[384,384]{1,0:T(8,128)S(1)}) custom-call(bf16[432,128]{1,0:T(8,128)(2,1)S(1)} %get-tuple-element.37.kv_ref.refs_0_, bf16[416,128]{1,0:T(8,128)(2,1)S(1)} %get-tuple-element.40.par_kv_ref.refs_1_, ...), custom_call_target="tpu_custom_call" | custom-call | tf_op jit(solution)/shard_map/pallas_call | solution.py:546
  10.1 1.1 %collective-permute-start.7 = (bf16[384,128]{1,0:T(8,128)(2,1)S(1)}, bf16[384,128]{1,0:T(8,128)(2,1)S(1)}, u32[]{:S(2)}, u32[]{:S(2)}) collective-permute-start(bf16[384,128]{1,0:T(8,128)(2,1)S(1)} %get-tuple-element.41.q_all), channel_id=1, source_target_pairs={{0,10},{2,8},{4,14},{6,12},{8,2},{10,0},{12,6},{14,4},{16,26},{18,... | collective-permute-start | bytes 294920 | tf_op jit(solution)/shard_map/ppermute | solution.py:515
  11.4 0.5 %shard_map.88 = (f32[384,384]{1,0:T(8,128)S(1)}, f32[384,384]{1,0:T(8,128)S(1)}, f32[8,384]{1,0:T(8,128)S(1)}) custom-call(bf16[384,128]{1,0:T(8,128)(2,1)S(1)} %get-tuple-element.41.q_all, bf16[384,128]{1,0:T(8,128)(2,1)S(1)} %get-tuple-element.42.g_all, f32[8,384]{1,0:T(8,128)S(1)} %get-tuple-element.43.table, f32[384,384]{1,0:T(8,128)S(1)} %get-tuple-element.44.s_own, ...), custom_call_target="tpu_custom_call" | custom-call | tf_op jit(solution)/shard_map/pallas_call | solution.py:554
  11.8 0.9 %collective-permute-done.5.refs_6_.refs_1_ = bf16[400,128]{1,0:T(8,128)(2,1)S(1)} collective-permute-done((bf16[400,128]{1,0:T(8,128)(2,1)S(1)}, bf16[400,128]{1,0:T(8,128)(2,1)S(1)}, u32[]{:S(2)}, u32[]{:S(2)}) %collective-permute-start.5) | collective-permute-done | bytes 102432 | tf_op jit(solution)/shard_map/ppermute | solution.py:515
  12.8 0.5 %shard_map.89 = (f32[384,384]{1,0:T(8,128)S(1)}, f32[576,256]{1,0:T(8,128)S(1)}, f32[8,384]{1,0:T(8,128)S(1)}) custom-call(bf16[384,128]{1,0:T(8,128)(2,1)S(1)} %get-tuple-element.41.q_all, bf16[384,128]{1,0:T(8,128)(2,1)S(1)} %get-tuple-element.42.g_all, f32[8,384]{1,0:T(8,128)S(1)} %get-tuple-element.43.table, f32[8,384]{1,0:T(8,128)S(1)} %get-tuple-element.48.part, ...), custom_call_target="tpu_custom_call" | custom-call | tf_op jit(solution)/shard_map/pallas_call | solution.py:557
  13.3 1.9 %collective-permute-start.6 = (f32[8,384]{1,0:T(8,128)S(1)}, f32[8,384]{1,0:T(8,128)S(1)}, u32[]{:S(2)}, u32[]{:S(2)}) collective-permute-start(f32[8,384]{1,0:T(8,128)S(1)} %get-tuple-element.52.refs_7_.refs_1_.refs_0_), channel_id=1, source_target_pairs={{0,24},{2,26},{4,28},{6,30},{8,16},{10,18},{12,20},{14,22},{16,8},... | collective-permute-start | bytes 36872 | tf_op jit(solution)/shard_map/ppermute | solution.py:515
  15.2 1.0 %collective-permute-start.9 = (bf16[384,128]{1,0:T(8,128)(2,1)S(1)}, bf16[384,128]{1,0:T(8,128)(2,1)S(1)}, u32[]{:S(2)}, u32[]{:S(2)}) collective-permute-start(bf16[384,128]{1,0:T(8,128)(2,1)S(1)} %get-tuple-element.42.g_all), channel_id=1, source_target_pairs={{0,10},{2,8},{4,14},{6,12},{8,2},{10,0},{12,6},{14,4},{16,26},{18,... | collective-permute-start | bytes 294920 | tf_op jit(solution)/shard_map/ppermute | solution.py:515
  16.2 0.5 %collective-permute-start.10 = (bf16[384,128]{1,0:T(8,128)(2,1)S(1)}, bf16[384,128]{1,0:T(8,128)(2,1)S(1)}, u32[]{:S(2)}, u32[]{:S(2)}) collective-permute-start(bf16[384,128]{1,0:T(8,128)(2,1)S(1)} %get-tuple-element.42.g_all), channel_id=1, source_target_pairs={{0,8},{2,12},{4,10},{6,14},{8,0},{10,4},{12,2},{14,6},{16,24},{18,... | collective-permute-start | bytes 294920 | tf_op jit(solution)/shard_map/ppermute | solution.py:515
  16.7 0.7 %collective-permute-start.11 = (bf16[400,128]{1,0:T(8,128)(2,1)S(1)}, bf16[400,128]{1,0:T(8,128)(2,1)S(1)}, u32[]{:S(2)}, u32[]{:S(2)}) collective-permute-start(bf16[400,128]{1,0:T(8,128)(2,1)S(1)} %collective-permute-done.5.refs_6_.refs_1_), channel_id=1, source_target_pairs={{0,10},{2,8},{4,14},{6,12},{8,2},{10,0},{12,6},{14,4},{16,26},{18,... | collective-permute-start | bytes 307208 | tf_op jit(solution)/shard_map/ppermute | solution.py:515
  17.5 1.2 %shard_map.90 = (bf16[384,384]{1,0:T(8,128)(2,1)S(1)}, bf16[384,384]{1,0:T(8,128)(2,1)S(1)}, bf16[192,256]{1,0:T(8,128)(2,1)S(1)}, bf16[192,256]{1,0:T(8,128)(2,...) custom-call(bf16[384,128]{1,0:T(8,128)(2,1)S(1)} %get-tuple-element.41.q_all, ...), custom_call_target="tpu_custom_call" | custom-call | tf_op jit(solution)/shard_map/pallas_call | solution.py:564
  18.8 1.2 %collective-permute-start.15 = (bf16[192,128]{1,0:T(8,128)(2,1)S(1)}, bf16[192,128]{1,0:T(8,128)(2,1)S(1)}, u32[]{:S(2)}, u32[]{:S(2)}) collective-permute-start(bf16[192,128]{1,0:T(8,128)(2,1)S(1)} %get-tuple-element.67), channel_id=1, source_target_pairs={{0,24},{2,26},{4,28},{6,30},{8,16},{10,18},{12,20},{14,22},{16,8},... | collective-permute-start | bytes 147464 | tf_op jit(solution)/shard_map/ppermute | solution.py:515
  20.0 0.3 %collective-permute-done.9.refs_2_ = bf16[384,128]{1,0:T(8,128)(2,1)S(1)} collective-permute-done((bf16[384,128]{1,0:T(8,128)(2,1)S(1)}, bf16[384,128]{1,0:T(8,128)(2,1)S(1)}, u32[]{:S(2)}, u32[]{:S(2)}) %collective-permute-start.9) | collective-permute-done | bytes 98336 | tf_op jit(solution)/shard_map/ppermute | solution.py:515
  20.3 1.8 %collective-permute-start.13 = (f32[8,384]{1,0:T(8,128)S(1)}, f32[8,384]{1,0:T(8,128)S(1)}, u32[]{:S(2)}, u32[]{:S(2)}) collective-permute-start(f32[8,384]{1,0:T(8,128)S(1)} %get-tuple-element.59.note), channel_id=1, source_target_pairs={{0,10},{2,8},{4,14},{6,12},{8,2},{10,0},{12,6},{14,4},{16,26},{18,... | collective-permute-start | bytes 36872 | tf_op jit(solution)/shard_map/ppermute | solution.py:515
  22.1 0.5 %shard_map.92 = (f32[2,384,128]{2,1,0:T(8,128)S(1)}, f32[384,128]{1,0:T(8,128)S(1)}) custom-call(bf16[384,128]{1,0:T(8,128)(2,1)S(1)} %get-tuple-element.41.q_all, bf16[384,128]{1,0:T(8,128)(2,1)S(1)} %get-tuple-element.42.g_all, bf16[384,384]{1,0:T(8,128)(2,1)S(1)} %get-tuple-element.53.e_ref, bf16[384,384]{1,0:T(8,128)(2,1)S(1)} %get-tuple-element.54.ds_ref, ...), custom_call_target="tpu_custom_call" | custom-call | tf_op jit(solution)/shard_map/pallas_call | solution.py:582
  22.7 0.9 %shard_map.93 = (bf16[768,384]{1,0:T(8,128)(2,1)S(1)}, bf16[768,384]{1,0:T(8,128)(2,1)S(1)}, bf16[384,256]{1,0:T(8,128)(2,1)S(1)}, bf16[384,256]{1,0:T(8,128)(2,1)S(1)}, f32[8,384]{1,0:T(8,128)S(1)}) custom-call(bf16[432,128]{1,0:T(8,128)(2,1)S(1)} %get-tuple-element.37.kv_ref.refs_0_, bf16[416,128]{1,0:T(8,128)(2,1)S(1)} %get-tuple-element.40.par_kv_ref.refs_1_, ...), custom_call_target="tpu_custom_call" | custom-call | tf_op jit(solution)/shard_map/pallas_call | solution.py:577
  23.6 0.7 %shard_map.94 = (bf16[2,192,128]{2,1,0:T(8,128)(2,1)S(1)}, bf16[192,128]{1,0:T(8,128)(2,1)S(1)}, bf16[3,192,128]{2,1,0:T(8,128)(2,1)S(1)}) custom-call(f32[2,384,128]{2,1,0:T(8,128)S(1)} %get-tuple-element.60.own_ref, f32[384,128]{1,0:T(8,128)S(1)} %get-tuple-element.61.dq_ref, bf16[768,384]{1,0:T(8,128)(2,1)S(1)} %get-tuple-element.62.e_ref, ...), custom_call_target="tpu_custom_call" | custom-call | tf_op jit(solution)/shard_map/pallas_call | solution.py:587
  24.3 0.6 %collective-permute-start.16 = (bf16[3,192,128]{2,1,0:T(8,128)(2,1)S(1)}, bf16[3,192,128]{2,1,0:T(8,128)(2,1)S(1)}, u32[]{:S(2)}, u32[]{:S(2)}) collective-permute-start(bf16[3,192,128]{2,1,0:T(8,128)(2,1)S(1)} %get-tuple-element.69), channel_id=1, source_target_pairs={{0,8},{8,0},{16,24},{24,16},{1,9},{9,1},{17,25},{25,17},{2,10},{10... | collective-permute-start | bytes 442376 | tf_op jit(solution)/shard_map/ppermute | solution.py:518
  24.8 1.0 %collective-permute-done.16.swap_ref = bf16[3,192,128]{2,1,0:T(8,128)(2,1)S(1)} collective-permute-done((bf16[3,192,128]{2,1,0:T(8,128)(2,1)S(1)}, bf16[3,192,128]{2,1,0:T(8,128)(2,1)S(1)}, u32[]{:S(2)}, u32[]{:S(2)}) %collective-permute-start.16) | collective-permute-done | bytes 147488 | tf_op jit(solution)/shard_map/ppermute | solution.py:518
  25.9 0.7 %shard_map.95 = (bf16[1,1,2,1,192,128]{5,4,3,2,1,0:T(8,128)(2,1)}, bf16[1,1,2,1,192,128]{5,4,3,2,1,0:T(8,128)(2,1)}, bf16[1,1,2,1,192,128]{5,4,3,2,1,0:T(8,128)(2,1)}) custom-call(bf16[2,192,128]{2,1,0:T(8,128)(2,1)S(1)} %get-tuple-element.68.mine_ref, bf16[3,192,128]{2,1,0:T(8,128)(2,1)S(1)} %collective-permute-done.16.swap_ref, ...), custom_call_target="tpu_custom_call" | custom-call | tf_op jit(solution)/shard_map/pallas_call | solution.py:592
  (21 shorter events, 0.8 us)
Async XLA Ops:
  1.8 3.3 %collective-permute-start = (bf16[976,128]{1,0:T(8,128)(2,1)S(1)}, bf16[976,128]{1,0:T(8,128)(2,1)S(1)}, u32[]{:S(2)}, u32[]{:S(2)}) collective-permute-start(bf16[976,128]{1,0:T(8,128)(2,1)S(1)} %get-tuple-element.39), channel_id=1, source_target_pairs={{0,8},{8,0},{16,24},{24,16},{1,9},{9,1},{17,25},{25,17},{2,10},{10... | collective-permute-start | bytes 749576 | tf_op jit(solution)/shard_map/ppermute | solution.py:518
  2.3 7.8 %collective-permute-start.1 = (bf16[432,128]{1,0:T(8,128)(2,1)S(1)}, bf16[432,128]{1,0:T(8,128)(2,1)S(1)}, u32[]{:S(2)}, u32[]{:S(2)}) collective-permute-start(bf16[432,128]{1,0:T(8,128)(2,1)S(1)} %get-tuple-element.37.kv_ref.refs_0_), channel_id=1, source_target_pairs={{0,10},{2,8},{4,14},{6,12},{8,2},{10,0},{12,6},{14,4},{16,26},{18,... | collective-permute-start | bytes 331784 | tf_op jit(solution)/shard_map/ppermute | solution.py:515
  5.0 6.2 %collective-permute-start.2 = (bf16[432,128]{1,0:T(8,128)(2,1)S(1)}, bf16[432,128]{1,0:T(8,128)(2,1)S(1)}, u32[]{:S(2)}, u32[]{:S(2)}) collective-permute-start(bf16[432,128]{1,0:T(8,128)(2,1)S(1)} %get-tuple-element.37.kv_ref.refs_0_), channel_id=1, source_target_pairs={{0,8},{2,12},{4,10},{6,14},{8,0},{10,4},{12,2},{14,6},{16,24},{18,... | collective-permute-start | bytes 331784 | tf_op jit(solution)/shard_map/ppermute | solution.py:515
  5.2 7.6 %collective-permute-start.3 = (bf16[416,128]{1,0:T(8,128)(2,1)S(1)}, bf16[416,128]{1,0:T(8,128)(2,1)S(1)}, u32[]{:S(2)}, u32[]{:S(2)}) collective-permute-start(bf16[416,128]{1,0:T(8,128)(2,1)S(1)} %get-tuple-element.40.par_kv_ref.refs_1_), channel_id=1, source_target_pairs={{0,10},{2,8},{4,14},{6,12},{8,2},{10,0},{12,6},{14,4},{16,26},{18,... | collective-permute-start | bytes 319496 | tf_op jit(solution)/shard_map/ppermute | solution.py:515
  8.1 4.7 %collective-permute-start.4 = (bf16[416,128]{1,0:T(8,128)(2,1)S(1)}, bf16[416,128]{1,0:T(8,128)(2,1)S(1)}, u32[]{:S(2)}, u32[]{:S(2)}) collective-permute-start(bf16[416,128]{1,0:T(8,128)(2,1)S(1)} %get-tuple-element.40.par_kv_ref.refs_1_), channel_id=1, source_target_pairs={{0,8},{2,12},{4,10},{6,14},{8,0},{10,4},{12,2},{14,6},{16,24},{18,... | collective-permute-start | bytes 319496 | tf_op jit(solution)/shard_map/ppermute | solution.py:515
  8.2 4.6 %collective-permute-start.5 = (bf16[400,128]{1,0:T(8,128)(2,1)S(1)}, bf16[400,128]{1,0:T(8,128)(2,1)S(1)}, u32[]{:S(2)}, u32[]{:S(2)}) collective-permute-start(bf16[400,128]{1,0:T(8,128)(2,1)S(1)} %get-tuple-element.49), channel_id=1, source_target_pairs={{0,24},{2,26},{4,28},{6,30},{8,16},{10,18},{12,20},{14,22},{16,8},... | collective-permute-start | bytes 307208 | tf_op jit(solution)/shard_map/ppermute | solution.py:515
  10.1 6.5 %collective-permute-start.7 = (bf16[384,128]{1,0:T(8,128)(2,1)S(1)}, bf16[384,128]{1,0:T(8,128)(2,1)S(1)}, u32[]{:S(2)}, u32[]{:S(2)}) collective-permute-start(bf16[384,128]{1,0:T(8,128)(2,1)S(1)} %get-tuple-element.41.q_all), channel_id=1, source_target_pairs={{0,10},{2,8},{4,14},{6,12},{8,2},{10,0},{12,6},{14,4},{16,26},{18,... | collective-permute-start | bytes 294920 | tf_op jit(solution)/shard_map/ppermute | solution.py:515
  11.2 7.6 %collective-permute-start.8 = (bf16[384,128]{1,0:T(8,128)(2,1)S(1)}, bf16[384,128]{1,0:T(8,128)(2,1)S(1)}, u32[]{:S(2)}, u32[]{:S(2)}) collective-permute-start(bf16[384,128]{1,0:T(8,128)(2,1)S(1)} %get-tuple-element.41.q_all), channel_id=1, source_target_pairs={{0,8},{2,12},{4,10},{6,14},{8,0},{10,4},{12,2},{14,6},{16,24},{18,... | collective-permute-start | bytes 294920 | tf_op jit(solution)/shard_map/ppermute | solution.py:515
  13.3 4.0 %collective-permute-start.6 = (f32[8,384]{1,0:T(8,128)S(1)}, f32[8,384]{1,0:T(8,128)S(1)}, u32[]{:S(2)}, u32[]{:S(2)}) collective-permute-start(f32[8,384]{1,0:T(8,128)S(1)} %get-tuple-element.52.refs_7_.refs_1_.refs_0_), channel_id=1, source_target_pairs={{0,24},{2,26},{4,28},{6,30},{8,16},{10,18},{12,20},{14,22},{16,8},... | collective-permute-start | bytes 36872 | tf_op jit(solution)/shard_map/ppermute | solution.py:515
  15.2 5.1 %collective-permute-start.9 = (bf16[384,128]{1,0:T(8,128)(2,1)S(1)}, bf16[384,128]{1,0:T(8,128)(2,1)S(1)}, u32[]{:S(2)}, u32[]{:S(2)}) collective-permute-start(bf16[384,128]{1,0:T(8,128)(2,1)S(1)} %get-tuple-element.42.g_all), channel_id=1, source_target_pairs={{0,10},{2,8},{4,14},{6,12},{8,2},{10,0},{12,6},{14,4},{16,26},{18,... | collective-permute-start | bytes 294920 | tf_op jit(solution)/shard_map/ppermute | solution.py:515
  16.2 5.9 %collective-permute-start.10 = (bf16[384,128]{1,0:T(8,128)(2,1)S(1)}, bf16[384,128]{1,0:T(8,128)(2,1)S(1)}, u32[]{:S(2)}, u32[]{:S(2)}) collective-permute-start(bf16[384,128]{1,0:T(8,128)(2,1)S(1)} %get-tuple-element.42.g_all), channel_id=1, source_target_pairs={{0,8},{2,12},{4,10},{6,14},{8,0},{10,4},{12,2},{14,6},{16,24},{18,... | collective-permute-start | bytes 294920 | tf_op jit(solution)/shard_map/ppermute | solution.py:515
  16.7 6.0 %collective-permute-start.11 = (bf16[400,128]{1,0:T(8,128)(2,1)S(1)}, bf16[400,128]{1,0:T(8,128)(2,1)S(1)}, u32[]{:S(2)}, u32[]{:S(2)}) collective-permute-start(bf16[400,128]{1,0:T(8,128)(2,1)S(1)} %collective-permute-done.5.refs_6_.refs_1_), channel_id=1, source_target_pairs={{0,10},{2,8},{4,14},{6,12},{8,2},{10,0},{12,6},{14,4},{16,26},{18,... | collective-permute-start | bytes 307208 | tf_op jit(solution)/shard_map/ppermute | solution.py:515
  17.4 5.3 %collective-permute-start.12 = (bf16[400,128]{1,0:T(8,128)(2,1)S(1)}, bf16[400,128]{1,0:T(8,128)(2,1)S(1)}, u32[]{:S(2)}, u32[]{:S(2)}) collective-permute-start(bf16[400,128]{1,0:T(8,128)(2,1)S(1)} %collective-permute-done.5.refs_6_.refs_1_), channel_id=1, source_target_pairs={{0,8},{2,12},{4,10},{6,14},{8,0},{10,4},{12,2},{14,6},{16,24},{18,... | collective-permute-start | bytes 307208 | tf_op jit(solution)/shard_map/ppermute | solution.py:515
  18.8 4.7 %collective-permute-start.15 = (bf16[192,128]{1,0:T(8,128)(2,1)S(1)}, bf16[192,128]{1,0:T(8,128)(2,1)S(1)}, u32[]{:S(2)}, u32[]{:S(2)}) collective-permute-start(bf16[192,128]{1,0:T(8,128)(2,1)S(1)} %get-tuple-element.67), channel_id=1, source_target_pairs={{0,24},{2,26},{4,28},{6,30},{8,16},{10,18},{12,20},{14,22},{16,8},... | collective-permute-start | bytes 147464 | tf_op jit(solution)/shard_map/ppermute | solution.py:515
  20.3 3.2 %collective-permute-start.13 = (f32[8,384]{1,0:T(8,128)S(1)}, f32[8,384]{1,0:T(8,128)S(1)}, u32[]{:S(2)}, u32[]{:S(2)}) collective-permute-start(f32[8,384]{1,0:T(8,128)S(1)} %get-tuple-element.59.note), channel_id=1, source_target_pairs={{0,10},{2,8},{4,14},{6,12},{8,2},{10,0},{12,6},{14,4},{16,26},{18,... | collective-permute-start | bytes 36872 | tf_op jit(solution)/shard_map/ppermute | solution.py:515
  22.1 1.4 %collective-permute-start.14 = (f32[8,384]{1,0:T(8,128)S(1)}, f32[8,384]{1,0:T(8,128)S(1)}, u32[]{:S(2)}, u32[]{:S(2)}) collective-permute-start(f32[8,384]{1,0:T(8,128)S(1)} %get-tuple-element.59.note), channel_id=1, source_target_pairs={{0,8},{2,12},{4,10},{6,14},{8,0},{10,4},{12,2},{14,6},{16,24},{18,... | collective-permute-start | bytes 36872 | tf_op jit(solution)/shard_map/ppermute | solution.py:515
  24.3 1.6 %collective-permute-start.16 = (bf16[3,192,128]{2,1,0:T(8,128)(2,1)S(1)}, bf16[3,192,128]{2,1,0:T(8,128)(2,1)S(1)}, u32[]{:S(2)}, u32[]{:S(2)}) collective-permute-start(bf16[3,192,128]{2,1,0:T(8,128)(2,1)S(1)} %get-tuple-element.69), channel_id=1, source_target_pairs={{0,8},{8,0},{16,24},{24,16},{1,9},{9,1},{17,25},{25,17},{2,10},{10... | collective-permute-start | bytes 442376 | tf_op jit(solution)/shard_map/ppermute | solution.py:518
where the time goes:
time: 26.8 us; the launch traced here: 26.6 us
  starting transfers between devices  16.8 us (63%)
  Pallas kernels  6.78 us (25%)
  waiting for transfers between devices  2.31 us (9%)
  between operations  0.74 us (3%)
    ppermute x15, starting transfers between devices, exchange(): return lax.ppermute(block, ('tm', 'height'), pairs)  15.7 us
    ppermute x15, waiting for transfers between devices, exchange(): return lax.ppermute(block, ('tm', 'height'), pairs)  1.3 us
    pallas_call x1, Pallas kernels, body(): call(functools.partial(middle_kernel, tok, sides, scale), [square(2, bf16...  1.16 us
    pallas_call x1, Pallas kernels, body(): call(functools.partial(pack_kernel, tok), [((2 * tok + extra, width), bf1...  1.13 us
    ppermute x2, starting transfers between devices, swap_cores(): return lax.ppermute(block, 'tm', [(t, t ^ 1) for t in range(times)])  1.08 us
    ppermute x2, waiting for transfers between devices, swap_cores(): return lax.ppermute(block, 'tm', [(t, t ^ 1) for t in range(times)])  1.01 us
    pallas_call x1, Pallas kernels, body(): call(functools.partial(line_query_kernel, tok, chips, heights, sides, sca...  0.85 us
    pallas_call x1, Pallas kernels, body(): call(final_kernel, [(queries.shape, bf16)] * 3, [VMEM] * 3)  0.74 us
  transfers between devices with their start and end apart: 17, of which 3 were waited for; matrix products, arithmetic and copies ran while one was open for 0% of the time, Pallas kernels for 16%

commit v1 on v0

--- a/solution.py
+++ b/solution.py
@@ -310,11 +310,21 @@
         far_dq[which][...] = dq
 
 
+def message_kernel(tok, q_all, g_all, *refs):
+    *foreign, out_ref = refs
+    out_ref[pl.ds(0, 2 * tok), :] = q_all[...]
+    out_ref[pl.ds(2 * tok, 2 * tok), :] = g_all[...]
+    for which, ref in enumerate(foreign):
+        far_part(out_ref, which, tok)[...] = ref[pl.ds(0, 2 * tok + 16), :]
+
+
+def far_part(ref, which, tok):
+    return ref.at[pl.ds(4 * tok + which * (2 * tok + 16), 2 * tok + 16), :]
+
+
 def total_kernel(tok, chips, sides, *refs):
-    far_dq, sent, came = (refs[i * sides : (i + 1) * sides] for i in range(3))
-    note_ref, *shares = refs[3 * sides :]
+    sent, came, note_ref = refs[:sides], refs[sides : 2 * sides], refs[2 * sides]
     y, _, _ = place()
-    width = far_dq[0].shape[0]
 
     def log_total(top, total, other_top, other_total):
         both = jnp.maximum(top, other_top)
@@ -326,12 +336,7 @@
         inside = within(y_at, chips)
         note = came[which]
         far_lse = log_total(note[0:1, :], note[1:2, :], sent[which][2:3, :], sent[which][3:4, :])
-        far_lse = jnp.where(inside, far_lse, 0.0)
-        far_rows.append(far_lse)
-        lanes = foreign_lanes(which, tok, width)
-        factor = jnp.where(inside, jnp.exp(sent[which][2:3, lanes] - far_lse[:, lanes]), 0.0)
-        share = (far_dq[which][...] * factor).T
-        shares[which][...] = (share[:tok] if which == 0 else share[2 * width - tok :]).astype(jnp.bfloat16)
+        far_rows.append(jnp.where(inside, far_lse, 0.0))
         other = jnp.where(inside, note[2:3, :], -1e30), jnp.where(inside, note[3:4, :], 0.0)
         if which == 0:
             lse = log_total(sent[0][0:1, :], sent[0][1:2, :], *other)
@@ -341,9 +346,20 @@
     note_ref[...] = jnp.concatenate(rows + [jnp.zeros((8 - len(rows), 2 * tok), jnp.float32)], axis=0)
 
 
+def share_kernel(tok, chips, sides, note, *refs):
+    far_dq, sent, shares = (refs[i * sides : (i + 1) * sides] for i in range(3))
+    y, _, _ = place()
+    width = far_dq[0].shape[0]
+    for which in range(sides):
+        _, y_at = pair(y, which)
+        lanes = foreign_lanes(which, tok, width)
+        factor = jnp.exp(sent[which][2:3, lanes] - note[1 + which : 2 + which, lanes])
+        share = (far_dq[which][...] * jnp.where(within(y_at, chips), factor, 0.0)).T
+        shares[which][...] = (share[:tok] if which == 0 else share[2 * width - tok :]).astype(jnp.bfloat16)
+
+
 def line_query_kernel(tok, chips, heights, sides, scale, kv_ref, par_kv_ref, *refs):
-    queries, grads_in, extras = refs[:2], refs[2:4], refs[4:6]
-    foreign, outs = refs[6 : 6 + 2 * sides], refs[6 + 2 * sides :]
+    queries, extras, outs = refs[:2], refs[2:4], refs[4:]
     e_ref, ds_ref, e_far, ds_far, top_ref = outs
     y, c, z = place()
     near = border_is_own(y, c)
@@ -363,7 +379,7 @@
         own_flags, par_flags = (pick(near, which, rows[0:9], rows[9:18]) for which in range(2))
         delta = [sum(rows[18 + 3 * i + part : 19 + 3 * i + part] for i in range(3)) for part in range(two // width)]
         delta = jnp.concatenate(delta, axis=1)
-        line_q, line_g = queries[line - 1][...], grads_in[line - 1][...]
+        line_q, line_g = (queries[line - 1][pl.ds(part * two, two), :] for part in range(2))
         scores = []
         for slot in range(2):
             row = flag_row(tok, slot, at, own_flags, par_flags, False)
@@ -378,7 +394,7 @@
             e_ref[kept, :] = weights.astype(bf16)
             ds_ref[kept, :] = (weights * grads * scale).astype(bf16)
         for which in range(sides):
-            ref = foreign[2 * which + line - 1]
+            ref = far_part(queries[line - 1], which, tok)
             y_rising, y_at = pair(y, which)
             flags = ref[pl.ds(2 * tok, 16), :].astype(f32)
             row = far_row(tok, which, jnp.where(y_rising, at(flags, 0), at(flags, 2)))
@@ -435,9 +451,8 @@
 
 
 def leave_kernel(tok, chips, sides, own_ref, dq_ref, e_ref, ds_ref, e_far, ds_far, top_ref, *refs):
-    queries, refs = (refs[0:2], refs[2:4]), refs[4:]
-    foreign, notes, backs = refs[: 2 * sides], refs[2 * sides : 2 + 2 * sides], refs[2 + 2 * sides : 2 + 3 * sides]
-    mine_ref, mine_q_ref, swap_ref = refs[2 + 3 * sides :]
+    queries, notes, backs = refs[:2], refs[2:4], refs[4 : 4 + sides]
+    mine_ref, mine_q_ref, swap_ref = refs[4 + sides :]
     y, c, _ = place()
     near = border_is_own(y, c)
     f32, bf16 = jnp.float32, jnp.bfloat16
@@ -446,13 +461,13 @@
     for line in (1, 2):
         note = notes[line - 1]
         factor = jnp.exp(top_ref[line - 1 : line, :] - note[0:1, :])
-        scaled = [times(queries[part][line - 1][...], factor) for part in range(2)]
+        scaled = [times(queries[line - 1][pl.ds(part * 2 * tok, 2 * tok), :], factor) for part in range(2)]
         far = []
         for which in range(sides):
             lanes = foreign_lanes(which, tok, width)
             at = 2 + sides * (line - 1) + which
             far_factor = jnp.exp(top_ref[at : at + 1, lanes] - note[1 + which : 2 + which, lanes])
-            rows = [foreign_rows(foreign[2 * which + line - 1], part, which, tok) for part in range(2)]
+            rows = [foreign_rows(far_part(queries[line - 1], which, tok), part, which, tok) for part in range(2)]
             far.append(
                 (e_far, ds_far, rows_at(2 * which + line - 1, tok), [times(block, far_factor) for block in rows])
             )
@@ -488,7 +503,7 @@
     sides = 1 if chips == 2 else 2
     bf16, f32 = jnp.bfloat16, jnp.float32
 
-    def call(kernel, shapes, specs, scratch=()):
+    def call(kernel, shapes, specs, scratch=(), cost=0):
         return pl.pallas_call(
             kernel,
             out_shape=[jax.ShapeDtypeStruct(*shape) for shape in shapes],
@@ -496,6 +511,7 @@
             out_specs=[VMEM] * len(shapes),
             scratch_shapes=list(scratch),
             compiler_params=LIMIT,
+            cost_estimate=pl.CostEstimate(flops=cost * 10**9, bytes_accessed=0, transcendentals=0) if cost else None,
         )
 
     def partner(index, which, size):
@@ -518,7 +534,7 @@
         return lax.ppermute(block, "tm", [(t, t ^ 1) for t in range(times)])
 
     line_shape, tile_shape = ((2, 2 * tok, width), bf16), ((2, tok, width), bf16)
-    extra = 48
+    extra = 64
     arguments = (keys, values, queries, grad_out, attn_out, window_mask)
     kv, rest, other = call(
         functools.partial(pack_kernel, tok),
@@ -528,7 +544,7 @@
     )(*(pltpu.with_memory_space_constraint(x, pltpu.HBM) for x in arguments))
     early = [exchange(kv, None, which) for which in range(2)]
     par = swap_cores(other)
-    border_shape, two = ((2 * tok + 16, width), bf16), 2 * tok
+    border_shape, two = ((2 * tok + 48, width), bf16), 2 * tok
     par_kv, *borders = call(
         functools.partial(line_kernel, tok), [((2 * tok + 32, width), bf16)] + [border_shape] * sides, [VMEM] * 2
     )(rest, par)
@@ -549,10 +565,14 @@
         [VMEM] * 4,
     )(kv, par_kv, rest, par)
     qg = (q_all, g_all)
-    queries_in = [exchange(block, None, which) for block in qg for which in range(2)]
-    foreign_in = [exchange(block, None, which) for block in foreign for which in range(2)]
+    (message,) = call(
+        functools.partial(message_kernel, tok),
+        [((4 * tok + sides * (2 * tok + 16), width), bf16)],
+        [VMEM] * (2 + sides),
+    )(*qg, *foreign)
+    queries_in = [exchange(message, None, which) for which in range(2)]
     s_early, d_early, part = call(
-        functools.partial(early_kernel, tok, scale), [square(2), square(2), note_shape], [VMEM] * 6
+        functools.partial(early_kernel, tok, scale), [square(2), square(2), note_shape], [VMEM] * 6, cost=20
     )(*qg, table, s_own, *early)
     s_late, s_far, *sent = call(
         functools.partial(score_kernel, tok, chips, heights, sides, scale),
@@ -565,20 +585,21 @@
         functools.partial(middle_kernel, tok, sides, scale),
         [square(2, bf16)] * 2 + [far_tile] * 2 + [raw_shape] + [((width, 2 * width), f32)] * sides,
         [VMEM] * (15 + 2 * sides),
+        cost=20,
     )(*qg, table, s_own, d_own, s_early, d_early, s_late, s_far, *tiles, *foreign, *sent)
-    note, *shares = call(
-        functools.partial(total_kernel, tok, chips, sides),
-        [note_shape] + [((tok, width), bf16)] * sides,
-        [VMEM] * (3 * sides),
-    )(*far_dq, *sent, *came)
+    (note,) = call(functools.partial(total_kernel, tok, chips, sides), [note_shape], [VMEM] * (2 * sides))(*sent, *came)
+    shares = call(
+        functools.partial(share_kernel, tok, chips, sides), [((tok, width), bf16)] * sides, [VMEM] * (1 + 2 * sides)
+    )(note, *far_dq, *sent)
     notes = [exchange(note, None, which) for which in range(2)]
     shares = [exchange(share, which, None) for which, share in enumerate(shares)]
     far_pair = ((2 * sides * tok, 2 * width), bf16)
     line_terms = call(
         functools.partial(line_query_kernel, tok, chips, heights, sides, scale),
         [square(4, bf16)] * 2 + [far_pair] * 2 + [note_shape],
-        [VMEM] * (8 + 2 * sides),
-    )(kv, par_kv, *queries_in, *late, *foreign_in)
+        [VMEM] * 6,
+        cost=20,
+    )(kv, par_kv, *queries_in, *late)
     own, dq = call(
         functools.partial(stay_kernel, tok, chips, sides),
         [((2, two, width), f32), ((two, width), f32)],
@@ -587,8 +608,8 @@
     mine, mine_q, leaving = call(
         functools.partial(leave_kernel, tok, chips, sides),
         [tile_shape, ((tok, width), bf16), ((3, tok, width), bf16)],
-        [VMEM] * (13 + 3 * sides),
-    )(own, dq, *line_terms, *queries_in, *foreign_in, *notes, *shares)
+        [VMEM] * (11 + sides),
+    )(own, dq, *line_terms, *queries_in, *notes, *shares)
     return call(final_kernel, [(queries.shape, bf16)] * 3, [VMEM] * 3)(mine, swap_cores(leaving), mine_q)
 
 

time: 26.8 us -> 26.4 us (0.985)
  starting transfers between devices: 16.8 us -> 14 us
  waiting for transfers between devices: 2.31 us -> 4.62 us
    ppermute x15 -> x11, starting transfers between devices: 15.7 us -> 12.9 us  [exchange(): return lax.ppermute(block, ('tm', 'height'), pairs)]
    ppermute x15 -> x11, waiting for transfers between devices: 1.3 us -> 3.61 us  [exchange(): return lax.ppermute(block, ('tm', 'height'), pairs)]
  transfers between devices with their start and end apart: 17 -> 13, of which waited for: 3 -> 5; matrix products, arithmetic and copies ran while one was open for 0% -> 0% of each run, Pallas kernels for 16% -> 16%
where the time goes in v1:
time: 26.4 us; the launch traced here: 26.2 us
  starting transfers between devices  14 us (53%)
  Pallas kernels  6.78 us (26%)
  waiting for transfers between devices  4.62 us (18%)
  between operations  0.75 us (3%)
    ppermute x11, starting transfers between devices, exchange(): return lax.ppermute(block, ('tm', 'height'), pairs)  12.9 us
    ppermute x11, waiting for transfers between devices, exchange(): return lax.ppermute(block, ('tm', 'height'), pairs)  3.61 us
    pallas_call x1, Pallas kernels, body(): call(functools.partial(middle_kernel, tok, sides, scale), [square(2, bf16...  1.15 us
    pallas_call x1, Pallas kernels, body(): call(functools.partial(pack_kernel, tok), [((2 * tok + extra, width), bf1...  1.13 us
    ppermute x2, starting transfers between devices, swap_cores(): return lax.ppermute(block, 'tm', [(t, t ^ 1) for t in range(times)])  1.12 us
    ppermute x2, waiting for transfers between devices, swap_cores(): return lax.ppermute(block, 'tm', [(t, t ^ 1) for t in range(times)])  1.01 us
    pallas_call x1, Pallas kernels, body(): call(functools.partial(line_query_kernel, tok, chips, heights, sides, sca...  0.85 us
    pallas_call x1, Pallas kernels, body(): call(final_kernel, [(queries.shape, bf16)] * 3, [VMEM] * 3)  0.74 us
  transfers between devices with their start and end apart: 13, of which 5 were waited for; matrix products, arithmetic and copies ran while one was open for 0% of the time, Pallas kernels for 16%

profile of v1, /device:TPU:0, one launch (start us, length us, event | category | flops | bytes accessed | tf_op | source)
XLA Modules:
  0.0 26.2 jit_solution(9869714172687690524)
XLA Ops:
  0.6 1.1 %shard_map.85 = (bf16[448,128]{1,0:T(8,128)(2,1)S(1)}, bf16[592,128]{1,0:T(8,128)(2,1)S(1)}, bf16[976,128]{1,0:T(8,128)(2,1)S(1)}) custom-call(bf16[1,1,2,1,192,128]{5,4,3,2,1,0:T(8,128)(2,1)} %k_ref.1, bf16[1,1,2,1,192,128]{5,4,3,2,1,0:T(8,128)(2,1)} %v_ref.1, bf16[1,1,2,1,192,128]{5,4,3,2,1,0:T(8,128)(2,1)} %q_ref.1, ...), custom_call_target="tpu_custom_call" | custom-call | tf_op jit(solution)/shard_map/pallas_call | solution.py:539
  1.8 0.5 %collective-permute-start = (bf16[976,128]{1,0:T(8,128)(2,1)S(1)}, bf16[976,128]{1,0:T(8,128)(2,1)S(1)}, u32[]{:S(2)}, u32[]{:S(2)}) collective-permute-start(bf16[976,128]{1,0:T(8,128)(2,1)S(1)} %get-tuple-element.37), channel_id=1, source_target_pairs={{0,8},{8,0},{16,24},{24,16},{1,9},{9,1},{17,25},{25,17},{2,10},{10... | collective-permute-start | bytes 749576 | tf_op jit(solution)/shard_map/ppermute | solution.py:534
  2.3 2.7 %collective-permute-start.1 = (bf16[448,128]{1,0:T(8,128)(2,1)S(1)}, bf16[448,128]{1,0:T(8,128)(2,1)S(1)}, u32[]{:S(2)}, u32[]{:S(2)}) collective-permute-start(bf16[448,128]{1,0:T(8,128)(2,1)S(1)} %get-tuple-element.35.kv_ref.refs_0_), channel_id=1, source_target_pairs={{0,10},{2,8},{4,14},{6,12},{8,2},{10,0},{12,6},{14,4},{16,26},{18,... | collective-permute-start | bytes 344072 | tf_op jit(solution)/shard_map/ppermute | solution.py:531
  5.2 2.9 %collective-permute-start.3 = (bf16[416,128]{1,0:T(8,128)(2,1)S(1)}, bf16[416,128]{1,0:T(8,128)(2,1)S(1)}, u32[]{:S(2)}, u32[]{:S(2)}) collective-permute-start(bf16[416,128]{1,0:T(8,128)(2,1)S(1)} %get-tuple-element.38.par_kv_ref.refs_1_), channel_id=1, source_target_pairs={{0,10},{2,8},{4,14},{6,12},{8,2},{10,0},{12,6},{14,4},{16,26},{18,... | collective-permute-start | bytes 319496 | tf_op jit(solution)/shard_map/ppermute | solution.py:531
  8.2 1.6 %collective-permute-start.5 = (bf16[432,128]{1,0:T(8,128)(2,1)S(1)}, bf16[432,128]{1,0:T(8,128)(2,1)S(1)}, u32[]{:S(2)}, u32[]{:S(2)}) collective-permute-start(bf16[432,128]{1,0:T(8,128)(2,1)S(1)} %get-tuple-element.47), channel_id=1, source_target_pairs={{0,24},{2,26},{4,28},{6,30},{8,16},{10,18},{12,20},{14,22},{16,8},... | collective-permute-start | bytes 331784 | tf_op jit(solution)/shard_map/ppermute | solution.py:531
  9.7 0.4 %shard_map.87 = (bf16[384,128]{1,0:T(8,128)(2,1)S(1)}, bf16[384,128]{1,0:T(8,128)(2,1)S(1)}, f32[8,384]{1,0:T(8,128)S(1)}, f32[384,384]{1,0:T(8,128)S(1)}, f32[384,384]{1,0:T(8,128)S(1)}) custom-call(bf16[448,128]{1,0:T(8,128)(2,1)S(1)} %get-tuple-element.35.kv_ref.refs_0_, bf16[416,128]{1,0:T(8,128)(2,1)S(1)} %get-tuple-element.38.par_kv_ref.refs_1_, ...), custom_call_target="tpu_custom_call" | custom-call | tf_op jit(solution)/shard_map/pallas_call | solution.py:562
  10.1 0.5 %shard_map.88 = (f32[384,384]{1,0:T(8,128)S(1)}, f32[384,384]{1,0:T(8,128)S(1)}, f32[8,384]{1,0:T(8,128)S(1)}) custom-call(bf16[384,128]{1,0:T(8,128)(2,1)S(1)} %get-tuple-element.39.q_all, bf16[384,128]{1,0:T(8,128)(2,1)S(1)} %get-tuple-element.40.g_all, f32[8,384]{1,0:T(8,128)S(1)} %get-tuple-element.41.table, f32[384,384]{1,0:T(8,128)S(1)} %get-tuple-element.42.s_own, ...), custom_call_target="tpu_custom_call" | custom-call | flops 20000000000 | tf_op jit(solution)/shard_map/pallas_call | solution.py:574
  10.6 2.3 %collective-permute-done.5.refs_6_.refs_1_.refs_0_ = bf16[432,128]{1,0:T(8,128)(2,1)S(1)} collective-permute-done((bf16[432,128]{1,0:T(8,128)(2,1)S(1)}, bf16[432,128]{1,0:T(8,128)(2,1)S(1)}, u32[]{:S(2)}, u32[]{:S(2)}) %collective-permute-start.5) | collective-permute-done | bytes 110624 | tf_op jit(solution)/shard_map/ppermute | solution.py:531
  13.0 1.4 %collective-permute-start.7 = (bf16[1168,128]{1,0:T(8,128)(2,1)S(1)}, bf16[1168,128]{1,0:T(8,128)(2,1)S(1)}, u32[]{:S(2)}, u32[]{:S(2)}) collective-permute-start(bf16[1168,128]{1,0:T(8,128)(2,1)S(1)} %shard_map.93), channel_id=1, source_target_pairs={{0,10},{2,8},{4,14},{6,12},{8,2},{10,0},{12,6},{14,4},{16,26},{18,... | collective-permute-start | bytes 897032 | tf_op jit(solution)/shard_map/ppermute | solution.py:531
  14.4 0.4 %collective-permute-start.8 = (bf16[1168,128]{1,0:T(8,128)(2,1)S(1)}, bf16[1168,128]{1,0:T(8,128)(2,1)S(1)}, u32[]{:S(2)}, u32[]{:S(2)}) collective-permute-start(bf16[1168,128]{1,0:T(8,128)(2,1)S(1)} %shard_map.93), channel_id=1, source_target_pairs={{0,8},{2,12},{4,10},{6,14},{8,0},{10,4},{12,2},{14,6},{16,24},{18,... | collective-permute-start | bytes 897032 | tf_op jit(solution)/shard_map/ppermute | solution.py:531
  14.7 0.5 %shard_map.89 = (f32[384,384]{1,0:T(8,128)S(1)}, f32[576,256]{1,0:T(8,128)S(1)}, f32[8,384]{1,0:T(8,128)S(1)}) custom-call(bf16[384,128]{1,0:T(8,128)(2,1)S(1)} %get-tuple-element.39.q_all, bf16[384,128]{1,0:T(8,128)(2,1)S(1)} %get-tuple-element.40.g_all, f32[8,384]{1,0:T(8,128)S(1)} %get-tuple-element.41.table, f32[8,384]{1,0:T(8,128)S(1)} %get-tuple-element.46.part, ...), custom_call_target="tpu_custom_call" | custom-call | tf_op jit(solution)/shard_map/pallas_call | solution.py:577
  15.3 1.3 %collective-permute-start.6 = (f32[8,384]{1,0:T(8,128)S(1)}, f32[8,384]{1,0:T(8,128)S(1)}, u32[]{:S(2)}, u32[]{:S(2)}) collective-permute-start(f32[8,384]{1,0:T(8,128)S(1)} %get-tuple-element.50.refs_7_.refs_0_.refs_1_), channel_id=1, source_target_pairs={{0,24},{2,26},{4,28},{6,30},{8,16},{10,18},{12,20},{14,22},{16,8},... | collective-permute-start | bytes 36872 | tf_op jit(solution)/shard_map/ppermute | solution.py:531
  16.6 1.1 %shard_map.90 = (bf16[384,384]{1,0:T(8,128)(2,1)S(1)}, bf16[384,384]{1,0:T(8,128)(2,1)S(1)}, bf16[192,256]{1,0:T(8,128)(2,1)S(1)}, bf16[192,256]{1,0:T(8,128)(2,...) custom-call(bf16[384,128]{1,0:T(8,128)(2,1)S(1)} %get-tuple-element.39.q_all, ...), custom_call_target="tpu_custom_call" | custom-call | flops 20000000000 | tf_op jit(solution)/shard_map/pallas_call | solution.py:584
  17.8 0.7 %collective-permute-done.6.refs_1_ = f32[8,384]{1,0:T(8,128)S(1)} collective-permute-done((f32[8,384]{1,0:T(8,128)S(1)}, f32[8,384]{1,0:T(8,128)S(1)}, u32[]{:S(2)}, u32[]{:S(2)}) %collective-permute-start.6) | collective-permute-done | bytes 12320 | tf_op jit(solution)/shard_map/ppermute | solution.py:531
  18.5 0.9 %collective-permute-start.9 = (f32[8,384]{1,0:T(8,128)S(1)}, f32[8,384]{1,0:T(8,128)S(1)}, u32[]{:S(2)}, u32[]{:S(2)}) collective-permute-start(f32[8,384]{1,0:T(8,128)S(1)} %shard_map.91.note), channel_id=1, source_target_pairs={{0,10},{2,8},{4,14},{6,12},{8,2},{10,0},{12,6},{14,4},{16,26},{18,... | collective-permute-start | bytes 36872 | tf_op jit(solution)/shard_map/ppermute | solution.py:531
  19.5 1.6 %collective-permute-start.11 = (bf16[192,128]{1,0:T(8,128)(2,1)S(1)}, bf16[192,128]{1,0:T(8,128)(2,1)S(1)}, u32[]{:S(2)}, u32[]{:S(2)}) collective-permute-start(bf16[192,128]{1,0:T(8,128)(2,1)S(1)} %shard_map.95), channel_id=1, source_target_pairs={{0,24},{2,26},{4,28},{6,30},{8,16},{10,18},{12,20},{14,22},{16,8},... | collective-permute-start | bytes 147464 | tf_op jit(solution)/shard_map/ppermute | solution.py:531
  21.2 0.5 %shard_map.92 = (f32[2,384,128]{2,1,0:T(8,128)S(1)}, f32[384,128]{1,0:T(8,128)S(1)}) custom-call(bf16[384,128]{1,0:T(8,128)(2,1)S(1)} %get-tuple-element.39.q_all, bf16[384,128]{1,0:T(8,128)(2,1)S(1)} %get-tuple-element.40.g_all, bf16[384,384]{1,0:T(8,128)(2,1)S(1)} %get-tuple-element.51.e_ref, bf16[384,384]{1,0:T(8,128)(2,1)S(1)} %get-tuple-element.52.ds_ref, ...), custom_call_target="tpu_custom_call" | custom-call | tf_op jit(solution)/shard_map/pallas_call | solution.py:603
  21.6 0.4 %collective-permute-done.7.refs_0_ = bf16[1168,128]{1,0:T(8,128)(2,1)S(1)} collective-permute-done((bf16[1168,128]{1,0:T(8,128)(2,1)S(1)}, bf16[1168,128]{1,0:T(8,128)(2,1)S(1)}, u32[]{:S(2)}, u32[]{:S(2)}) %collective-permute-start.7) | collective-permute-done | bytes 299040 | tf_op jit(solution)/shard_map/ppermute | solution.py:531
  22.0 0.8 %shard_map.94 = (bf16[768,384]{1,0:T(8,128)(2,1)S(1)}, bf16[768,384]{1,0:T(8,128)(2,1)S(1)}, bf16[384,256]{1,0:T(8,128)(2,1)S(1)}, bf16[384,256]{1,0:T(8,128)(2,1)S(1)}, f32[8,384]{1,0:T(8,128)S(1)}) custom-call(bf16[448,128]{1,0:T(8,128)(2,1)S(1)} %get-tuple-element.35.kv_ref.refs_0_, bf16[416,128]{1,0:T(8,128)(2,1)S(1)} %get-tuple-element.38.par_kv_ref.refs_1_, ...), custom_call_target="tpu_custom_call" | custom-call | flops 20000000000 | tf_op jit(solution)/shard_map/pallas_call | solution.py:597
  22.9 0.2 collective-permute-done.11.refs_4_
  23.1 0.7 %shard_map.96 = (bf16[2,192,128]{2,1,0:T(8,128)(2,1)S(1)}, bf16[192,128]{1,0:T(8,128)(2,1)S(1)}, bf16[3,192,128]{2,1,0:T(8,128)(2,1)S(1)}) custom-call(f32[2,384,128]{2,1,0:T(8,128)S(1)} %get-tuple-element.56.own_ref, f32[384,128]{1,0:T(8,128)S(1)} %get-tuple-element.57.dq_ref, bf16[768,384]{1,0:T(8,128)(2,1)S(1)} %get-tuple-element.58.e_ref, ...), custom_call_target="tpu_custom_call" | custom-call | tf_op jit(solution)/shard_map/pallas_call | solution.py:608
  23.8 0.6 %collective-permute-start.12 = (bf16[3,192,128]{2,1,0:T(8,128)(2,1)S(1)}, bf16[3,192,128]{2,1,0:T(8,128)(2,1)S(1)}, u32[]{:S(2)}, u32[]{:S(2)}) collective-permute-start(bf16[3,192,128]{2,1,0:T(8,128)(2,1)S(1)} %get-tuple-element.65), channel_id=1, source_target_pairs={{0,8},{8,0},{16,24},{24,16},{1,9},{9,1},{17,25},{25,17},{2,10},{10... | collective-permute-start | bytes 442376 | tf_op jit(solution)/shard_map/ppermute | solution.py:534
  24.4 1.0 %collective-permute-done.12.swap_ref = bf16[3,192,128]{2,1,0:T(8,128)(2,1)S(1)} collective-permute-done((bf16[3,192,128]{2,1,0:T(8,128)(2,1)S(1)}, bf16[3,192,128]{2,1,0:T(8,128)(2,1)S(1)}, u32[]{:S(2)}, u32[]{:S(2)}) %collective-permute-start.12) | collective-permute-done | bytes 147488 | tf_op jit(solution)/shard_map/ppermute | solution.py:534
  25.4 0.7 %shard_map.97 = (bf16[1,1,2,1,192,128]{5,4,3,2,1,0:T(8,128)(2,1)}, bf16[1,1,2,1,192,128]{5,4,3,2,1,0:T(8,128)(2,1)}, bf16[1,1,2,1,192,128]{5,4,3,2,1,0:T(8,128)(2,1)}) custom-call(bf16[2,192,128]{2,1,0:T(8,128)(2,1)S(1)} %get-tuple-element.64.mine_ref, bf16[3,192,128]{2,1,0:T(8,128)(2,1)S(1)} %collective-permute-done.12.swap_ref, ...), custom_call_target="tpu_custom_call" | custom-call | tf_op jit(solution)/shard_map/pallas_call | solution.py:613
  (15 shorter events, 0.5 us)
Async XLA Ops:
  1.8 3.3 %collective-permute-start = (bf16[976,128]{1,0:T(8,128)(2,1)S(1)}, bf16[976,128]{1,0:T(8,128)(2,1)S(1)}, u32[]{:S(2)}, u32[]{:S(2)}) collective-permute-start(bf16[976,128]{1,0:T(8,128)(2,1)S(1)} %get-tuple-element.37), channel_id=1, source_target_pairs={{0,8},{8,0},{16,24},{24,16},{1,9},{9,1},{17,25},{25,17},{2,10},{10... | collective-permute-start | bytes 749576 | tf_op jit(solution)/shard_map/ppermute | solution.py:534
  2.3 7.8 %collective-permute-start.1 = (bf16[448,128]{1,0:T(8,128)(2,1)S(1)}, bf16[448,128]{1,0:T(8,128)(2,1)S(1)}, u32[]{:S(2)}, u32[]{:S(2)}) collective-permute-start(bf16[448,128]{1,0:T(8,128)(2,1)S(1)} %get-tuple-element.35.kv_ref.refs_0_), channel_id=1, source_target_pairs={{0,10},{2,8},{4,14},{6,12},{8,2},{10,0},{12,6},{14,4},{16,26},{18,... | collective-permute-start | bytes 344072 | tf_op jit(solution)/shard_map/ppermute | solution.py:531
  5.0 5.1 %collective-permute-start.2 = (bf16[448,128]{1,0:T(8,128)(2,1)S(1)}, bf16[448,128]{1,0:T(8,128)(2,1)S(1)}, u32[]{:S(2)}, u32[]{:S(2)}) collective-permute-start(bf16[448,128]{1,0:T(8,128)(2,1)S(1)} %get-tuple-element.35.kv_ref.refs_0_), channel_id=1, source_target_pairs={{0,8},{2,12},{4,10},{6,14},{8,0},{10,4},{12,2},{14,6},{16,24},{18,... | collective-permute-start | bytes 344072 | tf_op jit(solution)/shard_map/ppermute | solution.py:531
  5.2 9.5 %collective-permute-start.3 = (bf16[416,128]{1,0:T(8,128)(2,1)S(1)}, bf16[416,128]{1,0:T(8,128)(2,1)S(1)}, u32[]{:S(2)}, u32[]{:S(2)}) collective-permute-start(bf16[416,128]{1,0:T(8,128)(2,1)S(1)} %get-tuple-element.38.par_kv_ref.refs_1_), channel_id=1, source_target_pairs={{0,10},{2,8},{4,14},{6,12},{8,2},{10,0},{12,6},{14,4},{16,26},{18,... | collective-permute-start | bytes 319496 | tf_op jit(solution)/shard_map/ppermute | solution.py:531
  8.1 6.6 %collective-permute-start.4 = (bf16[416,128]{1,0:T(8,128)(2,1)S(1)}, bf16[416,128]{1,0:T(8,128)(2,1)S(1)}, u32[]{:S(2)}, u32[]{:S(2)}) collective-permute-start(bf16[416,128]{1,0:T(8,128)(2,1)S(1)} %get-tuple-element.38.par_kv_ref.refs_1_), channel_id=1, source_target_pairs={{0,8},{2,12},{4,10},{6,14},{8,0},{10,4},{12,2},{14,6},{16,24},{18,... | collective-permute-start | bytes 319496 | tf_op jit(solution)/shard_map/ppermute | solution.py:531
  8.2 4.8 %collective-permute-start.5 = (bf16[432,128]{1,0:T(8,128)(2,1)S(1)}, bf16[432,128]{1,0:T(8,128)(2,1)S(1)}, u32[]{:S(2)}, u32[]{:S(2)}) collective-permute-start(bf16[432,128]{1,0:T(8,128)(2,1)S(1)} %get-tuple-element.47), channel_id=1, source_target_pairs={{0,24},{2,26},{4,28},{6,30},{8,16},{10,18},{12,20},{14,22},{16,8},... | collective-permute-start | bytes 331784 | tf_op jit(solution)/shard_map/ppermute | solution.py:531
  13.0 9.0 %collective-permute-start.7 = (bf16[1168,128]{1,0:T(8,128)(2,1)S(1)}, bf16[1168,128]{1,0:T(8,128)(2,1)S(1)}, u32[]{:S(2)}, u32[]{:S(2)}) collective-permute-start(bf16[1168,128]{1,0:T(8,128)(2,1)S(1)} %shard_map.93), channel_id=1, source_target_pairs={{0,10},{2,8},{4,14},{6,12},{8,2},{10,0},{12,6},{14,4},{16,26},{18,... | collective-permute-start | bytes 897032 | tf_op jit(solution)/shard_map/ppermute | solution.py:531
  14.4 7.6 %collective-permute-start.8 = (bf16[1168,128]{1,0:T(8,128)(2,1)S(1)}, bf16[1168,128]{1,0:T(8,128)(2,1)S(1)}, u32[]{:S(2)}, u32[]{:S(2)}) collective-permute-start(bf16[1168,128]{1,0:T(8,128)(2,1)S(1)} %shard_map.93), channel_id=1, source_target_pairs={{0,8},{2,12},{4,10},{6,14},{8,0},{10,4},{12,2},{14,6},{16,24},{18,... | collective-permute-start | bytes 897032 | tf_op jit(solution)/shard_map/ppermute | solution.py:531
  15.3 3.2 %collective-permute-start.6 = (f32[8,384]{1,0:T(8,128)S(1)}, f32[8,384]{1,0:T(8,128)S(1)}, u32[]{:S(2)}, u32[]{:S(2)}) collective-permute-start(f32[8,384]{1,0:T(8,128)S(1)} %get-tuple-element.50.refs_7_.refs_0_.refs_1_), channel_id=1, source_target_pairs={{0,24},{2,26},{4,28},{6,30},{8,16},{10,18},{12,20},{14,22},{16,8},... | collective-permute-start | bytes 36872 | tf_op jit(solution)/shard_map/ppermute | solution.py:531
  18.5 4.4 %collective-permute-start.9 = (f32[8,384]{1,0:T(8,128)S(1)}, f32[8,384]{1,0:T(8,128)S(1)}, u32[]{:S(2)}, u32[]{:S(2)}) collective-permute-start(f32[8,384]{1,0:T(8,128)S(1)} %shard_map.91.note), channel_id=1, source_target_pairs={{0,10},{2,8},{4,14},{6,12},{8,2},{10,0},{12,6},{14,4},{16,26},{18,... | collective-permute-start | bytes 36872 | tf_op jit(solution)/shard_map/ppermute | solution.py:531
  19.4 3.5 %collective-permute-start.10 = (f32[8,384]{1,0:T(8,128)S(1)}, f32[8,384]{1,0:T(8,128)S(1)}, u32[]{:S(2)}, u32[]{:S(2)}) collective-permute-start(f32[8,384]{1,0:T(8,128)S(1)} %shard_map.91.note), channel_id=1, source_target_pairs={{0,8},{2,12},{4,10},{6,14},{8,0},{10,4},{12,2},{14,6},{16,24},{18,... | collective-permute-start | bytes 36872 | tf_op jit(solution)/shard_map/ppermute | solution.py:531
  19.5 3.6 %collective-permute-start.11 = (bf16[192,128]{1,0:T(8,128)(2,1)S(1)}, bf16[192,128]{1,0:T(8,128)(2,1)S(1)}, u32[]{:S(2)}, u32[]{:S(2)}) collective-permute-start(bf16[192,128]{1,0:T(8,128)(2,1)S(1)} %shard_map.95), channel_id=1, source_target_pairs={{0,24},{2,26},{4,28},{6,30},{8,16},{10,18},{12,20},{14,22},{16,8},... | collective-permute-start | bytes 147464 | tf_op jit(solution)/shard_map/ppermute | solution.py:531
  23.8 1.6 %collective-permute-start.12 = (bf16[3,192,128]{2,1,0:T(8,128)(2,1)S(1)}, bf16[3,192,128]{2,1,0:T(8,128)(2,1)S(1)}, u32[]{:S(2)}, u32[]{:S(2)}) collective-permute-start(bf16[3,192,128]{2,1,0:T(8,128)(2,1)S(1)} %get-tuple-element.65), channel_id=1, source_target_pairs={{0,8},{8,0},{16,24},{24,16},{1,9},{9,1},{17,25},{25,17},{2,10},{10... | collective-permute-start | bytes 442376 | tf_op jit(solution)/shard_map/ppermute | solution.py:534

commit v2 on v1

--- a/solution.py
+++ b/solution.py
@@ -121,7 +121,7 @@
 def line_place(z, line, heights):
     if line == 0:
         return True, lambda flags, dt: flags[3 * dt + 1 : 3 * dt + 2]
-    rising, at = pair(z, line - 1)
+    rising, at = pair(z, 2 - line)
     return within(at, heights), lambda flags, dt: jnp.where(
         rising, flags[3 * dt + 2 : 3 * dt + 3], flags[3 * dt : 3 * dt + 1]
     )
@@ -238,7 +238,7 @@
 
 def score_kernel(tok, chips, heights, sides, scale, q_all, g_all, table, part, *refs):
     qg = (q_all, g_all)
-    keys, foreign, refs = refs[:6], refs[6 : 6 + sides], refs[6 + sides :]
+    foreign, keys, refs = refs[:sides], refs[sides : 6 + sides], refs[6 + sides :]
     s_late, s_far, *notes = refs
     y, c, z = place()
     near = border_is_own(y, c)
@@ -369,7 +369,7 @@
     tops, far_tops = [], []
     tiles = (kv_ref, par_kv_ref)
     for line in (1, 2):
-        rising, z_at = pair(z, line - 1)
+        rising, z_at = pair(z, 2 - line)
         inside = within(z_at, heights)
 
         def at(flags, dt):
@@ -542,14 +542,14 @@
         [HBM] * 6,
         [pltpu.SMEM(window_mask.shape, jnp.int32), pltpu.SemaphoreType.DMA((11,))],
     )(*(pltpu.with_memory_space_constraint(x, pltpu.HBM) for x in arguments))
-    early = [exchange(kv, None, which) for which in range(2)]
+    early = [exchange(kv, None, which) for which in (1, 0)]
     par = swap_cores(other)
     border_shape, two = ((2 * tok + 48, width), bf16), 2 * tok
     par_kv, *borders = call(
         functools.partial(line_kernel, tok), [((2 * tok + 32, width), bf16)] + [border_shape] * sides, [VMEM] * 2
     )(rest, par)
     foreign = [exchange(borders[which], which, None) for which in range(sides)]
-    late = [exchange(par_kv, None, which) for which in range(2)]
+    late = [exchange(par_kv, None, which) for which in (1, 0)]
     tiles = (kv, par_kv, late[0], early[0], late[1], early[1])
     note_shape, raw_shape = ((8, two), f32), ((width, two), f32)
 
@@ -570,15 +570,15 @@
         [((4 * tok + sides * (2 * tok + 16), width), bf16)],
         [VMEM] * (2 + sides),
     )(*qg, *foreign)
-    queries_in = [exchange(message, None, which) for which in range(2)]
+    queries_in = [exchange(message, None, which) for which in (1, 0)]
     s_early, d_early, part = call(
-        functools.partial(early_kernel, tok, scale), [square(2), square(2), note_shape], [VMEM] * 6, cost=20
+        functools.partial(early_kernel, tok, scale), [square(2), square(2), note_shape], [VMEM] * 6
     )(*qg, table, s_own, *early)
     s_late, s_far, *sent = call(
         functools.partial(score_kernel, tok, chips, heights, sides, scale),
         [square(2), far_square()] + [note_shape] * sides,
         [VMEM] * (10 + sides),
-    )(*qg, table, part, *tiles, *foreign)
+    )(*qg, table, part, *foreign, *tiles)
     came = [exchange(sent[which], which, None) for which in range(sides)]
     far_tile = ((sides * tok, 2 * width), bf16)
     e, ds, e_far, ds_far, raw_dq, *far_dq = call(
@@ -591,7 +591,7 @@
     shares = call(
         functools.partial(share_kernel, tok, chips, sides), [((tok, width), bf16)] * sides, [VMEM] * (1 + 2 * sides)
     )(note, *far_dq, *sent)
-    notes = [exchange(note, None, which) for which in range(2)]
+    notes = [exchange(note, None, which) for which in (1, 0)]
     shares = [exchange(share, which, None) for which, share in enumerate(shares)]
     far_pair = ((2 * sides * tok, 2 * width), bf16)
     line_terms = call(

time: 26.4 us -> 25.7 us (0.973)
  waiting for transfers between devices: 4.62 us -> 2.31 us
  starting transfers between devices: 14 us -> 15.7 us
    ppermute x11, waiting for transfers between devices: 3.61 us -> 1.3 us  [exchange(): return lax.ppermute(block, ('tm', 'height'), pairs)]
    ppermute x11, starting transfers between devices: 12.9 us -> 14.5 us  [exchange(): return lax.ppermute(block, ('tm', 'height'), pairs)]
where the time goes in v2:
time: 25.7 us; the launch traced here: 25.5 us
  starting transfers between devices  15.7 us (61%)
  Pallas kernels  6.79 us (26%)
  waiting for transfers between devices  2.31 us (9%)
  between operations  0.75 us (3%)
    ppermute x11, starting transfers between devices, exchange(): return lax.ppermute(block, ('tm', 'height'), pairs)  14.5 us
    ppermute x11, waiting for transfers between devices, exchange(): return lax.ppermute(block, ('tm', 'height'), pairs)  1.3 us
    ppermute x2, starting transfers between devices, swap_cores(): return lax.ppermute(block, 'tm', [(t, t ^ 1) for t in range(times)])  1.19 us
    pallas_call x1, Pallas kernels, body(): call(functools.partial(middle_kernel, tok, sides, scale), [square(2, bf16...  1.17 us
    pallas_call x1, Pallas kernels, body(): call(functools.partial(pack_kernel, tok), [((2 * tok + extra, width), bf1...  1.13 us
    ppermute x2, waiting for transfers between devices, swap_cores(): return lax.ppermute(block, 'tm', [(t, t ^ 1) for t in range(times)])  1.01 us
    pallas_call x1, Pallas kernels, body(): call(functools.partial(line_query_kernel, tok, chips, heights, sides, sca...  0.84 us
    pallas_call x1, Pallas kernels, body(): call(final_kernel, [(queries.shape, bf16)] * 3, [VMEM] * 3)  0.74 us
  transfers between devices with their start and end apart: 13, of which 5 were waited for; matrix products, arithmetic and copies ran while one was open for 0% of the time, Pallas kernels for 16%

profile of v2, /device:TPU:0, one launch (start us, length us, event | category | flops | bytes accessed | tf_op | source)
XLA Modules:
  0.0 25.5 jit_solution(12821269300420372621)
XLA Ops:
  0.6 1.1 %shard_map.85 = (bf16[448,128]{1,0:T(8,128)(2,1)S(1)}, bf16[592,128]{1,0:T(8,128)(2,1)S(1)}, bf16[976,128]{1,0:T(8,128)(2,1)S(1)}) custom-call(bf16[1,1,2,1,192,128]{5,4,3,2,1,0:T(8,128)(2,1)} %k_ref.1, bf16[1,1,2,1,192,128]{5,4,3,2,1,0:T(8,128)(2,1)} %v_ref.1, bf16[1,1,2,1,192,128]{5,4,3,2,1,0:T(8,128)(2,1)} %q_ref.1, ...), custom_call_target="tpu_custom_call" | custom-call | tf_op jit(solution)/shard_map/pallas_call | solution.py:539
  1.8 0.5 %collective-permute-start = (bf16[976,128]{1,0:T(8,128)(2,1)S(1)}, bf16[976,128]{1,0:T(8,128)(2,1)S(1)}, u32[]{:S(2)}, u32[]{:S(2)}) collective-permute-start(bf16[976,128]{1,0:T(8,128)(2,1)S(1)} %get-tuple-element.37), channel_id=1, source_target_pairs={{0,8},{8,0},{16,24},{24,16},{1,9},{9,1},{17,25},{25,17},{2,10},{10... | collective-permute-start | bytes 749576 | tf_op jit(solution)/shard_map/ppermute | solution.py:534
  2.4 3.9 %collective-permute-start.2 = (bf16[448,128]{1,0:T(8,128)(2,1)S(1)}, bf16[448,128]{1,0:T(8,128)(2,1)S(1)}, u32[]{:S(2)}, u32[]{:S(2)}) collective-permute-start(bf16[448,128]{1,0:T(8,128)(2,1)S(1)} %get-tuple-element.35.kv_ref.refs_1_.refs_0_), channel_id=1, source_target_pairs={{0,10},{2,8},{4,14},{6,12},{8,2},{10,0},{12,6},{14,4},{16,26},{18,... | collective-permute-start | bytes 344072 | tf_op jit(solution)/shard_map/ppermute | solution.py:531
  6.4 1.6 %collective-permute-start.3 = (bf16[432,128]{1,0:T(8,128)(2,1)S(1)}, bf16[432,128]{1,0:T(8,128)(2,1)S(1)}, u32[]{:S(2)}, u32[]{:S(2)}) collective-permute-start(bf16[432,128]{1,0:T(8,128)(2,1)S(1)} %get-tuple-element.47), channel_id=1, source_target_pairs={{0,24},{2,26},{4,28},{6,30},{8,16},{10,18},{12,20},{14,22},{16,8},... | collective-permute-start | bytes 331784 | tf_op jit(solution)/shard_map/ppermute | solution.py:531
  8.1 1.6 %collective-permute-start.5 = (bf16[416,128]{1,0:T(8,128)(2,1)S(1)}, bf16[416,128]{1,0:T(8,128)(2,1)S(1)}, u32[]{:S(2)}, u32[]{:S(2)}) collective-permute-start(bf16[416,128]{1,0:T(8,128)(2,1)S(1)} %get-tuple-element.38.par_kv_ref.refs_2_.refs_1_), channel_id=1, source_target_pairs={{0,10},{2,8},{4,14},{6,12},{8,2},{10,0},{12,6},{14,4},{16,26},{18,... | collective-permute-start | bytes 319496 | tf_op jit(solution)/shard_map/ppermute | solution.py:531
  9.7 0.4 %shard_map.87 = (bf16[384,128]{1,0:T(8,128)(2,1)S(1)}, bf16[384,128]{1,0:T(8,128)(2,1)S(1)}, f32[8,384]{1,0:T(8,128)S(1)}, f32[384,384]{1,0:T(8,128)S(1)}, f32[384,384]{1,0:T(8,128)S(1)}) custom-call(bf16[448,128]{1,0:T(8,128)(2,1)S(1)} %get-tuple-element.35.kv_ref.refs_1_.refs_0_, bf16[416,128]{1,0:T(8,128)(2,1)S(1)} %get-tuple-element.38.par_kv_ref.refs_2_.refs_1_, ...), custom_call_target="tpu_custom_call" | custom-call | tf_op jit(solution)/shard_map/pallas_call | solution.py:562
  10.1 0.5 %shard_map.88 = (f32[384,384]{1,0:T(8,128)S(1)}, f32[384,384]{1,0:T(8,128)S(1)}, f32[8,384]{1,0:T(8,128)S(1)}) custom-call(bf16[384,128]{1,0:T(8,128)(2,1)S(1)} %get-tuple-element.39.q_all, bf16[384,128]{1,0:T(8,128)(2,1)S(1)} %get-tuple-element.40.g_all, f32[8,384]{1,0:T(8,128)S(1)} %get-tuple-element.41.table, f32[384,384]{1,0:T(8,128)S(1)} %get-tuple-element.42.s_own, ...), custom_call_target="tpu_custom_call" | custom-call | tf_op jit(solution)/shard_map/pallas_call | solution.py:574
  10.6 0.6 %collective-permute-done.3.refs_0_.refs_6_.refs_1_ = bf16[432,128]{1,0:T(8,128)(2,1)S(1)} collective-permute-done((bf16[432,128]{1,0:T(8,128)(2,1)S(1)}, bf16[432,128]{1,0:T(8,128)(2,1)S(1)}, u32[]{:S(2)}, u32[]{:S(2)}) %collective-permute-start.3) | collective-permute-done | bytes 110624 | tf_op jit(solution)/shard_map/ppermute | solution.py:531
  11.3 0.8 %collective-permute-start.7 = (bf16[1168,128]{1,0:T(8,128)(2,1)S(1)}, bf16[1168,128]{1,0:T(8,128)(2,1)S(1)}, u32[]{:S(2)}, u32[]{:S(2)}) collective-permute-start(bf16[1168,128]{1,0:T(8,128)(2,1)S(1)} %shard_map.93), channel_id=1, source_target_pairs={{0,8},{2,12},{4,10},{6,14},{8,0},{10,4},{12,2},{14,6},{16,24},{18,... | collective-permute-start | bytes 897032 | tf_op jit(solution)/shard_map/ppermute | solution.py:531
  12.0 1.0 %collective-permute-start.8 = (bf16[1168,128]{1,0:T(8,128)(2,1)S(1)}, bf16[1168,128]{1,0:T(8,128)(2,1)S(1)}, u32[]{:S(2)}, u32[]{:S(2)}) collective-permute-start(bf16[1168,128]{1,0:T(8,128)(2,1)S(1)} %shard_map.93), channel_id=1, source_target_pairs={{0,10},{2,8},{4,14},{6,12},{8,2},{10,0},{12,6},{14,4},{16,26},{18,... | collective-permute-start | bytes 897032 | tf_op jit(solution)/shard_map/ppermute | solution.py:531
  13.1 0.5 %shard_map.89 = (f32[384,384]{1,0:T(8,128)S(1)}, f32[576,256]{1,0:T(8,128)S(1)}, f32[8,384]{1,0:T(8,128)S(1)}) custom-call(bf16[384,128]{1,0:T(8,128)(2,1)S(1)} %get-tuple-element.39.q_all, bf16[384,128]{1,0:T(8,128)(2,1)S(1)} %get-tuple-element.40.g_all, f32[8,384]{1,0:T(8,128)S(1)} %get-tuple-element.41.table, f32[8,384]{1,0:T(8,128)S(1)} %get-tuple-element.46.part, ...), custom_call_target="tpu_custom_call" | custom-call | tf_op jit(solution)/shard_map/pallas_call | solution.py:577
  13.6 1.9 %collective-permute-start.6 = (f32[8,384]{1,0:T(8,128)S(1)}, f32[8,384]{1,0:T(8,128)S(1)}, u32[]{:S(2)}, u32[]{:S(2)}) collective-permute-start(f32[8,384]{1,0:T(8,128)S(1)} %get-tuple-element.50.refs_7_.refs_0_.refs_1_), channel_id=1, source_target_pairs={{0,24},{2,26},{4,28},{6,30},{8,16},{10,18},{12,20},{14,22},{16,8},... | collective-permute-start | bytes 36872 | tf_op jit(solution)/shard_map/ppermute | solution.py:531
  15.5 1.2 %shard_map.90 = (bf16[384,384]{1,0:T(8,128)(2,1)S(1)}, bf16[384,384]{1,0:T(8,128)(2,1)S(1)}, bf16[192,256]{1,0:T(8,128)(2,1)S(1)}, bf16[192,256]{1,0:T(8,128)(2,...) custom-call(bf16[384,128]{1,0:T(8,128)(2,1)S(1)} %get-tuple-element.39.q_all, ...), custom_call_target="tpu_custom_call" | custom-call | flops 20000000000 | tf_op jit(solution)/shard_map/pallas_call | solution.py:584
  16.7 0.2 collective-permute-done.6.refs_1_
  16.9 1.0 %collective-permute-start.9 = (f32[8,384]{1,0:T(8,128)S(1)}, f32[8,384]{1,0:T(8,128)S(1)}, u32[]{:S(2)}, u32[]{:S(2)}) collective-permute-start(f32[8,384]{1,0:T(8,128)S(1)} %shard_map.91.note), channel_id=1, source_target_pairs={{0,8},{2,12},{4,10},{6,14},{8,0},{10,4},{12,2},{14,6},{16,24},{18,... | collective-permute-start | bytes 36872 | tf_op jit(solution)/shard_map/ppermute | solution.py:531
  17.9 0.8 %collective-permute-start.10 = (f32[8,384]{1,0:T(8,128)S(1)}, f32[8,384]{1,0:T(8,128)S(1)}, u32[]{:S(2)}, u32[]{:S(2)}) collective-permute-start(f32[8,384]{1,0:T(8,128)S(1)} %shard_map.91.note), channel_id=1, source_target_pairs={{0,10},{2,8},{4,14},{6,12},{8,2},{10,0},{12,6},{14,4},{16,26},{18,... | collective-permute-start | bytes 36872 | tf_op jit(solution)/shard_map/ppermute | solution.py:531
  18.8 1.9 %collective-permute-start.11 = (bf16[192,128]{1,0:T(8,128)(2,1)S(1)}, bf16[192,128]{1,0:T(8,128)(2,1)S(1)}, u32[]{:S(2)}, u32[]{:S(2)}) collective-permute-start(bf16[192,128]{1,0:T(8,128)(2,1)S(1)} %shard_map.95), channel_id=1, source_target_pairs={{0,24},{2,26},{4,28},{6,30},{8,16},{10,18},{12,20},{14,22},{16,8},... | collective-permute-start | bytes 147464 | tf_op jit(solution)/shard_map/ppermute | solution.py:531
  20.6 0.5 %shard_map.92 = (f32[2,384,128]{2,1,0:T(8,128)S(1)}, f32[384,128]{1,0:T(8,128)S(1)}) custom-call(bf16[384,128]{1,0:T(8,128)(2,1)S(1)} %get-tuple-element.39.q_all, bf16[384,128]{1,0:T(8,128)(2,1)S(1)} %get-tuple-element.40.g_all, bf16[384,384]{1,0:T(8,128)(2,1)S(1)} %get-tuple-element.51.e_ref, bf16[384,384]{1,0:T(8,128)(2,1)S(1)} %get-tuple-element.52.ds_ref, ...), custom_call_target="tpu_custom_call" | custom-call | tf_op jit(solution)/shard_map/pallas_call | solution.py:603
  21.2 0.8 %shard_map.94 = (bf16[768,384]{1,0:T(8,128)(2,1)S(1)}, bf16[768,384]{1,0:T(8,128)(2,1)S(1)}, bf16[384,256]{1,0:T(8,128)(2,1)S(1)}, bf16[384,256]{1,0:T(8,128)(2,1)S(1)}, f32[8,384]{1,0:T(8,128)S(1)}) custom-call(bf16[448,128]{1,0:T(8,128)(2,1)S(1)} %get-tuple-element.35.kv_ref.refs_1_.refs_0_, ...), custom_call_target="tpu_custom_call" | custom-call | flops 20000000000 | tf_op jit(solution)/shard_map/pallas_call | solution.py:597
  22.1 0.3 %collective-permute-done.11.refs_4_ = bf16[192,128]{1,0:T(8,128)(2,1)S(1)} collective-permute-done((bf16[192,128]{1,0:T(8,128)(2,1)S(1)}, bf16[192,128]{1,0:T(8,128)(2,1)S(1)}, u32[]{:S(2)}, u32[]{:S(2)}) %collective-permute-start.11) | collective-permute-done | bytes 49184 | tf_op jit(solution)/shard_map/ppermute | solution.py:531
  22.4 0.7 %shard_map.96 = (bf16[2,192,128]{2,1,0:T(8,128)(2,1)S(1)}, bf16[192,128]{1,0:T(8,128)(2,1)S(1)}, bf16[3,192,128]{2,1,0:T(8,128)(2,1)S(1)}) custom-call(f32[2,384,128]{2,1,0:T(8,128)S(1)} %get-tuple-element.56.own_ref, f32[384,128]{1,0:T(8,128)S(1)} %get-tuple-element.57.dq_ref, bf16[768,384]{1,0:T(8,128)(2,1)S(1)} %get-tuple-element.58.e_ref, ...), custom_call_target="tpu_custom_call" | custom-call | tf_op jit(solution)/shard_map/pallas_call | solution.py:608
  23.1 0.7 %collective-permute-start.12 = (bf16[3,192,128]{2,1,0:T(8,128)(2,1)S(1)}, bf16[3,192,128]{2,1,0:T(8,128)(2,1)S(1)}, u32[]{:S(2)}, u32[]{:S(2)}) collective-permute-start(bf16[3,192,128]{2,1,0:T(8,128)(2,1)S(1)} %get-tuple-element.65), channel_id=1, source_target_pairs={{0,8},{8,0},{16,24},{24,16},{1,9},{9,1},{17,25},{25,17},{2,10},{10... | collective-permute-start | bytes 442376 | tf_op jit(solution)/shard_map/ppermute | solution.py:534
  23.8 1.0 %collective-permute-done.12.swap_ref = bf16[3,192,128]{2,1,0:T(8,128)(2,1)S(1)} collective-permute-done((bf16[3,192,128]{2,1,0:T(8,128)(2,1)S(1)}, bf16[3,192,128]{2,1,0:T(8,128)(2,1)S(1)}, u32[]{:S(2)}, u32[]{:S(2)}) %collective-permute-start.12) | collective-permute-done | bytes 147488 | tf_op jit(solution)/shard_map/ppermute | solution.py:534
  24.8 0.7 %shard_map.97 = (bf16[1,1,2,1,192,128]{5,4,3,2,1,0:T(8,128)(2,1)}, bf16[1,1,2,1,192,128]{5,4,3,2,1,0:T(8,128)(2,1)}, bf16[1,1,2,1,192,128]{5,4,3,2,1,0:T(8,128)(2,1)}) custom-call(bf16[2,192,128]{2,1,0:T(8,128)(2,1)S(1)} %get-tuple-element.64.mine_ref, bf16[3,192,128]{2,1,0:T(8,128)(2,1)S(1)} %collective-permute-done.12.swap_ref, ...), custom_call_target="tpu_custom_call" | custom-call | tf_op jit(solution)/shard_map/pallas_call | solution.py:613
  (15 shorter events, 0.6 us)
Async XLA Ops:
  1.8 4.5 %collective-permute-start = (bf16[976,128]{1,0:T(8,128)(2,1)S(1)}, bf16[976,128]{1,0:T(8,128)(2,1)S(1)}, u32[]{:S(2)}, u32[]{:S(2)}) collective-permute-start(bf16[976,128]{1,0:T(8,128)(2,1)S(1)} %get-tuple-element.37), channel_id=1, source_target_pairs={{0,8},{8,0},{16,24},{24,16},{1,9},{9,1},{17,25},{25,17},{2,10},{10... | collective-permute-start | bytes 749576 | tf_op jit(solution)/shard_map/ppermute | solution.py:534
  2.3 7.8 %collective-permute-start.1 = (bf16[448,128]{1,0:T(8,128)(2,1)S(1)}, bf16[448,128]{1,0:T(8,128)(2,1)S(1)}, u32[]{:S(2)}, u32[]{:S(2)}) collective-permute-start(bf16[448,128]{1,0:T(8,128)(2,1)S(1)} %get-tuple-element.35.kv_ref.refs_1_.refs_0_), channel_id=1, source_target_pairs={{0,8},{2,12},{4,10},{6,14},{8,0},{10,4},{12,2},{14,6},{16,24},{18,... | collective-permute-start | bytes 344072 | tf_op jit(solution)/shard_map/ppermute | solution.py:531
  2.4 7.8 %collective-permute-start.2 = (bf16[448,128]{1,0:T(8,128)(2,1)S(1)}, bf16[448,128]{1,0:T(8,128)(2,1)S(1)}, u32[]{:S(2)}, u32[]{:S(2)}) collective-permute-start(bf16[448,128]{1,0:T(8,128)(2,1)S(1)} %get-tuple-element.35.kv_ref.refs_1_.refs_0_), channel_id=1, source_target_pairs={{0,10},{2,8},{4,14},{6,12},{8,2},{10,0},{12,6},{14,4},{16,26},{18,... | collective-permute-start | bytes 344072 | tf_op jit(solution)/shard_map/ppermute | solution.py:531
  6.4 4.9 %collective-permute-start.3 = (bf16[432,128]{1,0:T(8,128)(2,1)S(1)}, bf16[432,128]{1,0:T(8,128)(2,1)S(1)}, u32[]{:S(2)}, u32[]{:S(2)}) collective-permute-start(bf16[432,128]{1,0:T(8,128)(2,1)S(1)} %get-tuple-element.47), channel_id=1, source_target_pairs={{0,24},{2,26},{4,28},{6,30},{8,16},{10,18},{12,20},{14,22},{16,8},... | collective-permute-start | bytes 331784 | tf_op jit(solution)/shard_map/ppermute | solution.py:531
  8.1 5.0 %collective-permute-start.4 = (bf16[416,128]{1,0:T(8,128)(2,1)S(1)}, bf16[416,128]{1,0:T(8,128)(2,1)S(1)}, u32[]{:S(2)}, u32[]{:S(2)}) collective-permute-start(bf16[416,128]{1,0:T(8,128)(2,1)S(1)} %get-tuple-element.38.par_kv_ref.refs_2_.refs_1_), channel_id=1, source_target_pairs={{0,8},{2,12},{4,10},{6,14},{8,0},{10,4},{12,2},{14,6},{16,24},{18,... | collective-permute-start | bytes 319496 | tf_op jit(solution)/shard_map/ppermute | solution.py:531
  8.1 4.9 %collective-permute-start.5 = (bf16[416,128]{1,0:T(8,128)(2,1)S(1)}, bf16[416,128]{1,0:T(8,128)(2,1)S(1)}, u32[]{:S(2)}, u32[]{:S(2)}) collective-permute-start(bf16[416,128]{1,0:T(8,128)(2,1)S(1)} %get-tuple-element.38.par_kv_ref.refs_2_.refs_1_), channel_id=1, source_target_pairs={{0,10},{2,8},{4,14},{6,12},{8,2},{10,0},{12,6},{14,4},{16,26},{18,... | collective-permute-start | bytes 319496 | tf_op jit(solution)/shard_map/ppermute | solution.py:531
  11.3 9.8 %collective-permute-start.7 = (bf16[1168,128]{1,0:T(8,128)(2,1)S(1)}, bf16[1168,128]{1,0:T(8,128)(2,1)S(1)}, u32[]{:S(2)}, u32[]{:S(2)}) collective-permute-start(bf16[1168,128]{1,0:T(8,128)(2,1)S(1)} %shard_map.93), channel_id=1, source_target_pairs={{0,8},{2,12},{4,10},{6,14},{8,0},{10,4},{12,2},{14,6},{16,24},{18,... | collective-permute-start | bytes 897032 | tf_op jit(solution)/shard_map/ppermute | solution.py:531
  12.0 9.1 %collective-permute-start.8 = (bf16[1168,128]{1,0:T(8,128)(2,1)S(1)}, bf16[1168,128]{1,0:T(8,128)(2,1)S(1)}, u32[]{:S(2)}, u32[]{:S(2)}) collective-permute-start(bf16[1168,128]{1,0:T(8,128)(2,1)S(1)} %shard_map.93), channel_id=1, source_target_pairs={{0,10},{2,8},{4,14},{6,12},{8,2},{10,0},{12,6},{14,4},{16,26},{18,... | collective-permute-start | bytes 897032 | tf_op jit(solution)/shard_map/ppermute | solution.py:531
  13.6 3.3 %collective-permute-start.6 = (f32[8,384]{1,0:T(8,128)S(1)}, f32[8,384]{1,0:T(8,128)S(1)}, u32[]{:S(2)}, u32[]{:S(2)}) collective-permute-start(f32[8,384]{1,0:T(8,128)S(1)} %get-tuple-element.50.refs_7_.refs_0_.refs_1_), channel_id=1, source_target_pairs={{0,24},{2,26},{4,28},{6,30},{8,16},{10,18},{12,20},{14,22},{16,8},... | collective-permute-start | bytes 36872 | tf_op jit(solution)/shard_map/ppermute | solution.py:531
  16.9 5.1 %collective-permute-start.9 = (f32[8,384]{1,0:T(8,128)S(1)}, f32[8,384]{1,0:T(8,128)S(1)}, u32[]{:S(2)}, u32[]{:S(2)}) collective-permute-start(f32[8,384]{1,0:T(8,128)S(1)} %shard_map.91.note), channel_id=1, source_target_pairs={{0,8},{2,12},{4,10},{6,14},{8,0},{10,4},{12,2},{14,6},{16,24},{18,... | collective-permute-start | bytes 36872 | tf_op jit(solution)/shard_map/ppermute | solution.py:531
  17.9 4.2 %collective-permute-start.10 = (f32[8,384]{1,0:T(8,128)S(1)}, f32[8,384]{1,0:T(8,128)S(1)}, u32[]{:S(2)}, u32[]{:S(2)}) collective-permute-start(f32[8,384]{1,0:T(8,128)S(1)} %shard_map.91.note), channel_id=1, source_target_pairs={{0,10},{2,8},{4,14},{6,12},{8,2},{10,0},{12,6},{14,4},{16,26},{18,... | collective-permute-start | bytes 36872 | tf_op jit(solution)/shard_map/ppermute | solution.py:531
  18.8 3.6 %collective-permute-start.11 = (bf16[192,128]{1,0:T(8,128)(2,1)S(1)}, bf16[192,128]{1,0:T(8,128)(2,1)S(1)}, u32[]{:S(2)}, u32[]{:S(2)}) collective-permute-start(bf16[192,128]{1,0:T(8,128)(2,1)S(1)} %shard_map.95), channel_id=1, source_target_pairs={{0,24},{2,26},{4,28},{6,30},{8,16},{10,18},{12,20},{14,22},{16,8},... | collective-permute-start | bytes 147464 | tf_op jit(solution)/shard_map/ppermute | solution.py:531
  23.1 1.7 %collective-permute-start.12 = (bf16[3,192,128]{2,1,0:T(8,128)(2,1)S(1)}, bf16[3,192,128]{2,1,0:T(8,128)(2,1)S(1)}, u32[]{:S(2)}, u32[]{:S(2)}) collective-permute-start(bf16[3,192,128]{2,1,0:T(8,128)(2,1)S(1)} %get-tuple-element.65), channel_id=1, source_target_pairs={{0,8},{8,0},{16,24},{24,16},{1,9},{9,1},{17,25},{25,17},{2,10},{10... | collective-permute-start | bytes 442376 | tf_op jit(solution)/shard_map/ppermute | solution.py:534

commit v3 on v2

--- a/solution.py
+++ b/solution.py
@@ -269,15 +269,20 @@
         notes[which][...] = jnp.concatenate([top, total] + far[which] + [jnp.zeros((4, two), f32)], axis=0)
 
 
-def middle_kernel(tok, sides, scale, q_all, g_all, table, s_own, d_own, s_early, d_early, s_late, s_far, *refs):
+def middle_kernel(tok, heights, sides, scale, q_all, g_all, table, s_own, d_own, s_early, d_early, s_late, s_far, *refs):
     qg = (q_all, g_all)
     tiles, foreign, sent = refs[:6], refs[6 : 6 + sides], refs[6 + sides : 6 + 2 * sides]
-    e_ref, ds_ref, e_far, ds_far, dq_ref, *far_dq = refs[6 + 2 * sides :]
-    y, c, _ = place()
+    e_ref, ds_ref, e_far, ds_far, dq_ref, *refs = refs[6 + 2 * sides :]
+    shares, far_dq = refs[:sides], refs[sides:]
+    y, c, z = place()
     near = border_is_own(y, c)
-    f32, bf16 = jnp.float32, jnp.bfloat16
-    dq = jnp.zeros(dq_ref.shape, f32)
-    for line in range(3):
+    bf16 = jnp.bfloat16
+
+    def add(ref, line, value):
+        ref[...] = value if line == 0 else ref[...] + value
+
+    def work(line):
+        dq = 0.0
         for slot in range(2):
             i, at = 2 * line + slot, rows_at(line - 1 if line else slot, tok)
             scores = s_own if line == 0 else s_early if slot == EARLY else s_late
@@ -291,13 +296,11 @@
                 e_ref[rows_at(i, tok), :] = weights.astype(bf16)
                 ds_ref[rows_at(i, tok), :] = low
             dq = dq + dot(tiles[i][rows_at(0, tok), :], low, COLS_T)
-    dq_ref[...] = dq
-    for which in range(sides):
-        far_g = foreign_rows(foreign[which], 1, which, tok)
-        delta = foreign_delta(foreign[which], tok)
-        lanes = foreign_lanes(which, tok, qg[0].shape[1])
-        dq = jnp.zeros(far_dq[which].shape, f32)
-        for line in range(3):
+        add(dq_ref, line, dq)
+        for which in range(sides):
+            far_g = foreign_rows(foreign[which], 1, which, tok)
+            delta = foreign_delta(foreign[which], tok)
+            lanes = foreign_lanes(which, tok, qg[0].shape[1])
             rows = rows_at(3 * which + line, tok)
             own, par = tiles[2 * line], tiles[2 * line + 1]
             key, value = (pick(near, which, own[rows_at(i, tok), :], par[rows_at(i, tok), :]) for i in range(2))
@@ -306,8 +309,19 @@
             if line == 0:
                 e_far[rows_at(which, tok), :] = weights.astype(bf16)
                 ds_far[rows_at(which, tok), :] = low
-            dq = dq + dot(key, low, COLS_T)
-        far_dq[which][...] = dq
+            add(far_dq[which], line, dot(key, low, COLS_T))
+
+    for line in range(3):
+        if line == 0:
+            work(line)
+        else:
+            pl.when(line_place(z, line, heights)[0])(functools.partial(work, line))
+    for which in range(sides):
+        shares[which][...] = border_rows(which, tok, far_dq[which][...].T).astype(bf16)
+
+
+def border_rows(which, tok, block):
+    return block[:tok] if which == 0 else block[block.shape[0] - tok :]
 
 
 def message_kernel(tok, q_all, g_all, *refs):
@@ -346,18 +360,6 @@
     note_ref[...] = jnp.concatenate(rows + [jnp.zeros((8 - len(rows), 2 * tok), jnp.float32)], axis=0)
 
 
-def share_kernel(tok, chips, sides, note, *refs):
-    far_dq, sent, shares = (refs[i * sides : (i + 1) * sides] for i in range(3))
-    y, _, _ = place()
-    width = far_dq[0].shape[0]
-    for which in range(sides):
-        _, y_at = pair(y, which)
-        lanes = foreign_lanes(which, tok, width)
-        factor = jnp.exp(sent[which][2:3, lanes] - note[1 + which : 2 + which, lanes])
-        share = (far_dq[which][...] * jnp.where(within(y_at, chips), factor, 0.0)).T
-        shares[which][...] = (share[:tok] if which == 0 else share[2 * width - tok :]).astype(jnp.bfloat16)
-
-
 def line_query_kernel(tok, chips, heights, sides, scale, kv_ref, par_kv_ref, *refs):
     queries, extras, outs = refs[:2], refs[2:4], refs[4:]
     e_ref, ds_ref, e_far, ds_far, top_ref = outs
@@ -366,11 +368,10 @@
     two = 2 * tok
     width = kv_ref.shape[1]
     f32, bf16 = jnp.float32, jnp.bfloat16
-    tops, far_tops = [], []
     tiles = (kv_ref, par_kv_ref)
-    for line in (1, 2):
-        rising, z_at = pair(z, 2 - line)
-        inside = within(z_at, heights)
+
+    def work(line):
+        rising, _ = pair(z, 2 - line)
 
         def at(flags, dt):
             return jnp.where(rising, flags[3 * dt : 3 * dt + 1], flags[3 * dt + 2 : 3 * dt + 3])
@@ -383,12 +384,10 @@
         scores = []
         for slot in range(2):
             row = flag_row(tok, slot, at, own_flags, par_flags, False)
-            bias = jnp.where(inside, (row - 1.0) * 1e30, -1e30)
-            scores.append(dot(tiles[slot][rows_at(0, tok), :], line_q, ROWS_T) * scale + bias)
-        top = jnp.maximum(*(jnp.max(block, axis=0, keepdims=True) for block in scores))
-        tops.append(top)
+            scores.append(dot(tiles[slot][rows_at(0, tok), :], line_q, ROWS_T) * scale + (row - 1.0) * 1e30)
+        tops = [jnp.maximum(*(jnp.max(block, axis=0, keepdims=True) for block in scores))]
         for slot in range(2):
-            weights = jnp.exp(scores[slot] - top)
+            weights = jnp.exp(scores[slot] - tops[0])
             grads = dot(tiles[slot][rows_at(1, tok), :], line_g, ROWS_T) - delta
             kept = rows_at(2 * (line - 1) + slot, tok)
             e_ref[kept, :] = weights.astype(bf16)
@@ -398,18 +397,22 @@
             y_rising, y_at = pair(y, which)
             flags = ref[pl.ds(2 * tok, 16), :].astype(f32)
             row = far_row(tok, which, jnp.where(y_rising, at(flags, 0), at(flags, 2)))
-            bias = jnp.where(inside & within(y_at, chips), (row - 1.0) * 1e30, -1e30)
+            bias = jnp.where(within(y_at, chips), (row - 1.0) * 1e30, -1e30)
             key, value = (pick(near, which, *(tile[rows_at(i, tok), :] for tile in tiles)) for i in range(2))
             far_q, far_g = (foreign_rows(ref, part, which, tok) for part in range(2))
             block = dot(key, far_q, ROWS_T) * scale + bias
             top = jnp.max(block, axis=0, keepdims=True)
-            far_tops.append(to_lanes(which, tok, top, -1e30))
+            tops.append(to_lanes(which, tok, top, -1e30))
             weights = jnp.exp(block - top)
             grads = dot(value, far_g, ROWS_T) - foreign_delta(ref, tok)
             kept = rows_at(2 * which + line - 1, tok)
             e_far[kept, :] = weights.astype(bf16)
             ds_far[kept, :] = (weights * grads * scale).astype(bf16)
-    top_ref[...] = jnp.concatenate(tops + far_tops + [jnp.zeros((6 - 2 * sides, two), f32)], axis=0)
+        gap = jnp.zeros((7 - sides, two), f32)
+        top_ref[pl.ds(8 * (line - 1), 8), :] = jnp.concatenate(tops + [gap], axis=0)
+
+    for line in (1, 2):
+        pl.when(line_place(z, line, heights)[0])(functools.partial(work, line))
 
 
 def times(block, factor):
@@ -450,37 +453,44 @@
             own_ref[i, rows_at(slot, tok), :] = sums[slot][i]
 
 
-def leave_kernel(tok, chips, sides, own_ref, dq_ref, e_ref, ds_ref, e_far, ds_far, top_ref, *refs):
-    queries, notes, backs = refs[:2], refs[2:4], refs[4 : 4 + sides]
-    mine_ref, mine_q_ref, swap_ref = refs[4 + sides :]
-    y, c, _ = place()
+def leave_kernel(tok, chips, heights, sides, own_ref, dq_ref, note, e_ref, ds_ref, e_far, ds_far, top_ref, *refs):
+    queries, notes, refs = refs[:2], refs[2:4], refs[4:]
+    came, backs, (mine_ref, mine_q_ref, swap_ref, sums) = refs[:sides], refs[sides : 2 * sides], refs[2 * sides :]
+    y, c, z = place()
     near = border_is_own(y, c)
     f32, bf16 = jnp.float32, jnp.bfloat16
     width = dq_ref.shape[1]
-    sums = [[own_ref[i, rows_at(slot, tok), :] for i in range(2)] for slot in range(2)]
-    for line in (1, 2):
-        note = notes[line - 1]
-        factor = jnp.exp(top_ref[line - 1 : line, :] - note[0:1, :])
+    sums[...] = own_ref[...]
+
+    def work(line):
+        factor = jnp.exp(top_ref[8 * line - 8 : 8 * line - 7, :] - notes[line - 1][0:1, :])
         scaled = [times(queries[line - 1][pl.ds(part * 2 * tok, 2 * tok), :], factor) for part in range(2)]
         far = []
         for which in range(sides):
-            lanes = foreign_lanes(which, tok, width)
-            at = 2 + sides * (line - 1) + which
-            far_factor = jnp.exp(top_ref[at : at + 1, lanes] - note[1 + which : 2 + which, lanes])
+            lanes, at = foreign_lanes(which, tok, width), 8 * line - 7 + which
+            far_factor = jnp.exp(top_ref[at : at + 1, lanes] - notes[line - 1][1 + which : 2 + which, lanes])
             rows = [foreign_rows(far_part(queries[line - 1], which, tok), part, which, tok) for part in range(2)]
             far.append(
                 (e_far, ds_far, rows_at(2 * which + line - 1, tok), [times(block, far_factor) for block in rows])
             )
         more = key_sums(tok, near, line - 1, e_ref, ds_ref, scaled, far)
-        sums = [[sums[slot][i] + more[slot][i] for i in range(2)] for slot in range(2)]
+        for slot in range(2):
+            for i in range(2):
+                sums[i, rows_at(slot, tok), :] += more[slot][i]
+
+    for line in (1, 2):
+        pl.when(line_place(z, line, heights)[0])(functools.partial(work, line))
     for i in range(2):
-        mine_ref[i], swap_ref[i] = sums[0][i].astype(bf16), sums[1][i].astype(bf16)
+        mine_ref[i], swap_ref[i] = sums[i, rows_at(0, tok), :].astype(bf16), sums[i, rows_at(1, tok), :].astype(bf16)
     tiles = []
     for tile in range(2):
         value = dq_ref[rows_at(tile, tok), :]
         if tile < sides:
             _, y_at = pair(y, tile)
-            value = value + jnp.where(within(y_at, chips), backs[tile][...].astype(f32), 0.0)
+            lanes = foreign_lanes(tile, tok, width)
+            factor = jnp.exp(came[tile][2:3, lanes] - note[0:1, lanes])
+            column = border_rows(tile, tok, jnp.broadcast_to(factor, (width, 2 * width)).T)
+            value = value + jnp.where(within(y_at, chips), backs[tile][...].astype(f32) * column, 0.0)
         tiles.append(value.astype(bf16))
     mine_q_ref[...] = jnp.where(near, tiles[0], tiles[1])
     swap_ref[2] = jnp.where(near, tiles[1], tiles[0])
@@ -581,22 +591,20 @@
     )(*qg, table, part, *foreign, *tiles)
     came = [exchange(sent[which], which, None) for which in range(sides)]
     far_tile = ((sides * tok, 2 * width), bf16)
-    e, ds, e_far, ds_far, raw_dq, *far_dq = call(
-        functools.partial(middle_kernel, tok, sides, scale),
-        [square(2, bf16)] * 2 + [far_tile] * 2 + [raw_shape] + [((width, 2 * width), f32)] * sides,
+    e, ds, e_far, ds_far, raw_dq, *shares = call(
+        functools.partial(middle_kernel, tok, heights, sides, scale),
+        [square(2, bf16)] * 2 + [far_tile] * 2 + [raw_shape] + [((tok, width), bf16)] * sides,
         [VMEM] * (15 + 2 * sides),
+        [pltpu.VMEM((width, 2 * width), f32)] * sides,
         cost=20,
     )(*qg, table, s_own, d_own, s_early, d_early, s_late, s_far, *tiles, *foreign, *sent)
     (note,) = call(functools.partial(total_kernel, tok, chips, sides), [note_shape], [VMEM] * (2 * sides))(*sent, *came)
-    shares = call(
-        functools.partial(share_kernel, tok, chips, sides), [((tok, width), bf16)] * sides, [VMEM] * (1 + 2 * sides)
-    )(note, *far_dq, *sent)
     notes = [exchange(note, None, which) for which in (1, 0)]
     shares = [exchange(share, which, None) for which, share in enumerate(shares)]
     far_pair = ((2 * sides * tok, 2 * width), bf16)
     line_terms = call(
         functools.partial(line_query_kernel, tok, chips, heights, sides, scale),
-        [square(4, bf16)] * 2 + [far_pair] * 2 + [note_shape],
+        [square(4, bf16)] * 2 + [far_pair] * 2 + [((16, two), f32)],
         [VMEM] * 6,
         cost=20,
     )(kv, par_kv, *queries_in, *late)
@@ -606,10 +614,11 @@
         [VMEM] * (8 + 2 * sides),
     )(*qg, e, ds, e_far, ds_far, raw_dq, note, *sent, *foreign)
     mine, mine_q, leaving = call(
-        functools.partial(leave_kernel, tok, chips, sides),
+        functools.partial(leave_kernel, tok, chips, heights, sides),
         [tile_shape, ((tok, width), bf16), ((3, tok, width), bf16)],
-        [VMEM] * (11 + sides),
-    )(own, dq, *line_terms, *queries_in, *notes, *shares)
+        [VMEM] * (12 + 2 * sides),
+        [pltpu.VMEM((2, two, width), f32)],
+    )(own, dq, note, *line_terms, *queries_in, *notes, *came, *shares)
     return call(final_kernel, [(queries.shape, bf16)] * 3, [VMEM] * 3)(mine, swap_cores(leaving), mine_q)
 
 

time: 25.7 us -> 24.8 us (0.965)
  starting transfers between devices: 15.7 us -> 14.2 us
  waiting for transfers between devices: 2.31 us -> 3.3 us
  Pallas kernels: 6.79 us -> 6.3 us
    ppermute x11, starting transfers between devices: 14.5 us -> 13.2 us  [exchange(): return lax.ppermute(block, ('tm', 'height'), pairs)]
    ppermute x11, waiting for transfers between devices: 1.3 us -> 2.29 us  [exchange(): return lax.ppermute(block, ('tm', 'height'), pairs)]
    pallas_call x1, Pallas kernels: 0.84 us -> 0.49 us  [body(): call(functools.partial(line_query_kernel, tok, chips, heights, sides, sca...]
    pallas_call x3 -> x2, Pallas kernels: 1.98 us -> 1.84 us  [the longest x1 1.2 us: body(): call(functools.partial(middle_kernel, tok, heights, sides, scale), [squar...]
  transfers between devices with their start and end apart: 13 -> 13, of which waited for: 5 -> 4; matrix products, arithmetic and copies ran while one was open for 0% -> 0% of each run, Pallas kernels for 16% -> 15%
where the time goes in v3:
time: 24.8 us; the launch traced here: 24.5 us
  starting transfers between devices  14.2 us (57%)
  Pallas kernels  6.3 us (25%)
  waiting for transfers between devices  3.3 us (13%)
  between operations  0.75 us (3%)
    ppermute x11, starting transfers between devices, exchange(): return lax.ppermute(block, ('tm', 'height'), pairs)  13.2 us
    ppermute x11, waiting for transfers between devices, exchange(): return lax.ppermute(block, ('tm', 'height'), pairs)  2.29 us
    pallas_call x1, Pallas kernels, body(): call(functools.partial(middle_kernel, tok, heights, sides, scale), [squar...  1.2 us
    pallas_call x1, Pallas kernels, body(): call(functools.partial(pack_kernel, tok), [((2 * tok + extra, width), bf1...  1.13 us
    ppermute x2, waiting for transfers between devices, swap_cores(): return lax.ppermute(block, 'tm', [(t, t ^ 1) for t in range(times)])  1.01 us
    ppermute x2, starting transfers between devices, swap_cores(): return lax.ppermute(block, 'tm', [(t, t ^ 1) for t in range(times)])  0.96 us
    pallas_call x1, Pallas kernels, body(): call(final_kernel, [(queries.shape, bf16)] * 3, [VMEM] * 3)  0.74 us
    pallas_call x1, Pallas kernels, body(): call(functools.partial(leave_kernel, tok, chips, heights, sides), [tile_s...  0.64 us
  transfers between devices with their start and end apart: 13, of which 4 were waited for; matrix products, arithmetic and copies ran while one was open for 0% of the time, Pallas kernels for 15%

profile of v3, /device:TPU:0, one launch (start us, length us, event | category | flops | bytes accessed | tf_op | source)
XLA Modules:
  0.0 24.5 jit_solution(14784634511565410333)
XLA Ops:
  0.6 1.1 %shard_map.85 = (bf16[448,128]{1,0:T(8,128)(2,1)S(1)}, bf16[592,128]{1,0:T(8,128)(2,1)S(1)}, bf16[976,128]{1,0:T(8,128)(2,1)S(1)}) custom-call(bf16[1,1,2,1,192,128]{5,4,3,2,1,0:T(8,128)(2,1)} %k_ref.1, bf16[1,1,2,1,192,128]{5,4,3,2,1,0:T(8,128)(2,1)} %v_ref.1, bf16[1,1,2,1,192,128]{5,4,3,2,1,0:T(8,128)(2,1)} %q_ref.1, ...), custom_call_target="tpu_custom_call" | custom-call | tf_op jit(solution)/shard_map/pallas_call | solution.py:549
  1.8 0.5 %collective-permute-start = (bf16[976,128]{1,0:T(8,128)(2,1)S(1)}, bf16[976,128]{1,0:T(8,128)(2,1)S(1)}, u32[]{:S(2)}, u32[]{:S(2)}) collective-permute-start(bf16[976,128]{1,0:T(8,128)(2,1)S(1)} %get-tuple-element.37), channel_id=1, source_target_pairs={{0,8},{8,0},{16,24},{24,16},{1,9},{9,1},{17,25},{25,17},{2,10},{10... | collective-permute-start | bytes 749576 | tf_op jit(solution)/shard_map/ppermute | solution.py:544
  2.4 3.9 %collective-permute-start.2 = (bf16[448,128]{1,0:T(8,128)(2,1)S(1)}, bf16[448,128]{1,0:T(8,128)(2,1)S(1)}, u32[]{:S(2)}, u32[]{:S(2)}) collective-permute-start(bf16[448,128]{1,0:T(8,128)(2,1)S(1)} %get-tuple-element.35.kv_ref.refs_1_.refs_0_), channel_id=1, source_target_pairs={{0,10},{2,8},{4,14},{6,12},{8,2},{10,0},{12,6},{14,4},{16,26},{18,... | collective-permute-start | bytes 344072 | tf_op jit(solution)/shard_map/ppermute | solution.py:541
  6.2 0.2 shard_map.86
  6.4 1.6 %collective-permute-start.3 = (bf16[432,128]{1,0:T(8,128)(2,1)S(1)}, bf16[432,128]{1,0:T(8,128)(2,1)S(1)}, u32[]{:S(2)}, u32[]{:S(2)}) collective-permute-start(bf16[432,128]{1,0:T(8,128)(2,1)S(1)} %get-tuple-element.47), channel_id=1, source_target_pairs={{0,24},{2,26},{4,28},{6,30},{8,16},{10,18},{12,20},{14,22},{16,8},... | collective-permute-start | bytes 331784 | tf_op jit(solution)/shard_map/ppermute | solution.py:541
  8.1 1.6 %collective-permute-start.5 = (bf16[416,128]{1,0:T(8,128)(2,1)S(1)}, bf16[416,128]{1,0:T(8,128)(2,1)S(1)}, u32[]{:S(2)}, u32[]{:S(2)}) collective-permute-start(bf16[416,128]{1,0:T(8,128)(2,1)S(1)} %get-tuple-element.38.par_kv_ref.refs_2_.refs_1_), channel_id=1, source_target_pairs={{0,10},{2,8},{4,14},{6,12},{8,2},{10,0},{12,6},{14,4},{16,26},{18,... | collective-permute-start | bytes 319496 | tf_op jit(solution)/shard_map/ppermute | solution.py:541
  9.7 0.4 %shard_map.87 = (bf16[384,128]{1,0:T(8,128)(2,1)S(1)}, bf16[384,128]{1,0:T(8,128)(2,1)S(1)}, f32[8,384]{1,0:T(8,128)S(1)}, f32[384,384]{1,0:T(8,128)S(1)}, f32[384,384]{1,0:T(8,128)S(1)}) custom-call(bf16[448,128]{1,0:T(8,128)(2,1)S(1)} %get-tuple-element.35.kv_ref.refs_1_.refs_0_, bf16[416,128]{1,0:T(8,128)(2,1)S(1)} %get-tuple-element.38.par_kv_ref.refs_2_.refs_1_, ...), custom_call_target="tpu_custom_call" | custom-call | tf_op jit(solution)/shard_map/pallas_call | solution.py:572
  10.1 0.5 %shard_map.88 = (f32[384,384]{1,0:T(8,128)S(1)}, f32[384,384]{1,0:T(8,128)S(1)}, f32[8,384]{1,0:T(8,128)S(1)}) custom-call(bf16[384,128]{1,0:T(8,128)(2,1)S(1)} %get-tuple-element.39.q_all, bf16[384,128]{1,0:T(8,128)(2,1)S(1)} %get-tuple-element.40.g_all, f32[8,384]{1,0:T(8,128)S(1)} %get-tuple-element.41.table, f32[384,384]{1,0:T(8,128)S(1)} %get-tuple-element.42.s_own, ...), custom_call_target="tpu_custom_call" | custom-call | tf_op jit(solution)/shard_map/pallas_call | solution.py:584
  10.6 0.6 %collective-permute-done.3.refs_0_.refs_6_.refs_1_ = bf16[432,128]{1,0:T(8,128)(2,1)S(1)} collective-permute-done((bf16[432,128]{1,0:T(8,128)(2,1)S(1)}, bf16[432,128]{1,0:T(8,128)(2,1)S(1)}, u32[]{:S(2)}, u32[]{:S(2)}) %collective-permute-start.3) | collective-permute-done | bytes 110624 | tf_op jit(solution)/shard_map/ppermute | solution.py:541
  11.3 0.8 %collective-permute-start.7 = (bf16[1168,128]{1,0:T(8,128)(2,1)S(1)}, bf16[1168,128]{1,0:T(8,128)(2,1)S(1)}, u32[]{:S(2)}, u32[]{:S(2)}) collective-permute-start(bf16[1168,128]{1,0:T(8,128)(2,1)S(1)} %shard_map.93), channel_id=1, source_target_pairs={{0,8},{2,12},{4,10},{6,14},{8,0},{10,4},{12,2},{14,6},{16,24},{18,... | collective-permute-start | bytes 897032 | tf_op jit(solution)/shard_map/ppermute | solution.py:541
  12.0 1.0 %collective-permute-start.8 = (bf16[1168,128]{1,0:T(8,128)(2,1)S(1)}, bf16[1168,128]{1,0:T(8,128)(2,1)S(1)}, u32[]{:S(2)}, u32[]{:S(2)}) collective-permute-start(bf16[1168,128]{1,0:T(8,128)(2,1)S(1)} %shard_map.93), channel_id=1, source_target_pairs={{0,10},{2,8},{4,14},{6,12},{8,2},{10,0},{12,6},{14,4},{16,26},{18,... | collective-permute-start | bytes 897032 | tf_op jit(solution)/shard_map/ppermute | solution.py:541
  13.1 0.5 %shard_map.89 = (f32[384,384]{1,0:T(8,128)S(1)}, f32[576,256]{1,0:T(8,128)S(1)}, f32[8,384]{1,0:T(8,128)S(1)}) custom-call(bf16[384,128]{1,0:T(8,128)(2,1)S(1)} %get-tuple-element.39.q_all, bf16[384,128]{1,0:T(8,128)(2,1)S(1)} %get-tuple-element.40.g_all, f32[8,384]{1,0:T(8,128)S(1)} %get-tuple-element.41.table, f32[8,384]{1,0:T(8,128)S(1)} %get-tuple-element.46.part, ...), custom_call_target="tpu_custom_call" | custom-call | tf_op jit(solution)/shard_map/pallas_call | solution.py:587
  13.6 1.9 %collective-permute-start.6 = (f32[8,384]{1,0:T(8,128)S(1)}, f32[8,384]{1,0:T(8,128)S(1)}, u32[]{:S(2)}, u32[]{:S(2)}) collective-permute-start(f32[8,384]{1,0:T(8,128)S(1)} %get-tuple-element.50.refs_7_.refs_0_), channel_id=1, source_target_pairs={{0,24},{2,26},{4,28},{6,30},{8,16},{10,18},{12,20},{14,22},{16,8},... | collective-permute-start | bytes 36872 | tf_op jit(solution)/shard_map/ppermute | solution.py:541
  15.5 1.2 %shard_map.90 = (bf16[384,384]{1,0:T(8,128)(2,1)S(1)}, bf16[384,384]{1,0:T(8,128)(2,1)S(1)}, bf16[192,256]{1,0:T(8,128)(2,1)S(1)}, bf16[192,256]{1,0:T(8,128)(2,...) custom-call(bf16[384,128]{1,0:T(8,128)(2,1)S(1)} %get-tuple-element.39.q_all, ...), custom_call_target="tpu_custom_call" | custom-call | flops 20000000000 | tf_op jit(solution)/shard_map/pallas_call | solution.py:594
  16.8 0.1 collective-permute-done.6.refs_1_.refs_4_
  16.9 1.0 %collective-permute-start.9 = (f32[8,384]{1,0:T(8,128)S(1)}, f32[8,384]{1,0:T(8,128)S(1)}, u32[]{:S(2)}, u32[]{:S(2)}) collective-permute-start(f32[8,384]{1,0:T(8,128)S(1)} %shard_map.91.note), channel_id=1, source_target_pairs={{0,8},{2,12},{4,10},{6,14},{8,0},{10,4},{12,2},{14,6},{16,24},{18,... | collective-permute-start | bytes 36872 | tf_op jit(solution)/shard_map/ppermute | solution.py:541
  17.9 1.3 %collective-permute-start.10 = (f32[8,384]{1,0:T(8,128)S(1)}, f32[8,384]{1,0:T(8,128)S(1)}, u32[]{:S(2)}, u32[]{:S(2)}) collective-permute-start(f32[8,384]{1,0:T(8,128)S(1)} %shard_map.91.note), channel_id=1, source_target_pairs={{0,10},{2,8},{4,14},{6,12},{8,2},{10,0},{12,6},{14,4},{16,26},{18,... | collective-permute-start | bytes 36872 | tf_op jit(solution)/shard_map/ppermute | solution.py:541
  19.2 0.5 %shard_map.92 = (f32[2,384,128]{2,1,0:T(8,128)S(1)}, f32[384,128]{1,0:T(8,128)S(1)}) custom-call(bf16[384,128]{1,0:T(8,128)(2,1)S(1)} %get-tuple-element.39.q_all, bf16[384,128]{1,0:T(8,128)(2,1)S(1)} %get-tuple-element.40.g_all, bf16[384,384]{1,0:T(8,128)(2,1)S(1)} %get-tuple-element.51.e_ref, bf16[384,384]{1,0:T(8,128)(2,1)S(1)} %get-tuple-element.52.ds_ref, ...), custom_call_target="tpu_custom_call" | custom-call | tf_op jit(solution)/shard_map/pallas_call | solution.py:611
  19.7 1.5 %collective-permute-done.8.refs_1_ = bf16[1168,128]{1,0:T(8,128)(2,1)S(1)} collective-permute-done((bf16[1168,128]{1,0:T(8,128)(2,1)S(1)}, bf16[1168,128]{1,0:T(8,128)(2,1)S(1)}, u32[]{:S(2)}, u32[]{:S(2)}) %collective-permute-start.8) | collective-permute-done | bytes 299040 | tf_op jit(solution)/shard_map/ppermute | solution.py:541
  21.2 0.5 %shard_map.94 = (bf16[768,384]{1,0:T(8,128)(2,1)S(1)}, bf16[768,384]{1,0:T(8,128)(2,1)S(1)}, bf16[384,256]{1,0:T(8,128)(2,1)S(1)}, bf16[384,256]{1,0:T(8,128)(2,1)S(1)}, f32[16,384]{1,0:T(8,128)S(1)}) custom-call(bf16[448,128]{1,0:T(8,128)(2,1)S(1)} %get-tuple-element.35.kv_ref.refs_1_.refs_0_, ...), custom_call_target="tpu_custom_call" | custom-call | flops 20000000000 | tf_op jit(solution)/shard_map/pallas_call | solution.py:605
  21.7 0.6 %shard_map.95 = (bf16[2,192,128]{2,1,0:T(8,128)(2,1)S(1)}, bf16[192,128]{1,0:T(8,128)(2,1)S(1)}, bf16[3,192,128]{2,1,0:T(8,128)(2,1)S(1)}) custom-call(f32[2,384,128]{2,1,0:T(8,128)S(1)} %get-tuple-element.56.own_ref, f32[384,128]{1,0:T(8,128)S(1)} %get-tuple-element.57.dq_ref, f32[8,384]{1,0:T(8,128)S(1)} %shard_map.91.note, ...), custom_call_target="tpu_custom_call" | custom-call | tf_op jit(solution)/shard_map/pallas_call | solution.py:616
  22.4 0.4 %collective-permute-start.12 = (bf16[3,192,128]{2,1,0:T(8,128)(2,1)S(1)}, bf16[3,192,128]{2,1,0:T(8,128)(2,1)S(1)}, u32[]{:S(2)}, u32[]{:S(2)}) collective-permute-start(bf16[3,192,128]{2,1,0:T(8,128)(2,1)S(1)} %get-tuple-element.65), channel_id=1, source_target_pairs={{0,8},{8,0},{16,24},{24,16},{1,9},{9,1},{17,25},{25,17},{2,10},{10... | collective-permute-start | bytes 442376 | tf_op jit(solution)/shard_map/ppermute | solution.py:544
  22.8 1.0 %collective-permute-done.12.swap_ref = bf16[3,192,128]{2,1,0:T(8,128)(2,1)S(1)} collective-permute-done((bf16[3,192,128]{2,1,0:T(8,128)(2,1)S(1)}, bf16[3,192,128]{2,1,0:T(8,128)(2,1)S(1)}, u32[]{:S(2)}, u32[]{:S(2)}) %collective-permute-start.12) | collective-permute-done | bytes 147488 | tf_op jit(solution)/shard_map/ppermute | solution.py:544
  23.8 0.7 %shard_map.96 = (bf16[1,1,2,1,192,128]{5,4,3,2,1,0:T(8,128)(2,1)}, bf16[1,1,2,1,192,128]{5,4,3,2,1,0:T(8,128)(2,1)}, bf16[1,1,2,1,192,128]{5,4,3,2,1,0:T(8,128)(2,1)}) custom-call(bf16[2,192,128]{2,1,0:T(8,128)(2,1)S(1)} %get-tuple-element.64.mine_ref, bf16[3,192,128]{2,1,0:T(8,128)(2,1)S(1)} %collective-permute-done.12.swap_ref, ...), custom_call_target="tpu_custom_call" | custom-call | tf_op jit(solution)/shard_map/pallas_call | solution.py:622
  (14 shorter events, 0.3 us)
Async XLA Ops:
  1.8 4.5 %collective-permute-start = (bf16[976,128]{1,0:T(8,128)(2,1)S(1)}, bf16[976,128]{1,0:T(8,128)(2,1)S(1)}, u32[]{:S(2)}, u32[]{:S(2)}) collective-permute-start(bf16[976,128]{1,0:T(8,128)(2,1)S(1)} %get-tuple-element.37), channel_id=1, source_target_pairs={{0,8},{8,0},{16,24},{24,16},{1,9},{9,1},{17,25},{25,17},{2,10},{10... | collective-permute-start | bytes 749576 | tf_op jit(solution)/shard_map/ppermute | solution.py:544
  2.3 7.8 %collective-permute-start.1 = (bf16[448,128]{1,0:T(8,128)(2,1)S(1)}, bf16[448,128]{1,0:T(8,128)(2,1)S(1)}, u32[]{:S(2)}, u32[]{:S(2)}) collective-permute-start(bf16[448,128]{1,0:T(8,128)(2,1)S(1)} %get-tuple-element.35.kv_ref.refs_1_.refs_0_), channel_id=1, source_target_pairs={{0,8},{2,12},{4,10},{6,14},{8,0},{10,4},{12,2},{14,6},{16,24},{18,... | collective-permute-start | bytes 344072 | tf_op jit(solution)/shard_map/ppermute | solution.py:541
  2.4 7.8 %collective-permute-start.2 = (bf16[448,128]{1,0:T(8,128)(2,1)S(1)}, bf16[448,128]{1,0:T(8,128)(2,1)S(1)}, u32[]{:S(2)}, u32[]{:S(2)}) collective-permute-start(bf16[448,128]{1,0:T(8,128)(2,1)S(1)} %get-tuple-element.35.kv_ref.refs_1_.refs_0_), channel_id=1, source_target_pairs={{0,10},{2,8},{4,14},{6,12},{8,2},{10,0},{12,6},{14,4},{16,26},{18,... | collective-permute-start | bytes 344072 | tf_op jit(solution)/shard_map/ppermute | solution.py:541
  6.4 4.9 %collective-permute-start.3 = (bf16[432,128]{1,0:T(8,128)(2,1)S(1)}, bf16[432,128]{1,0:T(8,128)(2,1)S(1)}, u32[]{:S(2)}, u32[]{:S(2)}) collective-permute-start(bf16[432,128]{1,0:T(8,128)(2,1)S(1)} %get-tuple-element.47), channel_id=1, source_target_pairs={{0,24},{2,26},{4,28},{6,30},{8,16},{10,18},{12,20},{14,22},{16,8},... | collective-permute-start | bytes 331784 | tf_op jit(solution)/shard_map/ppermute | solution.py:541
  8.1 5.0 %collective-permute-start.4 = (bf16[416,128]{1,0:T(8,128)(2,1)S(1)}, bf16[416,128]{1,0:T(8,128)(2,1)S(1)}, u32[]{:S(2)}, u32[]{:S(2)}) collective-permute-start(bf16[416,128]{1,0:T(8,128)(2,1)S(1)} %get-tuple-element.38.par_kv_ref.refs_2_.refs_1_), channel_id=1, source_target_pairs={{0,8},{2,12},{4,10},{6,14},{8,0},{10,4},{12,2},{14,6},{16,24},{18,... | collective-permute-start | bytes 319496 | tf_op jit(solution)/shard_map/ppermute | solution.py:541
  8.1 4.9 %collective-permute-start.5 = (bf16[416,128]{1,0:T(8,128)(2,1)S(1)}, bf16[416,128]{1,0:T(8,128)(2,1)S(1)}, u32[]{:S(2)}, u32[]{:S(2)}) collective-permute-start(bf16[416,128]{1,0:T(8,128)(2,1)S(1)} %get-tuple-element.38.par_kv_ref.refs_2_.refs_1_), channel_id=1, source_target_pairs={{0,10},{2,8},{4,14},{6,12},{8,2},{10,0},{12,6},{14,4},{16,26},{18,... | collective-permute-start | bytes 319496 | tf_op jit(solution)/shard_map/ppermute | solution.py:541
  11.3 8.4 %collective-permute-start.7 = (bf16[1168,128]{1,0:T(8,128)(2,1)S(1)}, bf16[1168,128]{1,0:T(8,128)(2,1)S(1)}, u32[]{:S(2)}, u32[]{:S(2)}) collective-permute-start(bf16[1168,128]{1,0:T(8,128)(2,1)S(1)} %shard_map.93), channel_id=1, source_target_pairs={{0,8},{2,12},{4,10},{6,14},{8,0},{10,4},{12,2},{14,6},{16,24},{18,... | collective-permute-start | bytes 897032 | tf_op jit(solution)/shard_map/ppermute | solution.py:541
  12.0 9.1 %collective-permute-start.8 = (bf16[1168,128]{1,0:T(8,128)(2,1)S(1)}, bf16[1168,128]{1,0:T(8,128)(2,1)S(1)}, u32[]{:S(2)}, u32[]{:S(2)}) collective-permute-start(bf16[1168,128]{1,0:T(8,128)(2,1)S(1)} %shard_map.93), channel_id=1, source_target_pairs={{0,10},{2,8},{4,14},{6,12},{8,2},{10,0},{12,6},{14,4},{16,26},{18,... | collective-permute-start | bytes 897032 | tf_op jit(solution)/shard_map/ppermute | solution.py:541
  13.6 3.3 %collective-permute-start.6 = (f32[8,384]{1,0:T(8,128)S(1)}, f32[8,384]{1,0:T(8,128)S(1)}, u32[]{:S(2)}, u32[]{:S(2)}) collective-permute-start(f32[8,384]{1,0:T(8,128)S(1)} %get-tuple-element.50.refs_7_.refs_0_), channel_id=1, source_target_pairs={{0,24},{2,26},{4,28},{6,30},{8,16},{10,18},{12,20},{14,22},{16,8},... | collective-permute-start | bytes 36872 | tf_op jit(solution)/shard_map/ppermute | solution.py:541
  16.7 5.0 %collective-permute-start.11 = (bf16[192,128]{1,0:T(8,128)(2,1)S(1)}, bf16[192,128]{1,0:T(8,128)(2,1)S(1)}, u32[]{:S(2)}, u32[]{:S(2)}) collective-permute-start(bf16[192,128]{1,0:T(8,128)(2,1)S(1)} %get-tuple-element.63), channel_id=1, source_target_pairs={{0,24},{2,26},{4,28},{6,30},{8,16},{10,18},{12,20},{14,22},{16,8},... | collective-permute-start | bytes 147464 | tf_op jit(solution)/shard_map/ppermute | solution.py:541
  16.9 4.8 %collective-permute-start.9 = (f32[8,384]{1,0:T(8,128)S(1)}, f32[8,384]{1,0:T(8,128)S(1)}, u32[]{:S(2)}, u32[]{:S(2)}) collective-permute-start(f32[8,384]{1,0:T(8,128)S(1)} %shard_map.91.note), channel_id=1, source_target_pairs={{0,8},{2,12},{4,10},{6,14},{8,0},{10,4},{12,2},{14,6},{16,24},{18,... | collective-permute-start | bytes 36872 | tf_op jit(solution)/shard_map/ppermute | solution.py:541
  17.9 3.8 %collective-permute-start.10 = (f32[8,384]{1,0:T(8,128)S(1)}, f32[8,384]{1,0:T(8,128)S(1)}, u32[]{:S(2)}, u32[]{:S(2)}) collective-permute-start(f32[8,384]{1,0:T(8,128)S(1)} %shard_map.91.note), channel_id=1, source_target_pairs={{0,10},{2,8},{4,14},{6,12},{8,2},{10,0},{12,6},{14,4},{16,26},{18,... | collective-permute-start | bytes 36872 | tf_op jit(solution)/shard_map/ppermute | solution.py:541
  22.4 1.5 %collective-permute-start.12 = (bf16[3,192,128]{2,1,0:T(8,128)(2,1)S(1)}, bf16[3,192,128]{2,1,0:T(8,128)(2,1)S(1)}, u32[]{:S(2)}, u32[]{:S(2)}) collective-permute-start(bf16[3,192,128]{2,1,0:T(8,128)(2,1)S(1)} %get-tuple-element.65), channel_id=1, source_target_pairs={{0,8},{8,0},{16,24},{24,16},{1,9},{9,1},{17,25},{25,17},{2,10},{10... | collective-permute-start | bytes 442376 | tf_op jit(solution)/shard_map/ppermute | solution.py:544

commit v4 on v3

--- a/solution.py
+++ b/solution.py
@@ -269,19 +269,16 @@
         notes[which][...] = jnp.concatenate([top, total] + far[which] + [jnp.zeros((4, two), f32)], axis=0)
 
 
-def middle_kernel(tok, heights, sides, scale, q_all, g_all, table, s_own, d_own, s_early, d_early, s_late, s_far, *refs):
+def middle_kernel(tok, sides, scale, q_all, g_all, table, s_own, d_own, s_early, d_early, s_late, s_far, *refs):
     qg = (q_all, g_all)
     tiles, foreign, sent = refs[:6], refs[6 : 6 + sides], refs[6 + sides : 6 + 2 * sides]
-    e_ref, ds_ref, e_far, ds_far, dq_ref, *refs = refs[6 + 2 * sides :]
-    shares, far_dq = refs[:sides], refs[sides:]
-    y, c, z = place()
+    e_ref, ds_ref, e_far, ds_far, dq_ref, *shares = refs[6 + 2 * sides :]
+    y, c, _ = place()
     near = border_is_own(y, c)
     bf16 = jnp.bfloat16
 
-    def add(ref, line, value):
-        ref[...] = value if line == 0 else ref[...] + value
-
-    def work(line):
+    total, far_total = 0.0, [0.0] * sides
+    for line in range(3):
         dq = 0.0
         for slot in range(2):
             i, at = 2 * line + slot, rows_at(line - 1 if line else slot, tok)
@@ -296,7 +293,7 @@
                 e_ref[rows_at(i, tok), :] = weights.astype(bf16)
                 ds_ref[rows_at(i, tok), :] = low
             dq = dq + dot(tiles[i][rows_at(0, tok), :], low, COLS_T)
-        add(dq_ref, line, dq)
+        total = total + dq
         for which in range(sides):
             far_g = foreign_rows(foreign[which], 1, which, tok)
             delta = foreign_delta(foreign[which], tok)
@@ -309,15 +306,11 @@
             if line == 0:
                 e_far[rows_at(which, tok), :] = weights.astype(bf16)
                 ds_far[rows_at(which, tok), :] = low
-            add(far_dq[which], line, dot(key, low, COLS_T))
-
-    for line in range(3):
-        if line == 0:
-            work(line)
-        else:
-            pl.when(line_place(z, line, heights)[0])(functools.partial(work, line))
+            far_total[which] = far_total[which] + dot(key, low, COLS_T)
+
+    dq_ref[...] = total
     for which in range(sides):
-        shares[which][...] = border_rows(which, tok, far_dq[which][...].T).astype(bf16)
+        shares[which][...] = border_rows(which, tok, far_total[which].T).astype(bf16)
 
 
 def border_rows(which, tok, block):
@@ -360,9 +353,8 @@
     note_ref[...] = jnp.concatenate(rows + [jnp.zeros((8 - len(rows), 2 * tok), jnp.float32)], axis=0)
 
 
-def line_query_kernel(tok, chips, heights, sides, scale, kv_ref, par_kv_ref, *refs):
-    queries, extras, outs = refs[:2], refs[2:4], refs[4:]
-    e_ref, ds_ref, e_far, ds_far, top_ref = outs
+def line_query_kernel(tok, chips, heights, sides, scale, line, kv_ref, par_kv_ref, message, extras, *outs):
+    e_ref, ds_ref, e_far, ds_far, top_ref = outs[-5:]
     y, c, z = place()
     near = border_is_own(y, c)
     two = 2 * tok
@@ -370,17 +362,17 @@
     f32, bf16 = jnp.float32, jnp.bfloat16
     tiles = (kv_ref, par_kv_ref)
 
-    def work(line):
+    def work():
         rising, _ = pair(z, 2 - line)
 
         def at(flags, dt):
             return jnp.where(rising, flags[3 * dt : 3 * dt + 1], flags[3 * dt + 2 : 3 * dt + 3])
 
-        rows = extras[line - 1][pl.ds(2 * tok, 32), :].astype(f32)
+        rows = extras[pl.ds(2 * tok, 32), :].astype(f32)
         own_flags, par_flags = (pick(near, which, rows[0:9], rows[9:18]) for which in range(2))
         delta = [sum(rows[18 + 3 * i + part : 19 + 3 * i + part] for i in range(3)) for part in range(two // width)]
         delta = jnp.concatenate(delta, axis=1)
-        line_q, line_g = (queries[line - 1][pl.ds(part * two, two), :] for part in range(2))
+        line_q, line_g = (message[pl.ds(part * two, two), :] for part in range(2))
         scores = []
         for slot in range(2):
             row = flag_row(tok, slot, at, own_flags, par_flags, False)
@@ -389,11 +381,11 @@
         for slot in range(2):
             weights = jnp.exp(scores[slot] - tops[0])
             grads = dot(tiles[slot][rows_at(1, tok), :], line_g, ROWS_T) - delta
-            kept = rows_at(2 * (line - 1) + slot, tok)
+            kept = rows_at(slot, tok)
             e_ref[kept, :] = weights.astype(bf16)
             ds_ref[kept, :] = (weights * grads * scale).astype(bf16)
         for which in range(sides):
-            ref = far_part(queries[line - 1], which, tok)
+            ref = far_part(message, which, tok)
             y_rising, y_at = pair(y, which)
             flags = ref[pl.ds(2 * tok, 16), :].astype(f32)
             row = far_row(tok, which, jnp.where(y_rising, at(flags, 0), at(flags, 2)))
@@ -405,14 +397,12 @@
             tops.append(to_lanes(which, tok, top, -1e30))
             weights = jnp.exp(block - top)
             grads = dot(value, far_g, ROWS_T) - foreign_delta(ref, tok)
-            kept = rows_at(2 * which + line - 1, tok)
+            kept = rows_at(which, tok)
             e_far[kept, :] = weights.astype(bf16)
             ds_far[kept, :] = (weights * grads * scale).astype(bf16)
-        gap = jnp.zeros((7 - sides, two), f32)
-        top_ref[pl.ds(8 * (line - 1), 8), :] = jnp.concatenate(tops + [gap], axis=0)
-
-    for line in (1, 2):
-        pl.when(line_place(z, line, heights)[0])(functools.partial(work, line))
+        top_ref[...] = jnp.concatenate(tops + [jnp.zeros((7 - sides, two), f32)], axis=0)
+
+    pl.when(line_place(z, line, heights)[0])(work)
 
 
 def times(block, factor):
@@ -453,33 +443,42 @@
             own_ref[i, rows_at(slot, tok), :] = sums[slot][i]
 
 
-def leave_kernel(tok, chips, heights, sides, own_ref, dq_ref, note, e_ref, ds_ref, e_far, ds_far, top_ref, *refs):
-    queries, notes, refs = refs[:2], refs[2:4], refs[4:]
+def line_sums(tok, heights, sides, line, sums, message, note, e_ref, ds_ref, e_far, ds_far, top_ref):
+    y, c, z = place()
+    near = border_is_own(y, c)
+
+    def work():
+        factor = jnp.exp(top_ref[0:1, :] - note[0:1, :])
+        scaled = [times(message[pl.ds(part * 2 * tok, 2 * tok), :], factor) for part in range(2)]
+        far = []
+        for which in range(sides):
+            lanes, at = foreign_lanes(which, tok, message.shape[1]), 1 + which
+            far_factor = jnp.exp(top_ref[at : at + 1, lanes] - note[at : at + 1, lanes])
+            rows = [foreign_rows(far_part(message, which, tok), part, which, tok) for part in range(2)]
+            far.append((e_far, ds_far, rows_at(which, tok), [times(block, far_factor) for block in rows]))
+        more = key_sums(tok, near, 0, e_ref, ds_ref, scaled, far)
+        for slot in range(2):
+            for i in range(2):
+                sums[i, rows_at(slot, tok), :] += more[slot][i]
+
+    pl.when(line_place(z, line, heights)[0])(work)
+
+
+def join_kernel(tok, heights, sides, line, own_ref, message, note, *refs):
+    *terms, sums = refs
+    sums[...] = own_ref[...]
+    line_sums(tok, heights, sides, line, sums, message, note, *terms)
+
+
+def leave_kernel(tok, chips, heights, sides, line, own_ref, dq_ref, note, message, note_in, *refs):
+    terms, refs = refs[:5], refs[5:]
     came, backs, (mine_ref, mine_q_ref, swap_ref, sums) = refs[:sides], refs[sides : 2 * sides], refs[2 * sides :]
-    y, c, z = place()
+    y, c, _ = place()
     near = border_is_own(y, c)
     f32, bf16 = jnp.float32, jnp.bfloat16
     width = dq_ref.shape[1]
     sums[...] = own_ref[...]
-
-    def work(line):
-        factor = jnp.exp(top_ref[8 * line - 8 : 8 * line - 7, :] - notes[line - 1][0:1, :])
-        scaled = [times(queries[line - 1][pl.ds(part * 2 * tok, 2 * tok), :], factor) for part in range(2)]
-        far = []
-        for which in range(sides):
-            lanes, at = foreign_lanes(which, tok, width), 8 * line - 7 + which
-            far_factor = jnp.exp(top_ref[at : at + 1, lanes] - notes[line - 1][1 + which : 2 + which, lanes])
-            rows = [foreign_rows(far_part(queries[line - 1], which, tok), part, which, tok) for part in range(2)]
-            far.append(
-                (e_far, ds_far, rows_at(2 * which + line - 1, tok), [times(block, far_factor) for block in rows])
-            )
-        more = key_sums(tok, near, line - 1, e_ref, ds_ref, scaled, far)
-        for slot in range(2):
-            for i in range(2):
-                sums[i, rows_at(slot, tok), :] += more[slot][i]
-
-    for line in (1, 2):
-        pl.when(line_place(z, line, heights)[0])(functools.partial(work, line))
+    line_sums(tok, heights, sides, line, sums, message, note_in, *terms)
     for i in range(2):
         mine_ref[i], swap_ref[i] = sums[i, rows_at(0, tok), :].astype(bf16), sums[i, rows_at(1, tok), :].astype(bf16)
     tiles = []
@@ -592,33 +591,38 @@
     came = [exchange(sent[which], which, None) for which in range(sides)]
     far_tile = ((sides * tok, 2 * width), bf16)
     e, ds, e_far, ds_far, raw_dq, *shares = call(
-        functools.partial(middle_kernel, tok, heights, sides, scale),
+        functools.partial(middle_kernel, tok, sides, scale),
         [square(2, bf16)] * 2 + [far_tile] * 2 + [raw_shape] + [((tok, width), bf16)] * sides,
         [VMEM] * (15 + 2 * sides),
-        [pltpu.VMEM((width, 2 * width), f32)] * sides,
         cost=20,
     )(*qg, table, s_own, d_own, s_early, d_early, s_late, s_far, *tiles, *foreign, *sent)
     (note,) = call(functools.partial(total_kernel, tok, chips, sides), [note_shape], [VMEM] * (2 * sides))(*sent, *came)
     notes = [exchange(note, None, which) for which in (1, 0)]
     shares = [exchange(share, which, None) for which, share in enumerate(shares)]
-    far_pair = ((2 * sides * tok, 2 * width), bf16)
-    line_terms = call(
-        functools.partial(line_query_kernel, tok, chips, heights, sides, scale),
-        [square(4, bf16)] * 2 + [far_pair] * 2 + [((16, two), f32)],
-        [VMEM] * 6,
-        cost=20,
-    )(kv, par_kv, *queries_in, *late)
+    sums_shape = ((2, two, width), f32)
+
+    def line_terms(line, *earlier):
+        return call(
+            functools.partial(line_query_kernel, tok, chips, heights, sides, scale, line),
+            [square(2, bf16)] * 2 + [far_tile] * 2 + [note_shape],
+            [VMEM] * (4 + len(earlier)),
+            cost=20,
+        )(kv, par_kv, queries_in[line - 1], late[line - 1], *earlier)
+
     own, dq = call(
         functools.partial(stay_kernel, tok, chips, sides),
-        [((2, two, width), f32), ((two, width), f32)],
+        [sums_shape, ((two, width), f32)],
         [VMEM] * (8 + 2 * sides),
     )(*qg, e, ds, e_far, ds_far, raw_dq, note, *sent, *foreign)
+    (joined,) = call(
+        functools.partial(join_kernel, tok, heights, sides, 2), [sums_shape], [VMEM] * 8
+    )(own, queries_in[1], notes[1], *line_terms(2))
     mine, mine_q, leaving = call(
-        functools.partial(leave_kernel, tok, chips, heights, sides),
+        functools.partial(leave_kernel, tok, chips, heights, sides, 1),
         [tile_shape, ((tok, width), bf16), ((3, tok, width), bf16)],
-        [VMEM] * (12 + 2 * sides),
-        [pltpu.VMEM((2, two, width), f32)],
-    )(own, dq, note, *line_terms, *queries_in, *notes, *came, *shares)
+        [VMEM] * (10 + 2 * sides),
+        [pltpu.VMEM(*sums_shape)],
+    )(joined, dq, note, queries_in[0], notes[0], *line_terms(1, joined), *came, *shares)
     return call(final_kernel, [(queries.shape, bf16)] * 3, [VMEM] * 3)(mine, swap_cores(leaving), mine_q)
 
 

time: 24.8 us -> 24 us (0.968)
  waiting for transfers between devices: 3.3 us -> 2.69 us
    ppermute x11, starting transfers between devices: 13.2 us -> 12.6 us  [exchange(): return lax.ppermute(block, ('tm', 'height'), pairs)]
    ppermute x11, waiting for transfers between devices: 2.29 us -> 1.68 us  [exchange(): return lax.ppermute(block, ('tm', 'height'), pairs)]
    ppermute x2, starting transfers between devices: 0.96 us -> 1.38 us  [swap_cores(): return lax.ppermute(block, 'tm', [(t, t ^ 1) for t in range(times)])]
    pallas_call x4 -> x6, Pallas kernels: 2.81 us -> 2.89 us  [the longest x1 1.23 us: body(): call(functools.partial(middle_kernel, tok, sides, scale), [square(2, bf16...]
  transfers between devices with their start and end apart: 13 -> 13, of which waited for: 4 -> 5; matrix products, arithmetic and copies ran while one was open for 0% -> 0% of each run, Pallas kernels for 15% -> 18%
where the time goes in v4:
time: 24 us; the launch traced here: 23.8 us
  starting transfers between devices  14 us (58%)
  Pallas kernels  6.38 us (27%)
  waiting for transfers between devices  2.69 us (11%)
  between operations  0.76 us (3%)
    ppermute x11, starting transfers between devices, exchange(): return lax.ppermute(block, ('tm', 'height'), pairs)  12.6 us
    ppermute x11, waiting for transfers between devices, exchange(): return lax.ppermute(block, ('tm', 'height'), pairs)  1.68 us
    ppermute x2, starting transfers between devices, swap_cores(): return lax.ppermute(block, 'tm', [(t, t ^ 1) for t in range(times)])  1.38 us
    pallas_call x1, Pallas kernels, body(): call(functools.partial(middle_kernel, tok, sides, scale), [square(2, bf16...  1.23 us
    pallas_call x1, Pallas kernels, body(): call(functools.partial(pack_kernel, tok), [((2 * tok + extra, width), bf1...  1.13 us
    ppermute x2, waiting for transfers between devices, swap_cores(): return lax.ppermute(block, 'tm', [(t, t ^ 1) for t in range(times)])  1.01 us
    pallas_call x1, Pallas kernels, body(): call(final_kernel, [(queries.shape, bf16)] * 3, [VMEM] * 3)  0.74 us
    pallas_call x1, Pallas kernels, body(): call(functools.partial(score_kernel, tok, chips, heights, sides, scale),...  0.53 us
  transfers between devices with their start and end apart: 13, of which 5 were waited for; matrix products, arithmetic and copies ran while one was open for 0% of the time, Pallas kernels for 18%

profile of v4, /device:TPU:0, one launch (start us, length us, event | category | flops | bytes accessed | tf_op | source)
XLA Modules:
  0.0 23.8 jit_solution(7179757993249067769)
XLA Ops:
  0.6 1.1 %shard_map.85 = (bf16[448,128]{1,0:T(8,128)(2,1)S(1)}, bf16[592,128]{1,0:T(8,128)(2,1)S(1)}, bf16[976,128]{1,0:T(8,128)(2,1)S(1)}) custom-call(bf16[1,1,2,1,192,128]{5,4,3,2,1,0:T(8,128)(2,1)} %k_ref.1, bf16[1,1,2,1,192,128]{5,4,3,2,1,0:T(8,128)(2,1)} %v_ref.1, bf16[1,1,2,1,192,128]{5,4,3,2,1,0:T(8,128)(2,1)} %q_ref.1, ...), custom_call_target="tpu_custom_call" | custom-call | tf_op jit(solution)/shard_map/pallas_call | solution.py:548
  1.8 0.5 %collective-permute-start = (bf16[976,128]{1,0:T(8,128)(2,1)S(1)}, bf16[976,128]{1,0:T(8,128)(2,1)S(1)}, u32[]{:S(2)}, u32[]{:S(2)}) collective-permute-start(bf16[976,128]{1,0:T(8,128)(2,1)S(1)} %get-tuple-element.42), channel_id=1, source_target_pairs={{0,8},{8,0},{16,24},{24,16},{1,9},{9,1},{17,25},{25,17},{2,10},{10... | collective-permute-start | bytes 749576 | tf_op jit(solution)/shard_map/ppermute | solution.py:543
  2.4 3.9 %collective-permute-start.2 = (bf16[448,128]{1,0:T(8,128)(2,1)S(1)}, bf16[448,128]{1,0:T(8,128)(2,1)S(1)}, u32[]{:S(2)}, u32[]{:S(2)}) collective-permute-start(bf16[448,128]{1,0:T(8,128)(2,1)S(1)} %get-tuple-element.40.kv_ref.refs_1_.refs_0_), channel_id=1, source_target_pairs={{0,10},{2,8},{4,14},{6,12},{8,2},{10,0},{12,6},{14,4},{16,26},{18,... | collective-permute-start | bytes 344072 | tf_op jit(solution)/shard_map/ppermute | solution.py:540
  6.2 0.2 shard_map.86
  6.4 1.6 %collective-permute-start.3 = (bf16[432,128]{1,0:T(8,128)(2,1)S(1)}, bf16[432,128]{1,0:T(8,128)(2,1)S(1)}, u32[]{:S(2)}, u32[]{:S(2)}) collective-permute-start(bf16[432,128]{1,0:T(8,128)(2,1)S(1)} %get-tuple-element.52), channel_id=1, source_target_pairs={{0,24},{2,26},{4,28},{6,30},{8,16},{10,18},{12,20},{14,22},{16,8},... | collective-permute-start | bytes 331784 | tf_op jit(solution)/shard_map/ppermute | solution.py:540
  8.1 1.6 %collective-permute-start.5 = (bf16[416,128]{1,0:T(8,128)(2,1)S(1)}, bf16[416,128]{1,0:T(8,128)(2,1)S(1)}, u32[]{:S(2)}, u32[]{:S(2)}) collective-permute-start(bf16[416,128]{1,0:T(8,128)(2,1)S(1)} %get-tuple-element.43.par_kv_ref.refs_2_.refs_1_), channel_id=1, source_target_pairs={{0,10},{2,8},{4,14},{6,12},{8,2},{10,0},{12,6},{14,4},{16,26},{18,... | collective-permute-start | bytes 319496 | tf_op jit(solution)/shard_map/ppermute | solution.py:540
  9.7 0.4 %shard_map.87 = (bf16[384,128]{1,0:T(8,128)(2,1)S(1)}, bf16[384,128]{1,0:T(8,128)(2,1)S(1)}, f32[8,384]{1,0:T(8,128)S(1)}, f32[384,384]{1,0:T(8,128)S(1)}, f32[384,384]{1,0:T(8,128)S(1)}) custom-call(bf16[448,128]{1,0:T(8,128)(2,1)S(1)} %get-tuple-element.40.kv_ref.refs_1_.refs_0_, bf16[416,128]{1,0:T(8,128)(2,1)S(1)} %get-tuple-element.43.par_kv_ref.refs_2_.refs_1_, ...), custom_call_target="tpu_custom_call" | custom-call | tf_op jit(solution)/shard_map/pallas_call | solution.py:571
  10.1 0.5 %shard_map.88 = (f32[384,384]{1,0:T(8,128)S(1)}, f32[384,384]{1,0:T(8,128)S(1)}, f32[8,384]{1,0:T(8,128)S(1)}) custom-call(bf16[384,128]{1,0:T(8,128)(2,1)S(1)} %get-tuple-element.44.q_all, bf16[384,128]{1,0:T(8,128)(2,1)S(1)} %get-tuple-element.45.g_all, f32[8,384]{1,0:T(8,128)S(1)} %get-tuple-element.46.table, f32[384,384]{1,0:T(8,128)S(1)} %get-tuple-element.47.s_own, ...), custom_call_target="tpu_custom_call" | custom-call | tf_op jit(solution)/shard_map/pallas_call | solution.py:583
  10.6 0.6 %collective-permute-done.3.refs_0_.refs_6_.refs_1_ = bf16[432,128]{1,0:T(8,128)(2,1)S(1)} collective-permute-done((bf16[432,128]{1,0:T(8,128)(2,1)S(1)}, bf16[432,128]{1,0:T(8,128)(2,1)S(1)}, u32[]{:S(2)}, u32[]{:S(2)}) %collective-permute-start.3) | collective-permute-done | bytes 110624 | tf_op jit(solution)/shard_map/ppermute | solution.py:540
  11.3 1.0 %collective-permute-start.7 = (bf16[1168,128]{1,0:T(8,128)(2,1)S(1)}, bf16[1168,128]{1,0:T(8,128)(2,1)S(1)}, u32[]{:S(2)}, u32[]{:S(2)}) collective-permute-start(bf16[1168,128]{1,0:T(8,128)(2,1)S(1)} %shard_map.93), channel_id=1, source_target_pairs={{0,10},{2,8},{4,14},{6,12},{8,2},{10,0},{12,6},{14,4},{16,26},{18,... | collective-permute-start | bytes 897032 | tf_op jit(solution)/shard_map/ppermute | solution.py:540
  12.3 0.2 collective-permute-start.9
  12.5 0.3 %collective-permute-done.5.refs_5_.refs_4_.extras = bf16[416,128]{1,0:T(8,128)(2,1)S(1)} collective-permute-done((bf16[416,128]{1,0:T(8,128)(2,1)S(1)}, bf16[416,128]{1,0:T(8,128)(2,1)S(1)}, u32[]{:S(2)}, u32[]{:S(2)}) %collective-permute-start.5) | collective-permute-done | bytes 106528 | tf_op jit(solution)/shard_map/ppermute | solution.py:540
  12.8 0.5 %shard_map.89 = (f32[384,384]{1,0:T(8,128)S(1)}, f32[576,256]{1,0:T(8,128)S(1)}, f32[8,384]{1,0:T(8,128)S(1)}) custom-call(bf16[384,128]{1,0:T(8,128)(2,1)S(1)} %get-tuple-element.44.q_all, bf16[384,128]{1,0:T(8,128)(2,1)S(1)} %get-tuple-element.45.g_all, f32[8,384]{1,0:T(8,128)S(1)} %get-tuple-element.46.table, f32[8,384]{1,0:T(8,128)S(1)} %get-tuple-element.51.part, ...), custom_call_target="tpu_custom_call" | custom-call | tf_op jit(solution)/shard_map/pallas_call | solution.py:586
  13.4 1.5 %collective-permute-start.6 = (f32[8,384]{1,0:T(8,128)S(1)}, f32[8,384]{1,0:T(8,128)S(1)}, u32[]{:S(2)}, u32[]{:S(2)}) collective-permute-start(f32[8,384]{1,0:T(8,128)S(1)} %get-tuple-element.55.refs_7_.refs_0_), channel_id=1, source_target_pairs={{0,24},{2,26},{4,28},{6,30},{8,16},{10,18},{12,20},{14,22},{16,8},... | collective-permute-start | bytes 36872 | tf_op jit(solution)/shard_map/ppermute | solution.py:540
  14.8 1.2 %shard_map.90 = (bf16[384,384]{1,0:T(8,128)(2,1)S(1)}, bf16[384,384]{1,0:T(8,128)(2,1)S(1)}, bf16[192,256]{1,0:T(8,128)(2,1)S(1)}, bf16[192,256]{1,0:T(8,128)(2,...) custom-call(bf16[384,128]{1,0:T(8,128)(2,1)S(1)} %get-tuple-element.44.q_all, ...), custom_call_target="tpu_custom_call" | custom-call | flops 20000000000 | tf_op jit(solution)/shard_map/pallas_call | solution.py:593
  16.0 0.5 %collective-permute-start.11 = (bf16[192,128]{1,0:T(8,128)(2,1)S(1)}, bf16[192,128]{1,0:T(8,128)(2,1)S(1)}, u32[]{:S(2)}, u32[]{:S(2)}) collective-permute-start(bf16[192,128]{1,0:T(8,128)(2,1)S(1)} %get-tuple-element.73), channel_id=1, source_target_pairs={{0,24},{2,26},{4,28},{6,30},{8,16},{10,18},{12,20},{14,22},{16,8},... | collective-permute-start | bytes 147464 | tf_op jit(solution)/shard_map/ppermute | solution.py:540
  16.6 2.2 %collective-permute-start.8 = (f32[8,384]{1,0:T(8,128)S(1)}, f32[8,384]{1,0:T(8,128)S(1)}, u32[]{:S(2)}, u32[]{:S(2)}) collective-permute-start(f32[8,384]{1,0:T(8,128)S(1)} %shard_map.91.note), channel_id=1, source_target_pairs={{0,10},{2,8},{4,14},{6,12},{8,2},{10,0},{12,6},{14,4},{16,26},{18,... | collective-permute-start | bytes 36872 | tf_op jit(solution)/shard_map/ppermute | solution.py:540
  18.8 0.5 %shard_map.92 = (f32[2,384,128]{2,1,0:T(8,128)S(1)}, f32[384,128]{1,0:T(8,128)S(1)}) custom-call(bf16[384,128]{1,0:T(8,128)(2,1)S(1)} %get-tuple-element.44.q_all, bf16[384,128]{1,0:T(8,128)(2,1)S(1)} %get-tuple-element.45.g_all, bf16[384,384]{1,0:T(8,128)(2,1)S(1)} %get-tuple-element.56.e_ref, bf16[384,384]{1,0:T(8,128)(2,1)S(1)} %get-tuple-element.57.ds_ref, ...), custom_call_target="tpu_custom_call" | custom-call | tf_op jit(solution)/shard_map/pallas_call | solution.py:612
  19.3 0.6 %collective-permute-done.7.message = bf16[1168,128]{1,0:T(8,128)(2,1)S(1)} collective-permute-done((bf16[1168,128]{1,0:T(8,128)(2,1)S(1)}, bf16[1168,128]{1,0:T(8,128)(2,1)S(1)}, u32[]{:S(2)}, u32[]{:S(2)}) %collective-permute-start.7) | collective-permute-done | bytes 299040 | tf_op jit(solution)/shard_map/ppermute | solution.py:540
  19.9 0.5 %shard_map.94 = (bf16[384,384]{1,0:T(8,128)(2,1)S(1)}, bf16[384,384]{1,0:T(8,128)(2,1)S(1)}, bf16[192,256]{1,0:T(8,128)(2,1)S(1)}, bf16[192,256]{1,0:T(8,128)(2,1)S(1)}, f32[8,384]{1,0:T(8,128)S(1)}) custom-call(bf16[448,128]{1,0:T(8,128)(2,1)S(1)} %get-tuple-element.40.kv_ref.refs_1_.refs_0_, ...), custom_call_target="tpu_custom_call" | custom-call | flops 20000000000 | tf_op jit(solution)/shard_map/pallas_call | solution.py:605
  20.4 0.5 %shard_map.95.outs_0_.own_ref = f32[2,384,128]{2,1,0:T(8,128)S(1)} custom-call(f32[2,384,128]{2,1,0:T(8,128)S(1)} %get-tuple-element.61.own_ref, bf16[1168,128]{1,0:T(8,128)(2,1)S(1)} %collective-permute-done.7.message, f32[8,384]{1,0:T(8,128)S(1)} %collective-permute-done.8.note, bf16[384,384]{1,0:T(8,128)(2,1)S(1)} %get-tuple-element.62.refs_0_, ...), custom_call_target="tpu_custom_call" | custom-call | tf_op jit(solution)/shard_map/pallas_call | solution.py:617
  21.2 0.9 %collective-permute-start.12 = (bf16[3,192,128]{2,1,0:T(8,128)(2,1)S(1)}, bf16[3,192,128]{2,1,0:T(8,128)(2,1)S(1)}, u32[]{:S(2)}, u32[]{:S(2)}) collective-permute-start(bf16[3,192,128]{2,1,0:T(8,128)(2,1)S(1)} %get-tuple-element.75), channel_id=1, source_target_pairs={{0,8},{8,0},{16,24},{24,16},{1,9},{9,1},{17,25},{25,17},{2,10},{10... | collective-permute-start | bytes 442376 | tf_op jit(solution)/shard_map/ppermute | solution.py:543
  22.0 1.0 %collective-permute-done.12.swap_ref = bf16[3,192,128]{2,1,0:T(8,128)(2,1)S(1)} collective-permute-done((bf16[3,192,128]{2,1,0:T(8,128)(2,1)S(1)}, bf16[3,192,128]{2,1,0:T(8,128)(2,1)S(1)}, u32[]{:S(2)}, u32[]{:S(2)}) %collective-permute-start.12) | collective-permute-done | bytes 147488 | tf_op jit(solution)/shard_map/ppermute | solution.py:543
  23.0 0.7 %shard_map.98 = (bf16[1,1,2,1,192,128]{5,4,3,2,1,0:T(8,128)(2,1)}, bf16[1,1,2,1,192,128]{5,4,3,2,1,0:T(8,128)(2,1)}, bf16[1,1,2,1,192,128]{5,4,3,2,1,0:T(8,128)(2,1)}) custom-call(bf16[2,192,128]{2,1,0:T(8,128)(2,1)S(1)} %get-tuple-element.74.mine_ref, bf16[3,192,128]{2,1,0:T(8,128)(2,1)S(1)} %collective-permute-done.12.swap_ref, ...), custom_call_target="tpu_custom_call" | custom-call | tf_op jit(solution)/shard_map/pallas_call | solution.py:626
  (16 shorter events, 0.5 us)
Async XLA Ops:
  1.8 4.5 %collective-permute-start = (bf16[976,128]{1,0:T(8,128)(2,1)S(1)}, bf16[976,128]{1,0:T(8,128)(2,1)S(1)}, u32[]{:S(2)}, u32[]{:S(2)}) collective-permute-start(bf16[976,128]{1,0:T(8,128)(2,1)S(1)} %get-tuple-element.42), channel_id=1, source_target_pairs={{0,8},{8,0},{16,24},{24,16},{1,9},{9,1},{17,25},{25,17},{2,10},{10... | collective-permute-start | bytes 749576 | tf_op jit(solution)/shard_map/ppermute | solution.py:543
  2.3 7.8 %collective-permute-start.1 = (bf16[448,128]{1,0:T(8,128)(2,1)S(1)}, bf16[448,128]{1,0:T(8,128)(2,1)S(1)}, u32[]{:S(2)}, u32[]{:S(2)}) collective-permute-start(bf16[448,128]{1,0:T(8,128)(2,1)S(1)} %get-tuple-element.40.kv_ref.refs_1_.refs_0_), channel_id=1, source_target_pairs={{0,8},{2,12},{4,10},{6,14},{8,0},{10,4},{12,2},{14,6},{16,24},{18,... | collective-permute-start | bytes 344072 | tf_op jit(solution)/shard_map/ppermute | solution.py:540
  2.4 7.8 %collective-permute-start.2 = (bf16[448,128]{1,0:T(8,128)(2,1)S(1)}, bf16[448,128]{1,0:T(8,128)(2,1)S(1)}, u32[]{:S(2)}, u32[]{:S(2)}) collective-permute-start(bf16[448,128]{1,0:T(8,128)(2,1)S(1)} %get-tuple-element.40.kv_ref.refs_1_.refs_0_), channel_id=1, source_target_pairs={{0,10},{2,8},{4,14},{6,12},{8,2},{10,0},{12,6},{14,4},{16,26},{18,... | collective-permute-start | bytes 344072 | tf_op jit(solution)/shard_map/ppermute | solution.py:540
  6.4 4.9 %collective-permute-start.3 = (bf16[432,128]{1,0:T(8,128)(2,1)S(1)}, bf16[432,128]{1,0:T(8,128)(2,1)S(1)}, u32[]{:S(2)}, u32[]{:S(2)}) collective-permute-start(bf16[432,128]{1,0:T(8,128)(2,1)S(1)} %get-tuple-element.52), channel_id=1, source_target_pairs={{0,24},{2,26},{4,28},{6,30},{8,16},{10,18},{12,20},{14,22},{16,8},... | collective-permute-start | bytes 331784 | tf_op jit(solution)/shard_map/ppermute | solution.py:540
  8.1 4.4 %collective-permute-start.4 = (bf16[416,128]{1,0:T(8,128)(2,1)S(1)}, bf16[416,128]{1,0:T(8,128)(2,1)S(1)}, u32[]{:S(2)}, u32[]{:S(2)}) collective-permute-start(bf16[416,128]{1,0:T(8,128)(2,1)S(1)} %get-tuple-element.43.par_kv_ref.refs_2_.refs_1_), channel_id=1, source_target_pairs={{0,8},{2,12},{4,10},{6,14},{8,0},{10,4},{12,2},{14,6},{16,24},{18,... | collective-permute-start | bytes 319496 | tf_op jit(solution)/shard_map/ppermute | solution.py:540
  8.1 4.7 %collective-permute-start.5 = (bf16[416,128]{1,0:T(8,128)(2,1)S(1)}, bf16[416,128]{1,0:T(8,128)(2,1)S(1)}, u32[]{:S(2)}, u32[]{:S(2)}) collective-permute-start(bf16[416,128]{1,0:T(8,128)(2,1)S(1)} %get-tuple-element.43.par_kv_ref.refs_2_.refs_1_), channel_id=1, source_target_pairs={{0,10},{2,8},{4,14},{6,12},{8,2},{10,0},{12,6},{14,4},{16,26},{18,... | collective-permute-start | bytes 319496 | tf_op jit(solution)/shard_map/ppermute | solution.py:540
  11.3 8.6 %collective-permute-start.7 = (bf16[1168,128]{1,0:T(8,128)(2,1)S(1)}, bf16[1168,128]{1,0:T(8,128)(2,1)S(1)}, u32[]{:S(2)}, u32[]{:S(2)}) collective-permute-start(bf16[1168,128]{1,0:T(8,128)(2,1)S(1)} %shard_map.93), channel_id=1, source_target_pairs={{0,10},{2,8},{4,14},{6,12},{8,2},{10,0},{12,6},{14,4},{16,26},{18,... | collective-permute-start | bytes 897032 | tf_op jit(solution)/shard_map/ppermute | solution.py:540
  12.3 8.6 %collective-permute-start.9 = (bf16[1168,128]{1,0:T(8,128)(2,1)S(1)}, bf16[1168,128]{1,0:T(8,128)(2,1)S(1)}, u32[]{:S(2)}, u32[]{:S(2)}) collective-permute-start(bf16[1168,128]{1,0:T(8,128)(2,1)S(1)} %shard_map.93), channel_id=1, source_target_pairs={{0,8},{2,12},{4,10},{6,14},{8,0},{10,4},{12,2},{14,6},{16,24},{18,... | collective-permute-start | bytes 897032 | tf_op jit(solution)/shard_map/ppermute | solution.py:540
  13.4 3.2 %collective-permute-start.6 = (f32[8,384]{1,0:T(8,128)S(1)}, f32[8,384]{1,0:T(8,128)S(1)}, u32[]{:S(2)}, u32[]{:S(2)}) collective-permute-start(f32[8,384]{1,0:T(8,128)S(1)} %get-tuple-element.55.refs_7_.refs_0_), channel_id=1, source_target_pairs={{0,24},{2,26},{4,28},{6,30},{8,16},{10,18},{12,20},{14,22},{16,8},... | collective-permute-start | bytes 36872 | tf_op jit(solution)/shard_map/ppermute | solution.py:540
  16.0 5.0 %collective-permute-start.11 = (bf16[192,128]{1,0:T(8,128)(2,1)S(1)}, bf16[192,128]{1,0:T(8,128)(2,1)S(1)}, u32[]{:S(2)}, u32[]{:S(2)}) collective-permute-start(bf16[192,128]{1,0:T(8,128)(2,1)S(1)} %get-tuple-element.73), channel_id=1, source_target_pairs={{0,24},{2,26},{4,28},{6,30},{8,16},{10,18},{12,20},{14,22},{16,8},... | collective-permute-start | bytes 147464 | tf_op jit(solution)/shard_map/ppermute | solution.py:540
  16.6 3.8 %collective-permute-start.8 = (f32[8,384]{1,0:T(8,128)S(1)}, f32[8,384]{1,0:T(8,128)S(1)}, u32[]{:S(2)}, u32[]{:S(2)}) collective-permute-start(f32[8,384]{1,0:T(8,128)S(1)} %shard_map.91.note), channel_id=1, source_target_pairs={{0,10},{2,8},{4,14},{6,12},{8,2},{10,0},{12,6},{14,4},{16,26},{18,... | collective-permute-start | bytes 36872 | tf_op jit(solution)/shard_map/ppermute | solution.py:540
  18.8 2.2 %collective-permute-start.10 = (f32[8,384]{1,0:T(8,128)S(1)}, f32[8,384]{1,0:T(8,128)S(1)}, u32[]{:S(2)}, u32[]{:S(2)}) collective-permute-start(f32[8,384]{1,0:T(8,128)S(1)} %shard_map.91.note), channel_id=1, source_target_pairs={{0,8},{2,12},{4,10},{6,14},{8,0},{10,4},{12,2},{14,6},{16,24},{18,... | collective-permute-start | bytes 36872 | tf_op jit(solution)/shard_map/ppermute | solution.py:540
  21.2 1.9 %collective-permute-start.12 = (bf16[3,192,128]{2,1,0:T(8,128)(2,1)S(1)}, bf16[3,192,128]{2,1,0:T(8,128)(2,1)S(1)}, u32[]{:S(2)}, u32[]{:S(2)}) collective-permute-start(bf16[3,192,128]{2,1,0:T(8,128)(2,1)S(1)} %get-tuple-element.75), channel_id=1, source_target_pairs={{0,8},{8,0},{16,24},{24,16},{1,9},{9,1},{17,25},{25,17},{2,10},{10... | collective-permute-start | bytes 442376 | tf_op jit(solution)/shard_map/ppermute | solution.py:543

commit v5 on v4

--- a/solution.py
+++ b/solution.py
@@ -495,13 +495,18 @@
     swap_ref[2] = jnp.where(near, tiles[1], tiles[0])
 
 
-def final_kernel(mine_ref, swap_ref, mine_q_ref, gq_ref, gk_ref, gv_ref):
+def final_kernel(mine_ref, swap_ref, mine_q_ref, gq_ref, gk_ref, gv_ref, sems):
     head = head_at()
-    gq_ref[0, 0, head, 0] = mine_q_ref[...]
-    gq_ref[0, 0, 1 - head, 0] = swap_ref[2]
+    blocks = [(mine_q_ref, head, gq_ref), (swap_ref.at[2], 1 - head, gq_ref)]
     for i, ref in enumerate((gk_ref, gv_ref)):
-        ref[0, 0, head, 0] = mine_ref[i]
-        ref[0, 0, 1 - head, 0] = swap_ref[i]
+        blocks += [(mine_ref.at[i], head, ref), (swap_ref.at[i], 1 - head, ref)]
+    copies = [
+        pltpu.make_async_copy(block, ref.at[0, 0, at, 0], sems.at[i]) for i, (block, at, ref) in enumerate(blocks)
+    ]
+    for copy in copies:
+        copy.start()
+    for copy in copies:
+        copy.wait()
 
 
 def body(queries, keys, values, grad_out, attn_out, window_mask):
@@ -623,7 +628,14 @@
         [VMEM] * (10 + 2 * sides),
         [pltpu.VMEM(*sums_shape)],
     )(joined, dq, note, queries_in[0], notes[0], *line_terms(1, joined), *came, *shares)
-    return call(final_kernel, [(queries.shape, bf16)] * 3, [VMEM] * 3)(mine, swap_cores(leaving), mine_q)
+    return pl.pallas_call(
+        final_kernel,
+        out_shape=[jax.ShapeDtypeStruct(queries.shape, bf16)] * 3,
+        in_specs=[VMEM] * 3,
+        out_specs=[HBM] * 3,
+        scratch_shapes=[pltpu.SemaphoreType.DMA((6,))],
+        compiler_params=LIMIT,
+    )(mine, swap_cores(leaving), mine_q)
 
 
 def solution(mesh):

time: 24 us -> 24 us (level)
  no operation moved by 1% of the time
where the time goes in v5:
time: 24 us; the launch traced here: 23.8 us
  starting transfers between devices  14 us (58%)
  Pallas kernels  6.39 us (27%)
  waiting for transfers between devices  2.69 us (11%)
  between operations  0.76 us (3%)
    ppermute x11, starting transfers between devices, exchange(): return lax.ppermute(block, ('tm', 'height'), pairs)  12.6 us
    ppermute x11, waiting for transfers between devices, exchange(): return lax.ppermute(block, ('tm', 'height'), pairs)  1.68 us
    ppermute x2, starting transfers between devices, swap_cores(): return lax.ppermute(block, 'tm', [(t, t ^ 1) for t in range(times)])  1.38 us
    pallas_call x1, Pallas kernels, body(): call(functools.partial(middle_kernel, tok, sides, scale), [square(2, bf16...  1.23 us
    pallas_call x1, Pallas kernels, body(): call(functools.partial(pack_kernel, tok), [((2 * tok + extra, width), bf1...  1.13 us
    ppermute x2, waiting for transfers between devices, swap_cores(): return lax.ppermute(block, 'tm', [(t, t ^ 1) for t in range(times)])  1.01 us
    pallas_call x1, Pallas kernels, body(): pl.pallas_call(final_kernel, out_shape=[jax.ShapeDtypeStruct(queries.shap...  0.75 us
    pallas_call x1, Pallas kernels, body(): call(functools.partial(score_kernel, tok, chips, heights, sides, scale),...  0.53 us
  transfers between devices with their start and end apart: 13, of which 5 were waited for; matrix products, arithmetic and copies ran while one was open for 0% of the time, Pallas kernels for 18%

profile of v5, /device:TPU:0, one launch (start us, length us, event | category | flops | bytes accessed | tf_op | source)
XLA Modules:
  0.0 23.8 jit_solution(16034854558161649450)
XLA Ops:
  0.6 1.1 %shard_map.85 = (bf16[448,128]{1,0:T(8,128)(2,1)S(1)}, bf16[592,128]{1,0:T(8,128)(2,1)S(1)}, bf16[976,128]{1,0:T(8,128)(2,1)S(1)}) custom-call(bf16[1,1,2,1,192,128]{5,4,3,2,1,0:T(8,128)(2,1)} %k_ref.1, bf16[1,1,2,1,192,128]{5,4,3,2,1,0:T(8,128)(2,1)} %v_ref.1, bf16[1,1,2,1,192,128]{5,4,3,2,1,0:T(8,128)(2,1)} %q_ref.1, ...), custom_call_target="tpu_custom_call" | custom-call | tf_op jit(solution)/shard_map/pallas_call | solution.py:553
  1.8 0.5 %collective-permute-start = (bf16[976,128]{1,0:T(8,128)(2,1)S(1)}, bf16[976,128]{1,0:T(8,128)(2,1)S(1)}, u32[]{:S(2)}, u32[]{:S(2)}) collective-permute-start(bf16[976,128]{1,0:T(8,128)(2,1)S(1)} %get-tuple-element.42), channel_id=1, source_target_pairs={{0,8},{8,0},{16,24},{24,16},{1,9},{9,1},{17,25},{25,17},{2,10},{10... | collective-permute-start | bytes 749576 | tf_op jit(solution)/shard_map/ppermute | solution.py:548
  2.4 3.9 %collective-permute-start.2 = (bf16[448,128]{1,0:T(8,128)(2,1)S(1)}, bf16[448,128]{1,0:T(8,128)(2,1)S(1)}, u32[]{:S(2)}, u32[]{:S(2)}) collective-permute-start(bf16[448,128]{1,0:T(8,128)(2,1)S(1)} %get-tuple-element.40.kv_ref.refs_1_.refs_0_), channel_id=1, source_target_pairs={{0,10},{2,8},{4,14},{6,12},{8,2},{10,0},{12,6},{14,4},{16,26},{18,... | collective-permute-start | bytes 344072 | tf_op jit(solution)/shard_map/ppermute | solution.py:545
  6.2 0.2 shard_map.86
  6.4 1.6 %collective-permute-start.3 = (bf16[432,128]{1,0:T(8,128)(2,1)S(1)}, bf16[432,128]{1,0:T(8,128)(2,1)S(1)}, u32[]{:S(2)}, u32[]{:S(2)}) collective-permute-start(bf16[432,128]{1,0:T(8,128)(2,1)S(1)} %get-tuple-element.52), channel_id=1, source_target_pairs={{0,24},{2,26},{4,28},{6,30},{8,16},{10,18},{12,20},{14,22},{16,8},... | collective-permute-start | bytes 331784 | tf_op jit(solution)/shard_map/ppermute | solution.py:545
  8.1 1.6 %collective-permute-start.5 = (bf16[416,128]{1,0:T(8,128)(2,1)S(1)}, bf16[416,128]{1,0:T(8,128)(2,1)S(1)}, u32[]{:S(2)}, u32[]{:S(2)}) collective-permute-start(bf16[416,128]{1,0:T(8,128)(2,1)S(1)} %get-tuple-element.43.par_kv_ref.refs_2_.refs_1_), channel_id=1, source_target_pairs={{0,10},{2,8},{4,14},{6,12},{8,2},{10,0},{12,6},{14,4},{16,26},{18,... | collective-permute-start | bytes 319496 | tf_op jit(solution)/shard_map/ppermute | solution.py:545
  9.7 0.4 %shard_map.87 = (bf16[384,128]{1,0:T(8,128)(2,1)S(1)}, bf16[384,128]{1,0:T(8,128)(2,1)S(1)}, f32[8,384]{1,0:T(8,128)S(1)}, f32[384,384]{1,0:T(8,128)S(1)}, f32[384,384]{1,0:T(8,128)S(1)}) custom-call(bf16[448,128]{1,0:T(8,128)(2,1)S(1)} %get-tuple-element.40.kv_ref.refs_1_.refs_0_, bf16[416,128]{1,0:T(8,128)(2,1)S(1)} %get-tuple-element.43.par_kv_ref.refs_2_.refs_1_, ...), custom_call_target="tpu_custom_call" | custom-call | tf_op jit(solution)/shard_map/pallas_call | solution.py:576
  10.1 0.5 %shard_map.88 = (f32[384,384]{1,0:T(8,128)S(1)}, f32[384,384]{1,0:T(8,128)S(1)}, f32[8,384]{1,0:T(8,128)S(1)}) custom-call(bf16[384,128]{1,0:T(8,128)(2,1)S(1)} %get-tuple-element.44.q_all, bf16[384,128]{1,0:T(8,128)(2,1)S(1)} %get-tuple-element.45.g_all, f32[8,384]{1,0:T(8,128)S(1)} %get-tuple-element.46.table, f32[384,384]{1,0:T(8,128)S(1)} %get-tuple-element.47.s_own, ...), custom_call_target="tpu_custom_call" | custom-call | tf_op jit(solution)/shard_map/pallas_call | solution.py:588
  10.6 0.6 %collective-permute-done.3.refs_0_.refs_6_.refs_1_ = bf16[432,128]{1,0:T(8,128)(2,1)S(1)} collective-permute-done((bf16[432,128]{1,0:T(8,128)(2,1)S(1)}, bf16[432,128]{1,0:T(8,128)(2,1)S(1)}, u32[]{:S(2)}, u32[]{:S(2)}) %collective-permute-start.3) | collective-permute-done | bytes 110624 | tf_op jit(solution)/shard_map/ppermute | solution.py:545
  11.3 1.0 %collective-permute-start.7 = (bf16[1168,128]{1,0:T(8,128)(2,1)S(1)}, bf16[1168,128]{1,0:T(8,128)(2,1)S(1)}, u32[]{:S(2)}, u32[]{:S(2)}) collective-permute-start(bf16[1168,128]{1,0:T(8,128)(2,1)S(1)} %shard_map.93), channel_id=1, source_target_pairs={{0,10},{2,8},{4,14},{6,12},{8,2},{10,0},{12,6},{14,4},{16,26},{18,... | collective-permute-start | bytes 897032 | tf_op jit(solution)/shard_map/ppermute | solution.py:545
  12.3 0.2 collective-permute-start.9
  12.5 0.3 %collective-permute-done.5.refs_5_.refs_4_.extras = bf16[416,128]{1,0:T(8,128)(2,1)S(1)} collective-permute-done((bf16[416,128]{1,0:T(8,128)(2,1)S(1)}, bf16[416,128]{1,0:T(8,128)(2,1)S(1)}, u32[]{:S(2)}, u32[]{:S(2)}) %collective-permute-start.5) | collective-permute-done | bytes 106528 | tf_op jit(solution)/shard_map/ppermute | solution.py:545
  12.8 0.5 %shard_map.89 = (f32[384,384]{1,0:T(8,128)S(1)}, f32[576,256]{1,0:T(8,128)S(1)}, f32[8,384]{1,0:T(8,128)S(1)}) custom-call(bf16[384,128]{1,0:T(8,128)(2,1)S(1)} %get-tuple-element.44.q_all, bf16[384,128]{1,0:T(8,128)(2,1)S(1)} %get-tuple-element.45.g_all, f32[8,384]{1,0:T(8,128)S(1)} %get-tuple-element.46.table, f32[8,384]{1,0:T(8,128)S(1)} %get-tuple-element.51.part, ...), custom_call_target="tpu_custom_call" | custom-call | tf_op jit(solution)/shard_map/pallas_call | solution.py:591
  13.4 1.5 %collective-permute-start.6 = (f32[8,384]{1,0:T(8,128)S(1)}, f32[8,384]{1,0:T(8,128)S(1)}, u32[]{:S(2)}, u32[]{:S(2)}) collective-permute-start(f32[8,384]{1,0:T(8,128)S(1)} %get-tuple-element.55.refs_7_.refs_0_), channel_id=1, source_target_pairs={{0,24},{2,26},{4,28},{6,30},{8,16},{10,18},{12,20},{14,22},{16,8},... | collective-permute-start | bytes 36872 | tf_op jit(solution)/shard_map/ppermute | solution.py:545
  14.8 1.2 %shard_map.90 = (bf16[384,384]{1,0:T(8,128)(2,1)S(1)}, bf16[384,384]{1,0:T(8,128)(2,1)S(1)}, bf16[192,256]{1,0:T(8,128)(2,1)S(1)}, bf16[192,256]{1,0:T(8,128)(2,...) custom-call(bf16[384,128]{1,0:T(8,128)(2,1)S(1)} %get-tuple-element.44.q_all, ...), custom_call_target="tpu_custom_call" | custom-call | flops 20000000000 | tf_op jit(solution)/shard_map/pallas_call | solution.py:598
  16.0 0.5 %collective-permute-start.11 = (bf16[192,128]{1,0:T(8,128)(2,1)S(1)}, bf16[192,128]{1,0:T(8,128)(2,1)S(1)}, u32[]{:S(2)}, u32[]{:S(2)}) collective-permute-start(bf16[192,128]{1,0:T(8,128)(2,1)S(1)} %get-tuple-element.73), channel_id=1, source_target_pairs={{0,24},{2,26},{4,28},{6,30},{8,16},{10,18},{12,20},{14,22},{16,8},... | collective-permute-start | bytes 147464 | tf_op jit(solution)/shard_map/ppermute | solution.py:545
  16.6 2.2 %collective-permute-start.8 = (f32[8,384]{1,0:T(8,128)S(1)}, f32[8,384]{1,0:T(8,128)S(1)}, u32[]{:S(2)}, u32[]{:S(2)}) collective-permute-start(f32[8,384]{1,0:T(8,128)S(1)} %shard_map.91.note), channel_id=1, source_target_pairs={{0,10},{2,8},{4,14},{6,12},{8,2},{10,0},{12,6},{14,4},{16,26},{18,... | collective-permute-start | bytes 36872 | tf_op jit(solution)/shard_map/ppermute | solution.py:545
  18.8 0.5 %shard_map.92 = (f32[2,384,128]{2,1,0:T(8,128)S(1)}, f32[384,128]{1,0:T(8,128)S(1)}) custom-call(bf16[384,128]{1,0:T(8,128)(2,1)S(1)} %get-tuple-element.44.q_all, bf16[384,128]{1,0:T(8,128)(2,1)S(1)} %get-tuple-element.45.g_all, bf16[384,384]{1,0:T(8,128)(2,1)S(1)} %get-tuple-element.56.e_ref, bf16[384,384]{1,0:T(8,128)(2,1)S(1)} %get-tuple-element.57.ds_ref, ...), custom_call_target="tpu_custom_call" | custom-call | tf_op jit(solution)/shard_map/pallas_call | solution.py:617
  19.3 0.6 %collective-permute-done.7.message = bf16[1168,128]{1,0:T(8,128)(2,1)S(1)} collective-permute-done((bf16[1168,128]{1,0:T(8,128)(2,1)S(1)}, bf16[1168,128]{1,0:T(8,128)(2,1)S(1)}, u32[]{:S(2)}, u32[]{:S(2)}) %collective-permute-start.7) | collective-permute-done | bytes 299040 | tf_op jit(solution)/shard_map/ppermute | solution.py:545
  19.9 0.5 %shard_map.94 = (bf16[384,384]{1,0:T(8,128)(2,1)S(1)}, bf16[384,384]{1,0:T(8,128)(2,1)S(1)}, bf16[192,256]{1,0:T(8,128)(2,1)S(1)}, bf16[192,256]{1,0:T(8,128)(2,1)S(1)}, f32[8,384]{1,0:T(8,128)S(1)}) custom-call(bf16[448,128]{1,0:T(8,128)(2,1)S(1)} %get-tuple-element.40.kv_ref.refs_1_.refs_0_, ...), custom_call_target="tpu_custom_call" | custom-call | flops 20000000000 | tf_op jit(solution)/shard_map/pallas_call | solution.py:610
  20.4 0.5 %shard_map.95.outs_0_.own_ref = f32[2,384,128]{2,1,0:T(8,128)S(1)} custom-call(f32[2,384,128]{2,1,0:T(8,128)S(1)} %get-tuple-element.61.own_ref, bf16[1168,128]{1,0:T(8,128)(2,1)S(1)} %collective-permute-done.7.message, f32[8,384]{1,0:T(8,128)S(1)} %collective-permute-done.8.note, bf16[384,384]{1,0:T(8,128)(2,1)S(1)} %get-tuple-element.62.refs_0_, ...), custom_call_target="tpu_custom_call" | custom-call | tf_op jit(solution)/shard_map/pallas_call | solution.py:622
  21.2 0.9 %collective-permute-start.12 = (bf16[3,192,128]{2,1,0:T(8,128)(2,1)S(1)}, bf16[3,192,128]{2,1,0:T(8,128)(2,1)S(1)}, u32[]{:S(2)}, u32[]{:S(2)}) collective-permute-start(bf16[3,192,128]{2,1,0:T(8,128)(2,1)S(1)} %get-tuple-element.75), channel_id=1, source_target_pairs={{0,8},{8,0},{16,24},{24,16},{1,9},{9,1},{17,25},{25,17},{2,10},{10... | collective-permute-start | bytes 442376 | tf_op jit(solution)/shard_map/ppermute | solution.py:548
  22.0 1.0 %collective-permute-done.12.swap_ref = bf16[3,192,128]{2,1,0:T(8,128)(2,1)S(1)} collective-permute-done((bf16[3,192,128]{2,1,0:T(8,128)(2,1)S(1)}, bf16[3,192,128]{2,1,0:T(8,128)(2,1)S(1)}, u32[]{:S(2)}, u32[]{:S(2)}) %collective-permute-start.12) | collective-permute-done | bytes 147488 | tf_op jit(solution)/shard_map/ppermute | solution.py:548
  23.0 0.8 %shard_map.98 = (bf16[1,1,2,1,192,128]{5,4,3,2,1,0:T(8,128)(2,1)}, bf16[1,1,2,1,192,128]{5,4,3,2,1,0:T(8,128)(2,1)}, bf16[1,1,2,1,192,128]{5,4,3,2,1,0:T(8,128)(2,1)}) custom-call(bf16[2,192,128]{2,1,0:T(8,128)(2,1)S(1)} %get-tuple-element.74.mine_ref, bf16[3,192,128]{2,1,0:T(8,128)(2,1)S(1)} %collective-permute-done.12.swap_ref, ...), custom_call_target="tpu_custom_call" | custom-call | tf_op jit(solution)/shard_map/pallas_call | solution.py:631
  (16 shorter events, 0.5 us)
Async XLA Ops:
  1.8 4.5 %collective-permute-start = (bf16[976,128]{1,0:T(8,128)(2,1)S(1)}, bf16[976,128]{1,0:T(8,128)(2,1)S(1)}, u32[]{:S(2)}, u32[]{:S(2)}) collective-permute-start(bf16[976,128]{1,0:T(8,128)(2,1)S(1)} %get-tuple-element.42), channel_id=1, source_target_pairs={{0,8},{8,0},{16,24},{24,16},{1,9},{9,1},{17,25},{25,17},{2,10},{10... | collective-permute-start | bytes 749576 | tf_op jit(solution)/shard_map/ppermute | solution.py:548
  2.3 7.8 %collective-permute-start.1 = (bf16[448,128]{1,0:T(8,128)(2,1)S(1)}, bf16[448,128]{1,0:T(8,128)(2,1)S(1)}, u32[]{:S(2)}, u32[]{:S(2)}) collective-permute-start(bf16[448,128]{1,0:T(8,128)(2,1)S(1)} %get-tuple-element.40.kv_ref.refs_1_.refs_0_), channel_id=1, source_target_pairs={{0,8},{2,12},{4,10},{6,14},{8,0},{10,4},{12,2},{14,6},{16,24},{18,... | collective-permute-start | bytes 344072 | tf_op jit(solution)/shard_map/ppermute | solution.py:545
  2.4 7.8 %collective-permute-start.2 = (bf16[448,128]{1,0:T(8,128)(2,1)S(1)}, bf16[448,128]{1,0:T(8,128)(2,1)S(1)}, u32[]{:S(2)}, u32[]{:S(2)}) collective-permute-start(bf16[448,128]{1,0:T(8,128)(2,1)S(1)} %get-tuple-element.40.kv_ref.refs_1_.refs_0_), channel_id=1, source_target_pairs={{0,10},{2,8},{4,14},{6,12},{8,2},{10,0},{12,6},{14,4},{16,26},{18,... | collective-permute-start | bytes 344072 | tf_op jit(solution)/shard_map/ppermute | solution.py:545
  6.4 4.9 %collective-permute-start.3 = (bf16[432,128]{1,0:T(8,128)(2,1)S(1)}, bf16[432,128]{1,0:T(8,128)(2,1)S(1)}, u32[]{:S(2)}, u32[]{:S(2)}) collective-permute-start(bf16[432,128]{1,0:T(8,128)(2,1)S(1)} %get-tuple-element.52), channel_id=1, source_target_pairs={{0,24},{2,26},{4,28},{6,30},{8,16},{10,18},{12,20},{14,22},{16,8},... | collective-permute-start | bytes 331784 | tf_op jit(solution)/shard_map/ppermute | solution.py:545
  8.1 4.4 %collective-permute-start.4 = (bf16[416,128]{1,0:T(8,128)(2,1)S(1)}, bf16[416,128]{1,0:T(8,128)(2,1)S(1)}, u32[]{:S(2)}, u32[]{:S(2)}) collective-permute-start(bf16[416,128]{1,0:T(8,128)(2,1)S(1)} %get-tuple-element.43.par_kv_ref.refs_2_.refs_1_), channel_id=1, source_target_pairs={{0,8},{2,12},{4,10},{6,14},{8,0},{10,4},{12,2},{14,6},{16,24},{18,... | collective-permute-start | bytes 319496 | tf_op jit(solution)/shard_map/ppermute | solution.py:545
  8.1 4.7 %collective-permute-start.5 = (bf16[416,128]{1,0:T(8,128)(2,1)S(1)}, bf16[416,128]{1,0:T(8,128)(2,1)S(1)}, u32[]{:S(2)}, u32[]{:S(2)}) collective-permute-start(bf16[416,128]{1,0:T(8,128)(2,1)S(1)} %get-tuple-element.43.par_kv_ref.refs_2_.refs_1_), channel_id=1, source_target_pairs={{0,10},{2,8},{4,14},{6,12},{8,2},{10,0},{12,6},{14,4},{16,26},{18,... | collective-permute-start | bytes 319496 | tf_op jit(solution)/shard_map/ppermute | solution.py:545
  11.3 8.6 %collective-permute-start.7 = (bf16[1168,128]{1,0:T(8,128)(2,1)S(1)}, bf16[1168,128]{1,0:T(8,128)(2,1)S(1)}, u32[]{:S(2)}, u32[]{:S(2)}) collective-permute-start(bf16[1168,128]{1,0:T(8,128)(2,1)S(1)} %shard_map.93), channel_id=1, source_target_pairs={{0,10},{2,8},{4,14},{6,12},{8,2},{10,0},{12,6},{14,4},{16,26},{18,... | collective-permute-start | bytes 897032 | tf_op jit(solution)/shard_map/ppermute | solution.py:545
  12.3 8.6 %collective-permute-start.9 = (bf16[1168,128]{1,0:T(8,128)(2,1)S(1)}, bf16[1168,128]{1,0:T(8,128)(2,1)S(1)}, u32[]{:S(2)}, u32[]{:S(2)}) collective-permute-start(bf16[1168,128]{1,0:T(8,128)(2,1)S(1)} %shard_map.93), channel_id=1, source_target_pairs={{0,8},{2,12},{4,10},{6,14},{8,0},{10,4},{12,2},{14,6},{16,24},{18,... | collective-permute-start | bytes 897032 | tf_op jit(solution)/shard_map/ppermute | solution.py:545
  13.4 3.2 %collective-permute-start.6 = (f32[8,384]{1,0:T(8,128)S(1)}, f32[8,384]{1,0:T(8,128)S(1)}, u32[]{:S(2)}, u32[]{:S(2)}) collective-permute-start(f32[8,384]{1,0:T(8,128)S(1)} %get-tuple-element.55.refs_7_.refs_0_), channel_id=1, source_target_pairs={{0,24},{2,26},{4,28},{6,30},{8,16},{10,18},{12,20},{14,22},{16,8},... | collective-permute-start | bytes 36872 | tf_op jit(solution)/shard_map/ppermute | solution.py:545
  16.0 5.0 %collective-permute-start.11 = (bf16[192,128]{1,0:T(8,128)(2,1)S(1)}, bf16[192,128]{1,0:T(8,128)(2,1)S(1)}, u32[]{:S(2)}, u32[]{:S(2)}) collective-permute-start(bf16[192,128]{1,0:T(8,128)(2,1)S(1)} %get-tuple-element.73), channel_id=1, source_target_pairs={{0,24},{2,26},{4,28},{6,30},{8,16},{10,18},{12,20},{14,22},{16,8},... | collective-permute-start | bytes 147464 | tf_op jit(solution)/shard_map/ppermute | solution.py:545
  16.6 3.8 %collective-permute-start.8 = (f32[8,384]{1,0:T(8,128)S(1)}, f32[8,384]{1,0:T(8,128)S(1)}, u32[]{:S(2)}, u32[]{:S(2)}) collective-permute-start(f32[8,384]{1,0:T(8,128)S(1)} %shard_map.91.note), channel_id=1, source_target_pairs={{0,10},{2,8},{4,14},{6,12},{8,2},{10,0},{12,6},{14,4},{16,26},{18,... | collective-permute-start | bytes 36872 | tf_op jit(solution)/shard_map/ppermute | solution.py:545
  18.8 2.2 %collective-permute-start.10 = (f32[8,384]{1,0:T(8,128)S(1)}, f32[8,384]{1,0:T(8,128)S(1)}, u32[]{:S(2)}, u32[]{:S(2)}) collective-permute-start(f32[8,384]{1,0:T(8,128)S(1)} %shard_map.91.note), channel_id=1, source_target_pairs={{0,8},{2,12},{4,10},{6,14},{8,0},{10,4},{12,2},{14,6},{16,24},{18,... | collective-permute-start | bytes 36872 | tf_op jit(solution)/shard_map/ppermute | solution.py:545
  21.2 1.9 %collective-permute-start.12 = (bf16[3,192,128]{2,1,0:T(8,128)(2,1)S(1)}, bf16[3,192,128]{2,1,0:T(8,128)(2,1)S(1)}, u32[]{:S(2)}, u32[]{:S(2)}) collective-permute-start(bf16[3,192,128]{2,1,0:T(8,128)(2,1)S(1)} %get-tuple-element.75), channel_id=1, source_target_pairs={{0,8},{8,0},{16,24},{24,16},{1,9},{9,1},{17,25},{25,17},{2,10},{10... | collective-permute-start | bytes 442376 | tf_op jit(solution)/shard_map/ppermute | solution.py:548

commit v6 on v4

--- a/solution.py
+++ b/solution.py
@@ -410,14 +410,15 @@
     return (block.astype(jnp.float32) * column).astype(jnp.bfloat16)
 
 
-def key_sums(tok, near, line, e_ref, ds_ref, scaled, far):
-    rows = [rows_at(2 * line + slot, tok) for slot in range(2)]
+def key_sums(tok, near, line, e_ref, ds_ref, scaled, far, slots=(0, 1)):
+    rows = [rows_at(2 * line + slot, tok) for slot in slots]
     sums = [[dot(ref[at, :], scaled[i]) for i, ref in enumerate((ds_ref, e_ref))] for at in rows]
     for which, (e_far, ds_far, at, far_scaled) in enumerate(far):
         for i, ref in enumerate((ds_far, e_far)):
             block = dot(ref[at, :], far_scaled[i])
-            for slot in range(2):
-                sums[slot][i] = sums[slot][i] + jnp.where(near == ((slot == 0) == (which == 0)), block, 0.0)
+            for at_slot, slot in enumerate(slots):
+                mine = near == ((slot == 0) == (which == 0))
+                sums[at_slot][i] = sums[at_slot][i] + jnp.where(mine, block, 0.0)
     return sums
 
 
@@ -443,7 +444,7 @@
             own_ref[i, rows_at(slot, tok), :] = sums[slot][i]
 
 
-def line_sums(tok, heights, sides, line, sums, message, note, e_ref, ds_ref, e_far, ds_far, top_ref):
+def line_sums(tok, heights, sides, line, slot, sums, message, note, e_ref, ds_ref, e_far, ds_far, top_ref):
     y, c, z = place()
     near = border_is_own(y, c)
 
@@ -456,31 +457,38 @@
             far_factor = jnp.exp(top_ref[at : at + 1, lanes] - note[at : at + 1, lanes])
             rows = [foreign_rows(far_part(message, which, tok), part, which, tok) for part in range(2)]
             far.append((e_far, ds_far, rows_at(which, tok), [times(block, far_factor) for block in rows]))
-        more = key_sums(tok, near, 0, e_ref, ds_ref, scaled, far)
-        for slot in range(2):
-            for i in range(2):
-                sums[i, rows_at(slot, tok), :] += more[slot][i]
+        more = key_sums(tok, near, 0, e_ref, ds_ref, scaled, far, (slot,))
+        for i in range(2):
+            sums[i] += more[0][i]
 
     pl.when(line_place(z, line, heights)[0])(work)
 
 
 def join_kernel(tok, heights, sides, line, own_ref, message, note, *refs):
     *terms, sums = refs
-    sums[...] = own_ref[...]
-    line_sums(tok, heights, sides, line, sums, message, note, *terms)
+    sums[...] = own_ref[:, rows_at(1, tok), :]
+    line_sums(tok, heights, sides, line, 1, sums, message, note, *terms)
+
+
+def own_kernel(tok, heights, sides, own_ref, *refs):
+    *refs, mine_ref, sums = refs
+    sums[...] = own_ref[:, rows_at(0, tok), :]
+    for i, line in enumerate((2, 1)):
+        line_sums(tok, heights, sides, line, 0, sums, *refs[7 * i : 7 * i + 7])
+    mine_ref[...] = sums[...].astype(jnp.bfloat16)
 
 
 def leave_kernel(tok, chips, heights, sides, line, own_ref, dq_ref, note, message, note_in, *refs):
     terms, refs = refs[:5], refs[5:]
-    came, backs, (mine_ref, mine_q_ref, swap_ref, sums) = refs[:sides], refs[sides : 2 * sides], refs[2 * sides :]
+    came, backs, (mine_q_ref, swap_ref, sums) = refs[:sides], refs[sides : 2 * sides], refs[2 * sides :]
     y, c, _ = place()
     near = border_is_own(y, c)
     f32, bf16 = jnp.float32, jnp.bfloat16
     width = dq_ref.shape[1]
     sums[...] = own_ref[...]
-    line_sums(tok, heights, sides, line, sums, message, note_in, *terms)
+    line_sums(tok, heights, sides, line, 1, sums, message, note_in, *terms)
     for i in range(2):
-        mine_ref[i], swap_ref[i] = sums[i, rows_at(0, tok), :].astype(bf16), sums[i, rows_at(1, tok), :].astype(bf16)
+        swap_ref[i] = sums[i].astype(bf16)
     tiles = []
     for tile in range(2):
         value = dq_ref[rows_at(tile, tok), :]
@@ -614,15 +622,25 @@
         [sums_shape, ((two, width), f32)],
         [VMEM] * (8 + 2 * sides),
     )(*qg, e, ds, e_far, ds_far, raw_dq, note, *sent, *foreign)
+    part_shape = ((2, tok, width), f32)
+    even_terms = line_terms(2)
     (joined,) = call(
-        functools.partial(join_kernel, tok, heights, sides, 2), [sums_shape], [VMEM] * 8
-    )(own, queries_in[1], notes[1], *line_terms(2))
-    mine, mine_q, leaving = call(
+        functools.partial(join_kernel, tok, heights, sides, 2), [part_shape], [VMEM] * 8
+    )(own, queries_in[1], notes[1], *even_terms)
+    odd_terms = line_terms(1, joined)
+    mine_q, leaving = call(
         functools.partial(leave_kernel, tok, chips, heights, sides, 1),
-        [tile_shape, ((tok, width), bf16), ((3, tok, width), bf16)],
+        [((tok, width), bf16), ((3, tok, width), bf16)],
         [VMEM] * (10 + 2 * sides),
-        [pltpu.VMEM(*sums_shape)],
-    )(joined, dq, note, queries_in[0], notes[0], *line_terms(1, joined), *came, *shares)
+        [pltpu.VMEM(*part_shape)],
+    )(joined, dq, note, queries_in[0], notes[0], *odd_terms, *came, *shares)
+    (mine,) = call(
+        functools.partial(own_kernel, tok, heights, sides),
+        [tile_shape],
+        [VMEM] * 15,
+        [pltpu.VMEM(*part_shape)],
+        cost=20,
+    )(own, queries_in[1], notes[1], *even_terms, queries_in[0], notes[0], *odd_terms)
     return call(final_kernel, [(queries.shape, bf16)] * 3, [VMEM] * 3)(mine, swap_cores(leaving), mine_q)
 
 

time: 24 us -> 23.9 us (level)
  waiting for transfers between devices: 2.69 us -> 2.23 us
  Pallas kernels: 6.38 us -> 6.74 us
    ppermute x2, waiting for transfers between devices: 1.01 us -> 0.56 us  [swap_cores(): return lax.ppermute(block, 'tm', [(t, t ^ 1) for t in range(times)])]
    pallas_call x2 -> x3, Pallas kernels: 0.67 us -> 1.03 us  [the longest x1 0.45 us: body(): call(functools.partial(own_kernel, tok, heights, sides), [tile_shape], [V...]
  transfers between devices with their start and end apart: 13 -> 13, of which waited for: 5 -> 5; matrix products, arithmetic and copies ran while one was open for 0% -> 0% of each run, Pallas kernels for 18% -> 20%
where the time goes in v6:
time: 23.9 us; the launch traced here: 23.7 us
  starting transfers between devices  13.9 us (58%)
  Pallas kernels  6.74 us (28%)
  waiting for transfers between devices  2.23 us (9%)
  between operations  0.77 us (3%)
    ppermute x11, starting transfers between devices, exchange(): return lax.ppermute(block, ('tm', 'height'), pairs)  12.6 us
    ppermute x11, waiting for transfers between devices, exchange(): return lax.ppermute(block, ('tm', 'height'), pairs)  1.68 us
    ppermute x2, starting transfers between devices, swap_cores(): return lax.ppermute(block, 'tm', [(t, t ^ 1) for t in range(times)])  1.38 us
    pallas_call x1, Pallas kernels, body(): call(functools.partial(middle_kernel, tok, sides, scale), [square(2, bf16...  1.24 us
    pallas_call x1, Pallas kernels, body(): call(functools.partial(pack_kernel, tok), [((2 * tok + extra, width), bf1...  1.13 us
    pallas_call x1, Pallas kernels, body(): call(final_kernel, [(queries.shape, bf16)] * 3, [VMEM] * 3)  0.74 us
    ppermute x2, waiting for transfers between devices, swap_cores(): return lax.ppermute(block, 'tm', [(t, t ^ 1) for t in range(times)])  0.56 us
    pallas_call x1, Pallas kernels, body(): call(functools.partial(score_kernel, tok, chips, heights, sides, scale),...  0.53 us
  transfers between devices with their start and end apart: 13, of which 5 were waited for; matrix products, arithmetic and copies ran while one was open for 0% of the time, Pallas kernels for 20%

profile of v6, /device:TPU:0, one launch (start us, length us, event | category | flops | bytes accessed | tf_op | source)
XLA Modules:
  0.0 23.7 jit_solution(10909097187358194561)
XLA Ops:
  0.6 1.1 %shard_map.85 = (bf16[448,128]{1,0:T(8,128)(2,1)S(1)}, bf16[592,128]{1,0:T(8,128)(2,1)S(1)}, bf16[976,128]{1,0:T(8,128)(2,1)S(1)}) custom-call(bf16[1,1,2,1,192,128]{5,4,3,2,1,0:T(8,128)(2,1)} %k_ref.1, bf16[1,1,2,1,192,128]{5,4,3,2,1,0:T(8,128)(2,1)} %v_ref.1, bf16[1,1,2,1,192,128]{5,4,3,2,1,0:T(8,128)(2,1)} %q_ref.1, ...), custom_call_target="tpu_custom_call" | custom-call | tf_op jit(solution)/shard_map/pallas_call | solution.py:556
  1.8 0.5 %collective-permute-start = (bf16[976,128]{1,0:T(8,128)(2,1)S(1)}, bf16[976,128]{1,0:T(8,128)(2,1)S(1)}, u32[]{:S(2)}, u32[]{:S(2)}) collective-permute-start(bf16[976,128]{1,0:T(8,128)(2,1)S(1)} %get-tuple-element.41), channel_id=1, source_target_pairs={{0,8},{8,0},{16,24},{24,16},{1,9},{9,1},{17,25},{25,17},{2,10},{10... | collective-permute-start | bytes 749576 | tf_op jit(solution)/shard_map/ppermute | solution.py:551
  2.4 3.9 %collective-permute-start.2 = (bf16[448,128]{1,0:T(8,128)(2,1)S(1)}, bf16[448,128]{1,0:T(8,128)(2,1)S(1)}, u32[]{:S(2)}, u32[]{:S(2)}) collective-permute-start(bf16[448,128]{1,0:T(8,128)(2,1)S(1)} %get-tuple-element.39.kv_ref.refs_1_.refs_0_), channel_id=1, source_target_pairs={{0,10},{2,8},{4,14},{6,12},{8,2},{10,0},{12,6},{14,4},{16,26},{18,... | collective-permute-start | bytes 344072 | tf_op jit(solution)/shard_map/ppermute | solution.py:548
  6.2 0.2 shard_map.86
  6.4 1.6 %collective-permute-start.3 = (bf16[432,128]{1,0:T(8,128)(2,1)S(1)}, bf16[432,128]{1,0:T(8,128)(2,1)S(1)}, u32[]{:S(2)}, u32[]{:S(2)}) collective-permute-start(bf16[432,128]{1,0:T(8,128)(2,1)S(1)} %get-tuple-element.51), channel_id=1, source_target_pairs={{0,24},{2,26},{4,28},{6,30},{8,16},{10,18},{12,20},{14,22},{16,8},... | collective-permute-start | bytes 331784 | tf_op jit(solution)/shard_map/ppermute | solution.py:548
  8.1 1.6 %collective-permute-start.5 = (bf16[416,128]{1,0:T(8,128)(2,1)S(1)}, bf16[416,128]{1,0:T(8,128)(2,1)S(1)}, u32[]{:S(2)}, u32[]{:S(2)}) collective-permute-start(bf16[416,128]{1,0:T(8,128)(2,1)S(1)} %get-tuple-element.42.par_kv_ref.refs_2_.refs_1_), channel_id=1, source_target_pairs={{0,10},{2,8},{4,14},{6,12},{8,2},{10,0},{12,6},{14,4},{16,26},{18,... | collective-permute-start | bytes 319496 | tf_op jit(solution)/shard_map/ppermute | solution.py:548
  9.7 0.4 %shard_map.87 = (bf16[384,128]{1,0:T(8,128)(2,1)S(1)}, bf16[384,128]{1,0:T(8,128)(2,1)S(1)}, f32[8,384]{1,0:T(8,128)S(1)}, f32[384,384]{1,0:T(8,128)S(1)}, f32[384,384]{1,0:T(8,128)S(1)}) custom-call(bf16[448,128]{1,0:T(8,128)(2,1)S(1)} %get-tuple-element.39.kv_ref.refs_1_.refs_0_, bf16[416,128]{1,0:T(8,128)(2,1)S(1)} %get-tuple-element.42.par_kv_ref.refs_2_.refs_1_, ...), custom_call_target="tpu_custom_call" | custom-call | tf_op jit(solution)/shard_map/pallas_call | solution.py:579
  10.1 0.5 %shard_map.88 = (f32[384,384]{1,0:T(8,128)S(1)}, f32[384,384]{1,0:T(8,128)S(1)}, f32[8,384]{1,0:T(8,128)S(1)}) custom-call(bf16[384,128]{1,0:T(8,128)(2,1)S(1)} %get-tuple-element.43.q_all, bf16[384,128]{1,0:T(8,128)(2,1)S(1)} %get-tuple-element.44.g_all, f32[8,384]{1,0:T(8,128)S(1)} %get-tuple-element.45.table, f32[384,384]{1,0:T(8,128)S(1)} %get-tuple-element.46.s_own, ...), custom_call_target="tpu_custom_call" | custom-call | tf_op jit(solution)/shard_map/pallas_call | solution.py:591
  10.6 0.6 %collective-permute-done.3.refs_0_.refs_6_.refs_1_ = bf16[432,128]{1,0:T(8,128)(2,1)S(1)} collective-permute-done((bf16[432,128]{1,0:T(8,128)(2,1)S(1)}, bf16[432,128]{1,0:T(8,128)(2,1)S(1)}, u32[]{:S(2)}, u32[]{:S(2)}) %collective-permute-start.3) | collective-permute-done | bytes 110624 | tf_op jit(solution)/shard_map/ppermute | solution.py:548
  11.3 1.0 %collective-permute-start.7 = (bf16[1168,128]{1,0:T(8,128)(2,1)S(1)}, bf16[1168,128]{1,0:T(8,128)(2,1)S(1)}, u32[]{:S(2)}, u32[]{:S(2)}) collective-permute-start(bf16[1168,128]{1,0:T(8,128)(2,1)S(1)} %shard_map.93), channel_id=1, source_target_pairs={{0,10},{2,8},{4,14},{6,12},{8,2},{10,0},{12,6},{14,4},{16,26},{18,... | collective-permute-start | bytes 897032 | tf_op jit(solution)/shard_map/ppermute | solution.py:548
  12.5 0.3 %collective-permute-done.5.refs_5_.refs_4_.extras = bf16[416,128]{1,0:T(8,128)(2,1)S(1)} collective-permute-done((bf16[416,128]{1,0:T(8,128)(2,1)S(1)}, bf16[416,128]{1,0:T(8,128)(2,1)S(1)}, u32[]{:S(2)}, u32[]{:S(2)}) %collective-permute-start.5) | collective-permute-done | bytes 106528 | tf_op jit(solution)/shard_map/ppermute | solution.py:548
  12.8 0.5 %shard_map.89 = (f32[384,384]{1,0:T(8,128)S(1)}, f32[576,256]{1,0:T(8,128)S(1)}, f32[8,384]{1,0:T(8,128)S(1)}) custom-call(bf16[384,128]{1,0:T(8,128)(2,1)S(1)} %get-tuple-element.43.q_all, bf16[384,128]{1,0:T(8,128)(2,1)S(1)} %get-tuple-element.44.g_all, f32[8,384]{1,0:T(8,128)S(1)} %get-tuple-element.45.table, f32[8,384]{1,0:T(8,128)S(1)} %get-tuple-element.50.part, ...), custom_call_target="tpu_custom_call" | custom-call | tf_op jit(solution)/shard_map/pallas_call | solution.py:594
  13.4 1.5 %collective-permute-start.6 = (f32[8,384]{1,0:T(8,128)S(1)}, f32[8,384]{1,0:T(8,128)S(1)}, u32[]{:S(2)}, u32[]{:S(2)}) collective-permute-start(f32[8,384]{1,0:T(8,128)S(1)} %get-tuple-element.54.refs_7_.refs_0_), channel_id=1, source_target_pairs={{0,24},{2,26},{4,28},{6,30},{8,16},{10,18},{12,20},{14,22},{16,8},... | collective-permute-start | bytes 36872 | tf_op jit(solution)/shard_map/ppermute | solution.py:548
  14.8 1.2 %shard_map.90 = (bf16[384,384]{1,0:T(8,128)(2,1)S(1)}, bf16[384,384]{1,0:T(8,128)(2,1)S(1)}, bf16[192,256]{1,0:T(8,128)(2,1)S(1)}, bf16[192,256]{1,0:T(8,128)(2,...) custom-call(bf16[384,128]{1,0:T(8,128)(2,1)S(1)} %get-tuple-element.43.q_all, ...), custom_call_target="tpu_custom_call" | custom-call | flops 20000000000 | tf_op jit(solution)/shard_map/pallas_call | solution.py:601
  16.0 0.5 %collective-permute-start.11 = (bf16[192,128]{1,0:T(8,128)(2,1)S(1)}, bf16[192,128]{1,0:T(8,128)(2,1)S(1)}, u32[]{:S(2)}, u32[]{:S(2)}) collective-permute-start(bf16[192,128]{1,0:T(8,128)(2,1)S(1)} %get-tuple-element.72), channel_id=1, source_target_pairs={{0,24},{2,26},{4,28},{6,30},{8,16},{10,18},{12,20},{14,22},{16,8},... | collective-permute-start | bytes 147464 | tf_op jit(solution)/shard_map/ppermute | solution.py:548
  16.6 2.2 %collective-permute-start.8 = (f32[8,384]{1,0:T(8,128)S(1)}, f32[8,384]{1,0:T(8,128)S(1)}, u32[]{:S(2)}, u32[]{:S(2)}) collective-permute-start(f32[8,384]{1,0:T(8,128)S(1)} %shard_map.91.note), channel_id=1, source_target_pairs={{0,10},{2,8},{4,14},{6,12},{8,2},{10,0},{12,6},{14,4},{16,26},{18,... | collective-permute-start | bytes 36872 | tf_op jit(solution)/shard_map/ppermute | solution.py:548
  18.8 0.5 %shard_map.92 = (f32[2,384,128]{2,1,0:T(8,128)S(1)}, f32[384,128]{1,0:T(8,128)S(1)}) custom-call(bf16[384,128]{1,0:T(8,128)(2,1)S(1)} %get-tuple-element.43.q_all, bf16[384,128]{1,0:T(8,128)(2,1)S(1)} %get-tuple-element.44.g_all, bf16[384,384]{1,0:T(8,128)(2,1)S(1)} %get-tuple-element.55.e_ref, bf16[384,384]{1,0:T(8,128)(2,1)S(1)} %get-tuple-element.56.ds_ref, ...), custom_call_target="tpu_custom_call" | custom-call | tf_op jit(solution)/shard_map/pallas_call | solution.py:620
  19.3 0.6 %collective-permute-done.7.message.refs_0_ = bf16[1168,128]{1,0:T(8,128)(2,1)S(1)} collective-permute-done((bf16[1168,128]{1,0:T(8,128)(2,1)S(1)}, bf16[1168,128]{1,0:T(8,128)(2,1)S(1)}, u32[]{:S(2)}, u32[]{:S(2)}) %collective-permute-start.7) | collective-permute-done | bytes 299040 | tf_op jit(solution)/shard_map/ppermute | solution.py:548
  19.9 0.5 %shard_map.94 = (bf16[384,384]{1,0:T(8,128)(2,1)S(1)}, bf16[384,384]{1,0:T(8,128)(2,1)S(1)}, bf16[192,256]{1,0:T(8,128)(2,1)S(1)}, bf16[192,256]{1,0:T(8,128)(2,1)S(1)}, f32[8,384]{1,0:T(8,128)S(1)}) custom-call(bf16[448,128]{1,0:T(8,128)(2,1)S(1)} %get-tuple-element.39.kv_ref.refs_1_.refs_0_, ...), custom_call_target="tpu_custom_call" | custom-call | flops 20000000000 | tf_op jit(solution)/shard_map/pallas_call | solution.py:613
  20.4 0.4 %shard_map.95.outs_0_.own_ref = f32[2,192,128]{2,1,0:T(8,128)S(1)} custom-call(f32[2,384,128]{2,1,0:T(8,128)S(1)} %get-tuple-element.60.own_ref, bf16[1168,128]{1,0:T(8,128)(2,1)S(1)} %collective-permute-done.7.message.refs_0_, f32[8,384]{1,0:T(8,128)S(1)} %collective-permute-done.8.note.refs_1_, bf16[384,384]{1,0:T(8,128)(2,1)S(1)} %get-tuple-element.61.refs_0_.refs_2_, ...), custom_call_target="tpu_custom_call" | custom-call | tf_op jit(solution)/shard_map/pallas_call | solution.py:627
  21.1 0.9 %collective-permute-start.12 = (bf16[3,192,128]{2,1,0:T(8,128)(2,1)S(1)}, bf16[3,192,128]{2,1,0:T(8,128)(2,1)S(1)}, u32[]{:S(2)}, u32[]{:S(2)}) collective-permute-start(bf16[3,192,128]{2,1,0:T(8,128)(2,1)S(1)} %get-tuple-element.73), channel_id=1, source_target_pairs={{0,8},{8,0},{16,24},{24,16},{1,9},{9,1},{17,25},{25,17},{2,10},{10... | collective-permute-start | bytes 442376 | tf_op jit(solution)/shard_map/ppermute | solution.py:551
  21.9 0.4 %shard_map.97.mine_ref = bf16[2,192,128]{2,1,0:T(8,128)(2,1)S(1)} custom-call(f32[2,384,128]{2,1,0:T(8,128)S(1)} %get-tuple-element.60.own_ref, bf16[1168,128]{1,0:T(8,128)(2,1)S(1)} %collective-permute-done.7.message.refs_0_, f32[8,384]{1,0:T(8,128)S(1)} %collective-permute-done.8.note.refs_1_, bf16[384,384]{1,0:T(8,128)(2,1)S(1)} %get-tuple-element.61.refs_0_.refs_2_, ...), custom_call_target="tpu_custom_call" | custom-call | flops 20000000000 | tf_op jit(solution)/shard_map/pallas_call | solution.py:637
  22.4 0.6 %collective-permute-done.12.swap_ref = bf16[3,192,128]{2,1,0:T(8,128)(2,1)S(1)} collective-permute-done((bf16[3,192,128]{2,1,0:T(8,128)(2,1)S(1)}, bf16[3,192,128]{2,1,0:T(8,128)(2,1)S(1)}, u32[]{:S(2)}, u32[]{:S(2)}) %collective-permute-start.12) | collective-permute-done | bytes 147488 | tf_op jit(solution)/shard_map/ppermute | solution.py:551
  23.0 0.7 %shard_map.99 = (bf16[1,1,2,1,192,128]{5,4,3,2,1,0:T(8,128)(2,1)}, bf16[1,1,2,1,192,128]{5,4,3,2,1,0:T(8,128)(2,1)}, bf16[1,1,2,1,192,128]{5,4,3,2,1,0:T(8,128)(2,1)}) custom-call(bf16[2,192,128]{2,1,0:T(8,128)(2,1)S(1)} %shard_map.97.mine_ref, bf16[3,192,128]{2,1,0:T(8,128)(2,1)S(1)} %collective-permute-done.12.swap_ref, ...), custom_call_target="tpu_custom_call" | custom-call | tf_op jit(solution)/shard_map/pallas_call | solution.py:644
  (17 shorter events, 0.6 us)
Async XLA Ops:
  1.8 4.5 %collective-permute-start = (bf16[976,128]{1,0:T(8,128)(2,1)S(1)}, bf16[976,128]{1,0:T(8,128)(2,1)S(1)}, u32[]{:S(2)}, u32[]{:S(2)}) collective-permute-start(bf16[976,128]{1,0:T(8,128)(2,1)S(1)} %get-tuple-element.41), channel_id=1, source_target_pairs={{0,8},{8,0},{16,24},{24,16},{1,9},{9,1},{17,25},{25,17},{2,10},{10... | collective-permute-start | bytes 749576 | tf_op jit(solution)/shard_map/ppermute | solution.py:551
  2.3 7.8 %collective-permute-start.1 = (bf16[448,128]{1,0:T(8,128)(2,1)S(1)}, bf16[448,128]{1,0:T(8,128)(2,1)S(1)}, u32[]{:S(2)}, u32[]{:S(2)}) collective-permute-start(bf16[448,128]{1,0:T(8,128)(2,1)S(1)} %get-tuple-element.39.kv_ref.refs_1_.refs_0_), channel_id=1, source_target_pairs={{0,8},{2,12},{4,10},{6,14},{8,0},{10,4},{12,2},{14,6},{16,24},{18,... | collective-permute-start | bytes 344072 | tf_op jit(solution)/shard_map/ppermute | solution.py:548
  2.4 7.8 %collective-permute-start.2 = (bf16[448,128]{1,0:T(8,128)(2,1)S(1)}, bf16[448,128]{1,0:T(8,128)(2,1)S(1)}, u32[]{:S(2)}, u32[]{:S(2)}) collective-permute-start(bf16[448,128]{1,0:T(8,128)(2,1)S(1)} %get-tuple-element.39.kv_ref.refs_1_.refs_0_), channel_id=1, source_target_pairs={{0,10},{2,8},{4,14},{6,12},{8,2},{10,0},{12,6},{14,4},{16,26},{18,... | collective-permute-start | bytes 344072 | tf_op jit(solution)/shard_map/ppermute | solution.py:548
  6.4 4.9 %collective-permute-start.3 = (bf16[432,128]{1,0:T(8,128)(2,1)S(1)}, bf16[432,128]{1,0:T(8,128)(2,1)S(1)}, u32[]{:S(2)}, u32[]{:S(2)}) collective-permute-start(bf16[432,128]{1,0:T(8,128)(2,1)S(1)} %get-tuple-element.51), channel_id=1, source_target_pairs={{0,24},{2,26},{4,28},{6,30},{8,16},{10,18},{12,20},{14,22},{16,8},... | collective-permute-start | bytes 331784 | tf_op jit(solution)/shard_map/ppermute | solution.py:548
  8.1 4.4 %collective-permute-start.4 = (bf16[416,128]{1,0:T(8,128)(2,1)S(1)}, bf16[416,128]{1,0:T(8,128)(2,1)S(1)}, u32[]{:S(2)}, u32[]{:S(2)}) collective-permute-start(bf16[416,128]{1,0:T(8,128)(2,1)S(1)} %get-tuple-element.42.par_kv_ref.refs_2_.refs_1_), channel_id=1, source_target_pairs={{0,8},{2,12},{4,10},{6,14},{8,0},{10,4},{12,2},{14,6},{16,24},{18,... | collective-permute-start | bytes 319496 | tf_op jit(solution)/shard_map/ppermute | solution.py:548
  8.1 4.7 %collective-permute-start.5 = (bf16[416,128]{1,0:T(8,128)(2,1)S(1)}, bf16[416,128]{1,0:T(8,128)(2,1)S(1)}, u32[]{:S(2)}, u32[]{:S(2)}) collective-permute-start(bf16[416,128]{1,0:T(8,128)(2,1)S(1)} %get-tuple-element.42.par_kv_ref.refs_2_.refs_1_), channel_id=1, source_target_pairs={{0,10},{2,8},{4,14},{6,12},{8,2},{10,0},{12,6},{14,4},{16,26},{18,... | collective-permute-start | bytes 319496 | tf_op jit(solution)/shard_map/ppermute | solution.py:548
  11.3 8.6 %collective-permute-start.7 = (bf16[1168,128]{1,0:T(8,128)(2,1)S(1)}, bf16[1168,128]{1,0:T(8,128)(2,1)S(1)}, u32[]{:S(2)}, u32[]{:S(2)}) collective-permute-start(bf16[1168,128]{1,0:T(8,128)(2,1)S(1)} %shard_map.93), channel_id=1, source_target_pairs={{0,10},{2,8},{4,14},{6,12},{8,2},{10,0},{12,6},{14,4},{16,26},{18,... | collective-permute-start | bytes 897032 | tf_op jit(solution)/shard_map/ppermute | solution.py:548
  12.3 8.5 %collective-permute-start.9 = (bf16[1168,128]{1,0:T(8,128)(2,1)S(1)}, bf16[1168,128]{1,0:T(8,128)(2,1)S(1)}, u32[]{:S(2)}, u32[]{:S(2)}) collective-permute-start(bf16[1168,128]{1,0:T(8,128)(2,1)S(1)} %shard_map.93), channel_id=1, source_target_pairs={{0,8},{2,12},{4,10},{6,14},{8,0},{10,4},{12,2},{14,6},{16,24},{18,... | collective-permute-start | bytes 897032 | tf_op jit(solution)/shard_map/ppermute | solution.py:548
  13.4 3.2 %collective-permute-start.6 = (f32[8,384]{1,0:T(8,128)S(1)}, f32[8,384]{1,0:T(8,128)S(1)}, u32[]{:S(2)}, u32[]{:S(2)}) collective-permute-start(f32[8,384]{1,0:T(8,128)S(1)} %get-tuple-element.54.refs_7_.refs_0_), channel_id=1, source_target_pairs={{0,24},{2,26},{4,28},{6,30},{8,16},{10,18},{12,20},{14,22},{16,8},... | collective-permute-start | bytes 36872 | tf_op jit(solution)/shard_map/ppermute | solution.py:548
  16.0 4.9 %collective-permute-start.11 = (bf16[192,128]{1,0:T(8,128)(2,1)S(1)}, bf16[192,128]{1,0:T(8,128)(2,1)S(1)}, u32[]{:S(2)}, u32[]{:S(2)}) collective-permute-start(bf16[192,128]{1,0:T(8,128)(2,1)S(1)} %get-tuple-element.72), channel_id=1, source_target_pairs={{0,24},{2,26},{4,28},{6,30},{8,16},{10,18},{12,20},{14,22},{16,8},... | collective-permute-start | bytes 147464 | tf_op jit(solution)/shard_map/ppermute | solution.py:548
  16.6 3.8 %collective-permute-start.8 = (f32[8,384]{1,0:T(8,128)S(1)}, f32[8,384]{1,0:T(8,128)S(1)}, u32[]{:S(2)}, u32[]{:S(2)}) collective-permute-start(f32[8,384]{1,0:T(8,128)S(1)} %shard_map.91.note), channel_id=1, source_target_pairs={{0,10},{2,8},{4,14},{6,12},{8,2},{10,0},{12,6},{14,4},{16,26},{18,... | collective-permute-start | bytes 36872 | tf_op jit(solution)/shard_map/ppermute | solution.py:548
  18.8 2.1 %collective-permute-start.10 = (f32[8,384]{1,0:T(8,128)S(1)}, f32[8,384]{1,0:T(8,128)S(1)}, u32[]{:S(2)}, u32[]{:S(2)}) collective-permute-start(f32[8,384]{1,0:T(8,128)S(1)} %shard_map.91.note), channel_id=1, source_target_pairs={{0,8},{2,12},{4,10},{6,14},{8,0},{10,4},{12,2},{14,6},{16,24},{18,... | collective-permute-start | bytes 36872 | tf_op jit(solution)/shard_map/ppermute | solution.py:548
  21.1 1.9 %collective-permute-start.12 = (bf16[3,192,128]{2,1,0:T(8,128)(2,1)S(1)}, bf16[3,192,128]{2,1,0:T(8,128)(2,1)S(1)}, u32[]{:S(2)}, u32[]{:S(2)}) collective-permute-start(bf16[3,192,128]{2,1,0:T(8,128)(2,1)S(1)} %get-tuple-element.73), channel_id=1, source_target_pairs={{0,8},{8,0},{16,24},{24,16},{1,9},{9,1},{17,25},{25,17},{2,10},{10... | collective-permute-start | bytes 442376 | tf_op jit(solution)/shard_map/ppermute | solution.py:551

commit v7 on v6

--- a/solution.py
+++ b/solution.py
@@ -198,7 +198,7 @@
     return jnp.sum(total, axis=0, keepdims=True)
 
 
-def early_kernel(tok, scale, q_all, g_all, table, s_own, one_ref, two_ref, s_ref, d_ref, part_ref):
+def early_kernel(tok, scale, q_all, g_all, table, s_own, one_ref, two_ref, _, s_ref, d_ref, part_ref):
     qg = (q_all, g_all)
     for i, source in enumerate((one_ref, two_ref)):
         rows = rows_at(i, tok)
@@ -589,8 +589,8 @@
     )(*qg, *foreign)
     queries_in = [exchange(message, None, which) for which in (1, 0)]
     s_early, d_early, part = call(
-        functools.partial(early_kernel, tok, scale), [square(2), square(2), note_shape], [VMEM] * 6
-    )(*qg, table, s_own, *early)
+        functools.partial(early_kernel, tok, scale), [square(2), square(2), note_shape], [VMEM] * 7
+    )(*qg, table, s_own, *early, message)
     s_late, s_far, *sent = call(
         functools.partial(score_kernel, tok, chips, heights, sides, scale),
         [square(2), far_square()] + [note_shape] * sides,

time: 23.9 us -> 24.2 us (1.013)
  waiting for transfers between devices: 2.23 us -> 2.54 us
    ppermute x11, waiting for transfers between devices: 1.68 us -> 1.98 us  [exchange(): return lax.ppermute(block, ('tm', 'height'), pairs)]
where the time goes in v7:
time: 24.2 us; the launch traced here: 24 us
  starting transfers between devices  14 us (58%)
  Pallas kernels  6.74 us (28%)
  waiting for transfers between devices  2.54 us (10%)
  between operations  0.76 us (3%)
    ppermute x11, starting transfers between devices, exchange(): return lax.ppermute(block, ('tm', 'height'), pairs)  12.8 us
    ppermute x11, waiting for transfers between devices, exchange(): return lax.ppermute(block, ('tm', 'height'), pairs)  1.98 us
    pallas_call x1, Pallas kernels, body(): call(functools.partial(middle_kernel, tok, sides, scale), [square(2, bf16...  1.26 us
    ppermute x2, starting transfers between devices, swap_cores(): return lax.ppermute(block, 'tm', [(t, t ^ 1) for t in range(times)])  1.19 us
    pallas_call x1, Pallas kernels, body(): call(functools.partial(pack_kernel, tok), [((2 * tok + extra, width), bf1...  1.13 us
    pallas_call x1, Pallas kernels, body(): call(final_kernel, [(queries.shape, bf16)] * 3, [VMEM] * 3)  0.74 us
    ppermute x2, waiting for transfers between devices, swap_cores(): return lax.ppermute(block, 'tm', [(t, t ^ 1) for t in range(times)])  0.56 us
    pallas_call x1, Pallas kernels, body(): call(functools.partial(score_kernel, tok, chips, heights, sides, scale),...  0.53 us
  transfers between devices with their start and end apart: 13, of which 5 were waited for; matrix products, arithmetic and copies ran while one was open for 0% of the time, Pallas kernels for 20%

profile of v7, /device:TPU:0, one launch (start us, length us, event | category | flops | bytes accessed | tf_op | source)
XLA Modules:
  0.0 24.0 jit_solution(2722688646976258814)
XLA Ops:
  0.6 1.1 %shard_map.85 = (bf16[448,128]{1,0:T(8,128)(2,1)S(1)}, bf16[592,128]{1,0:T(8,128)(2,1)S(1)}, bf16[976,128]{1,0:T(8,128)(2,1)S(1)}) custom-call(bf16[1,1,2,1,192,128]{5,4,3,2,1,0:T(8,128)(2,1)} %k_ref.1, bf16[1,1,2,1,192,128]{5,4,3,2,1,0:T(8,128)(2,1)} %v_ref.1, bf16[1,1,2,1,192,128]{5,4,3,2,1,0:T(8,128)(2,1)} %q_ref.1, ...), custom_call_target="tpu_custom_call" | custom-call | tf_op jit(solution)/shard_map/pallas_call | solution.py:556
  1.8 0.5 %collective-permute-start = (bf16[976,128]{1,0:T(8,128)(2,1)S(1)}, bf16[976,128]{1,0:T(8,128)(2,1)S(1)}, u32[]{:S(2)}, u32[]{:S(2)}) collective-permute-start(bf16[976,128]{1,0:T(8,128)(2,1)S(1)} %get-tuple-element.41), channel_id=1, source_target_pairs={{0,8},{8,0},{16,24},{24,16},{1,9},{9,1},{17,25},{25,17},{2,10},{10... | collective-permute-start | bytes 749576 | tf_op jit(solution)/shard_map/ppermute | solution.py:551
  2.4 3.9 %collective-permute-start.2 = (bf16[448,128]{1,0:T(8,128)(2,1)S(1)}, bf16[448,128]{1,0:T(8,128)(2,1)S(1)}, u32[]{:S(2)}, u32[]{:S(2)}) collective-permute-start(bf16[448,128]{1,0:T(8,128)(2,1)S(1)} %get-tuple-element.39.kv_ref.refs_1_.refs_0_), channel_id=1, source_target_pairs={{0,10},{2,8},{4,14},{6,12},{8,2},{10,0},{12,6},{14,4},{16,26},{18,... | collective-permute-start | bytes 344072 | tf_op jit(solution)/shard_map/ppermute | solution.py:548
  6.2 0.2 shard_map.86
  6.4 1.6 %collective-permute-start.3 = (bf16[432,128]{1,0:T(8,128)(2,1)S(1)}, bf16[432,128]{1,0:T(8,128)(2,1)S(1)}, u32[]{:S(2)}, u32[]{:S(2)}) collective-permute-start(bf16[432,128]{1,0:T(8,128)(2,1)S(1)} %get-tuple-element.48), channel_id=1, source_target_pairs={{0,24},{2,26},{4,28},{6,30},{8,16},{10,18},{12,20},{14,22},{16,8},... | collective-permute-start | bytes 331784 | tf_op jit(solution)/shard_map/ppermute | solution.py:548
  8.1 1.6 %collective-permute-start.5 = (bf16[416,128]{1,0:T(8,128)(2,1)S(1)}, bf16[416,128]{1,0:T(8,128)(2,1)S(1)}, u32[]{:S(2)}, u32[]{:S(2)}) collective-permute-start(bf16[416,128]{1,0:T(8,128)(2,1)S(1)} %get-tuple-element.42.par_kv_ref.refs_2_.refs_1_), channel_id=1, source_target_pairs={{0,10},{2,8},{4,14},{6,12},{8,2},{10,0},{12,6},{14,4},{16,26},{18,... | collective-permute-start | bytes 319496 | tf_op jit(solution)/shard_map/ppermute | solution.py:548
  9.7 0.4 %shard_map.87 = (bf16[384,128]{1,0:T(8,128)(2,1)S(1)}, bf16[384,128]{1,0:T(8,128)(2,1)S(1)}, f32[8,384]{1,0:T(8,128)S(1)}, f32[384,384]{1,0:T(8,128)S(1)}, f32[384,384]{1,0:T(8,128)S(1)}) custom-call(bf16[448,128]{1,0:T(8,128)(2,1)S(1)} %get-tuple-element.39.kv_ref.refs_1_.refs_0_, bf16[416,128]{1,0:T(8,128)(2,1)S(1)} %get-tuple-element.42.par_kv_ref.refs_2_.refs_1_, ...), custom_call_target="tpu_custom_call" | custom-call | tf_op jit(solution)/shard_map/pallas_call | solution.py:579
  10.1 1.2 %collective-permute-done.3.refs_0_.refs_6_.refs_1_ = bf16[432,128]{1,0:T(8,128)(2,1)S(1)} collective-permute-done((bf16[432,128]{1,0:T(8,128)(2,1)S(1)}, bf16[432,128]{1,0:T(8,128)(2,1)S(1)}, u32[]{:S(2)}, u32[]{:S(2)}) %collective-permute-start.3) | collective-permute-done | bytes 110624 | tf_op jit(solution)/shard_map/ppermute | solution.py:548
  11.3 0.7 %collective-permute-start.7 = (bf16[1168,128]{1,0:T(8,128)(2,1)S(1)}, bf16[1168,128]{1,0:T(8,128)(2,1)S(1)}, u32[]{:S(2)}, u32[]{:S(2)}) collective-permute-start(bf16[1168,128]{1,0:T(8,128)(2,1)S(1)} %shard_map.88._), channel_id=1, source_target_pairs={{0,10},{2,8},{4,14},{6,12},{8,2},{10,0},{12,6},{14,4},{16,26},{18,... | collective-permute-start | bytes 897032 | tf_op jit(solution)/shard_map/ppermute | solution.py:548
  12.2 0.5 %shard_map.89 = (f32[384,384]{1,0:T(8,128)S(1)}, f32[384,384]{1,0:T(8,128)S(1)}, f32[8,384]{1,0:T(8,128)S(1)}) custom-call(bf16[384,128]{1,0:T(8,128)(2,1)S(1)} %get-tuple-element.43.q_all, bf16[384,128]{1,0:T(8,128)(2,1)S(1)} %get-tuple-element.44.g_all, f32[8,384]{1,0:T(8,128)S(1)} %get-tuple-element.45.table, f32[384,384]{1,0:T(8,128)S(1)} %get-tuple-element.46.s_own, ...), custom_call_target="tpu_custom_call" | custom-call | tf_op jit(solution)/shard_map/pallas_call | solution.py:591
  12.7 0.2 collective-permute-done.5.refs_5_.refs_4_.extras
  12.8 0.5 %shard_map.90 = (f32[384,384]{1,0:T(8,128)S(1)}, f32[576,256]{1,0:T(8,128)S(1)}, f32[8,384]{1,0:T(8,128)S(1)}) custom-call(bf16[384,128]{1,0:T(8,128)(2,1)S(1)} %get-tuple-element.43.q_all, bf16[384,128]{1,0:T(8,128)(2,1)S(1)} %get-tuple-element.44.g_all, f32[8,384]{1,0:T(8,128)S(1)} %get-tuple-element.45.table, f32[8,384]{1,0:T(8,128)S(1)} %get-tuple-element.51.part, ...), custom_call_target="tpu_custom_call" | custom-call | tf_op jit(solution)/shard_map/pallas_call | solution.py:594
  13.4 1.4 %collective-permute-start.6 = (f32[8,384]{1,0:T(8,128)S(1)}, f32[8,384]{1,0:T(8,128)S(1)}, u32[]{:S(2)}, u32[]{:S(2)}) collective-permute-start(f32[8,384]{1,0:T(8,128)S(1)} %get-tuple-element.54.refs_7_.refs_0_), channel_id=1, source_target_pairs={{0,24},{2,26},{4,28},{6,30},{8,16},{10,18},{12,20},{14,22},{16,8},... | collective-permute-start | bytes 36872 | tf_op jit(solution)/shard_map/ppermute | solution.py:548
  14.7 1.3 %shard_map.91 = (bf16[384,384]{1,0:T(8,128)(2,1)S(1)}, bf16[384,384]{1,0:T(8,128)(2,1)S(1)}, bf16[192,256]{1,0:T(8,128)(2,1)S(1)}, bf16[192,256]{1,0:T(8,128)(2,...) custom-call(bf16[384,128]{1,0:T(8,128)(2,1)S(1)} %get-tuple-element.43.q_all, ...), custom_call_target="tpu_custom_call" | custom-call | flops 20000000000 | tf_op jit(solution)/shard_map/pallas_call | solution.py:601
  16.0 0.5 %collective-permute-start.11 = (bf16[192,128]{1,0:T(8,128)(2,1)S(1)}, bf16[192,128]{1,0:T(8,128)(2,1)S(1)}, u32[]{:S(2)}, u32[]{:S(2)}) collective-permute-start(bf16[192,128]{1,0:T(8,128)(2,1)S(1)} %get-tuple-element.72), channel_id=1, source_target_pairs={{0,24},{2,26},{4,28},{6,30},{8,16},{10,18},{12,20},{14,22},{16,8},... | collective-permute-start | bytes 147464 | tf_op jit(solution)/shard_map/ppermute | solution.py:548
  16.6 2.8 %collective-permute-start.8 = (f32[8,384]{1,0:T(8,128)S(1)}, f32[8,384]{1,0:T(8,128)S(1)}, u32[]{:S(2)}, u32[]{:S(2)}) collective-permute-start(f32[8,384]{1,0:T(8,128)S(1)} %shard_map.92.note), channel_id=1, source_target_pairs={{0,10},{2,8},{4,14},{6,12},{8,2},{10,0},{12,6},{14,4},{16,26},{18,... | collective-permute-start | bytes 36872 | tf_op jit(solution)/shard_map/ppermute | solution.py:548
  19.3 0.5 %shard_map.93 = (f32[2,384,128]{2,1,0:T(8,128)S(1)}, f32[384,128]{1,0:T(8,128)S(1)}) custom-call(bf16[384,128]{1,0:T(8,128)(2,1)S(1)} %get-tuple-element.43.q_all, bf16[384,128]{1,0:T(8,128)(2,1)S(1)} %get-tuple-element.44.g_all, bf16[384,384]{1,0:T(8,128)(2,1)S(1)} %get-tuple-element.55.e_ref, bf16[384,384]{1,0:T(8,128)(2,1)S(1)} %get-tuple-element.56.ds_ref, ...), custom_call_target="tpu_custom_call" | custom-call | tf_op jit(solution)/shard_map/pallas_call | solution.py:620
  19.9 0.5 %shard_map.94 = (bf16[384,384]{1,0:T(8,128)(2,1)S(1)}, bf16[384,384]{1,0:T(8,128)(2,1)S(1)}, bf16[192,256]{1,0:T(8,128)(2,1)S(1)}, bf16[192,256]{1,0:T(8,128)(2,1)S(1)}, f32[8,384]{1,0:T(8,128)S(1)}) custom-call(bf16[448,128]{1,0:T(8,128)(2,1)S(1)} %get-tuple-element.39.kv_ref.refs_1_.refs_0_, ...), custom_call_target="tpu_custom_call" | custom-call | flops 20000000000 | tf_op jit(solution)/shard_map/pallas_call | solution.py:613
  20.4 0.5 %collective-permute-done.8.note.refs_1_ = f32[8,384]{1,0:T(8,128)S(1)} collective-permute-done((f32[8,384]{1,0:T(8,128)S(1)}, f32[8,384]{1,0:T(8,128)S(1)}, u32[]{:S(2)}, u32[]{:S(2)}) %collective-permute-start.8) | collective-permute-done | bytes 12320 | tf_op jit(solution)/shard_map/ppermute | solution.py:548
  20.9 0.4 %shard_map.95.outs_0_.own_ref = f32[2,192,128]{2,1,0:T(8,128)S(1)} custom-call(f32[2,384,128]{2,1,0:T(8,128)S(1)} %get-tuple-element.60.own_ref, bf16[1168,128]{1,0:T(8,128)(2,1)S(1)} %collective-permute-done.7.message.refs_0_, f32[8,384]{1,0:T(8,128)S(1)} %collective-permute-done.8.note.refs_1_, bf16[384,384]{1,0:T(8,128)(2,1)S(1)} %get-tuple-element.61.refs_0_.refs_2_, ...), custom_call_target="tpu_custom_call" | custom-call | tf_op jit(solution)/shard_map/pallas_call | solution.py:627
  21.6 0.7 %collective-permute-start.12 = (bf16[3,192,128]{2,1,0:T(8,128)(2,1)S(1)}, bf16[3,192,128]{2,1,0:T(8,128)(2,1)S(1)}, u32[]{:S(2)}, u32[]{:S(2)}) collective-permute-start(bf16[3,192,128]{2,1,0:T(8,128)(2,1)S(1)} %get-tuple-element.73), channel_id=1, source_target_pairs={{0,8},{8,0},{16,24},{24,16},{1,9},{9,1},{17,25},{25,17},{2,10},{10... | collective-permute-start | bytes 442376 | tf_op jit(solution)/shard_map/ppermute | solution.py:551
  22.2 0.4 %shard_map.97.mine_ref = bf16[2,192,128]{2,1,0:T(8,128)(2,1)S(1)} custom-call(f32[2,384,128]{2,1,0:T(8,128)S(1)} %get-tuple-element.60.own_ref, bf16[1168,128]{1,0:T(8,128)(2,1)S(1)} %collective-permute-done.7.message.refs_0_, f32[8,384]{1,0:T(8,128)S(1)} %collective-permute-done.8.note.refs_1_, bf16[384,384]{1,0:T(8,128)(2,1)S(1)} %get-tuple-element.61.refs_0_.refs_2_, ...), custom_call_target="tpu_custom_call" | custom-call | flops 20000000000 | tf_op jit(solution)/shard_map/pallas_call | solution.py:637
  22.7 0.6 %collective-permute-done.12.swap_ref = bf16[3,192,128]{2,1,0:T(8,128)(2,1)S(1)} collective-permute-done((bf16[3,192,128]{2,1,0:T(8,128)(2,1)S(1)}, bf16[3,192,128]{2,1,0:T(8,128)(2,1)S(1)}, u32[]{:S(2)}, u32[]{:S(2)}) %collective-permute-start.12) | collective-permute-done | bytes 147488 | tf_op jit(solution)/shard_map/ppermute | solution.py:551
  23.2 0.7 %shard_map.99 = (bf16[1,1,2,1,192,128]{5,4,3,2,1,0:T(8,128)(2,1)}, bf16[1,1,2,1,192,128]{5,4,3,2,1,0:T(8,128)(2,1)}, bf16[1,1,2,1,192,128]{5,4,3,2,1,0:T(8,128)(2,1)}) custom-call(bf16[2,192,128]{2,1,0:T(8,128)(2,1)S(1)} %shard_map.97.mine_ref, bf16[3,192,128]{2,1,0:T(8,128)(2,1)S(1)} %collective-permute-done.12.swap_ref, ...), custom_call_target="tpu_custom_call" | custom-call | tf_op jit(solution)/shard_map/pallas_call | solution.py:644
  (17 shorter events, 0.7 us)
Async XLA Ops:
  1.8 4.5 %collective-permute-start = (bf16[976,128]{1,0:T(8,128)(2,1)S(1)}, bf16[976,128]{1,0:T(8,128)(2,1)S(1)}, u32[]{:S(2)}, u32[]{:S(2)}) collective-permute-start(bf16[976,128]{1,0:T(8,128)(2,1)S(1)} %get-tuple-element.41), channel_id=1, source_target_pairs={{0,8},{8,0},{16,24},{24,16},{1,9},{9,1},{17,25},{25,17},{2,10},{10... | collective-permute-start | bytes 749576 | tf_op jit(solution)/shard_map/ppermute | solution.py:551
  2.3 9.7 %collective-permute-start.1 = (bf16[448,128]{1,0:T(8,128)(2,1)S(1)}, bf16[448,128]{1,0:T(8,128)(2,1)S(1)}, u32[]{:S(2)}, u32[]{:S(2)}) collective-permute-start(bf16[448,128]{1,0:T(8,128)(2,1)S(1)} %get-tuple-element.39.kv_ref.refs_1_.refs_0_), channel_id=1, source_target_pairs={{0,8},{2,12},{4,10},{6,14},{8,0},{10,4},{12,2},{14,6},{16,24},{18,... | collective-permute-start | bytes 344072 | tf_op jit(solution)/shard_map/ppermute | solution.py:548
  2.4 9.8 %collective-permute-start.2 = (bf16[448,128]{1,0:T(8,128)(2,1)S(1)}, bf16[448,128]{1,0:T(8,128)(2,1)S(1)}, u32[]{:S(2)}, u32[]{:S(2)}) collective-permute-start(bf16[448,128]{1,0:T(8,128)(2,1)S(1)} %get-tuple-element.39.kv_ref.refs_1_.refs_0_), channel_id=1, source_target_pairs={{0,10},{2,8},{4,14},{6,12},{8,2},{10,0},{12,6},{14,4},{16,26},{18,... | collective-permute-start | bytes 344072 | tf_op jit(solution)/shard_map/ppermute | solution.py:548
  6.4 4.9 %collective-permute-start.3 = (bf16[432,128]{1,0:T(8,128)(2,1)S(1)}, bf16[432,128]{1,0:T(8,128)(2,1)S(1)}, u32[]{:S(2)}, u32[]{:S(2)}) collective-permute-start(bf16[432,128]{1,0:T(8,128)(2,1)S(1)} %get-tuple-element.48), channel_id=1, source_target_pairs={{0,24},{2,26},{4,28},{6,30},{8,16},{10,18},{12,20},{14,22},{16,8},... | collective-permute-start | bytes 331784 | tf_op jit(solution)/shard_map/ppermute | solution.py:548
  8.1 4.6 %collective-permute-start.4 = (bf16[416,128]{1,0:T(8,128)(2,1)S(1)}, bf16[416,128]{1,0:T(8,128)(2,1)S(1)}, u32[]{:S(2)}, u32[]{:S(2)}) collective-permute-start(bf16[416,128]{1,0:T(8,128)(2,1)S(1)} %get-tuple-element.42.par_kv_ref.refs_2_.refs_1_), channel_id=1, source_target_pairs={{0,8},{2,12},{4,10},{6,14},{8,0},{10,4},{12,2},{14,6},{16,24},{18,... | collective-permute-start | bytes 319496 | tf_op jit(solution)/shard_map/ppermute | solution.py:548
  8.1 4.7 %collective-permute-start.5 = (bf16[416,128]{1,0:T(8,128)(2,1)S(1)}, bf16[416,128]{1,0:T(8,128)(2,1)S(1)}, u32[]{:S(2)}, u32[]{:S(2)}) collective-permute-start(bf16[416,128]{1,0:T(8,128)(2,1)S(1)} %get-tuple-element.42.par_kv_ref.refs_2_.refs_1_), channel_id=1, source_target_pairs={{0,10},{2,8},{4,14},{6,12},{8,2},{10,0},{12,6},{14,4},{16,26},{18,... | collective-permute-start | bytes 319496 | tf_op jit(solution)/shard_map/ppermute | solution.py:548
  11.3 8.6 %collective-permute-start.7 = (bf16[1168,128]{1,0:T(8,128)(2,1)S(1)}, bf16[1168,128]{1,0:T(8,128)(2,1)S(1)}, u32[]{:S(2)}, u32[]{:S(2)}) collective-permute-start(bf16[1168,128]{1,0:T(8,128)(2,1)S(1)} %shard_map.88._), channel_id=1, source_target_pairs={{0,10},{2,8},{4,14},{6,12},{8,2},{10,0},{12,6},{14,4},{16,26},{18,... | collective-permute-start | bytes 897032 | tf_op jit(solution)/shard_map/ppermute | solution.py:548
  12.0 9.4 %collective-permute-start.9 = (bf16[1168,128]{1,0:T(8,128)(2,1)S(1)}, bf16[1168,128]{1,0:T(8,128)(2,1)S(1)}, u32[]{:S(2)}, u32[]{:S(2)}) collective-permute-start(bf16[1168,128]{1,0:T(8,128)(2,1)S(1)} %shard_map.88._), channel_id=1, source_target_pairs={{0,8},{2,12},{4,10},{6,14},{8,0},{10,4},{12,2},{14,6},{16,24},{18,... | collective-permute-start | bytes 897032 | tf_op jit(solution)/shard_map/ppermute | solution.py:548
  13.4 3.2 %collective-permute-start.6 = (f32[8,384]{1,0:T(8,128)S(1)}, f32[8,384]{1,0:T(8,128)S(1)}, u32[]{:S(2)}, u32[]{:S(2)}) collective-permute-start(f32[8,384]{1,0:T(8,128)S(1)} %get-tuple-element.54.refs_7_.refs_0_), channel_id=1, source_target_pairs={{0,24},{2,26},{4,28},{6,30},{8,16},{10,18},{12,20},{14,22},{16,8},... | collective-permute-start | bytes 36872 | tf_op jit(solution)/shard_map/ppermute | solution.py:548
  16.0 5.4 %collective-permute-start.11 = (bf16[192,128]{1,0:T(8,128)(2,1)S(1)}, bf16[192,128]{1,0:T(8,128)(2,1)S(1)}, u32[]{:S(2)}, u32[]{:S(2)}) collective-permute-start(bf16[192,128]{1,0:T(8,128)(2,1)S(1)} %get-tuple-element.72), channel_id=1, source_target_pairs={{0,24},{2,26},{4,28},{6,30},{8,16},{10,18},{12,20},{14,22},{16,8},... | collective-permute-start | bytes 147464 | tf_op jit(solution)/shard_map/ppermute | solution.py:548
  16.6 4.3 %collective-permute-start.8 = (f32[8,384]{1,0:T(8,128)S(1)}, f32[8,384]{1,0:T(8,128)S(1)}, u32[]{:S(2)}, u32[]{:S(2)}) collective-permute-start(f32[8,384]{1,0:T(8,128)S(1)} %shard_map.92.note), channel_id=1, source_target_pairs={{0,10},{2,8},{4,14},{6,12},{8,2},{10,0},{12,6},{14,4},{16,26},{18,... | collective-permute-start | bytes 36872 | tf_op jit(solution)/shard_map/ppermute | solution.py:548
  19.3 2.1 %collective-permute-start.10 = (f32[8,384]{1,0:T(8,128)S(1)}, f32[8,384]{1,0:T(8,128)S(1)}, u32[]{:S(2)}, u32[]{:S(2)}) collective-permute-start(f32[8,384]{1,0:T(8,128)S(1)} %shard_map.92.note), channel_id=1, source_target_pairs={{0,8},{2,12},{4,10},{6,14},{8,0},{10,4},{12,2},{14,6},{16,24},{18,... | collective-permute-start | bytes 36872 | tf_op jit(solution)/shard_map/ppermute | solution.py:548
  21.6 1.7 %collective-permute-start.12 = (bf16[3,192,128]{2,1,0:T(8,128)(2,1)S(1)}, bf16[3,192,128]{2,1,0:T(8,128)(2,1)S(1)}, u32[]{:S(2)}, u32[]{:S(2)}) collective-permute-start(bf16[3,192,128]{2,1,0:T(8,128)(2,1)S(1)} %get-tuple-element.73), channel_id=1, source_target_pairs={{0,8},{8,0},{16,24},{24,16},{1,9},{9,1},{17,25},{25,17},{2,10},{10... | collective-permute-start | bytes 442376 | tf_op jit(solution)/shard_map/ppermute | solution.py:551

commit v8 on v6

--- a/solution.py
+++ b/solution.py
@@ -551,7 +551,7 @@
         return lax.ppermute(block, "tm", [(t, t ^ 1) for t in range(times)])
 
     line_shape, tile_shape = ((2, 2 * tok, width), bf16), ((2, tok, width), bf16)
-    extra = 64
+    extra = 56
     arguments = (keys, values, queries, grad_out, attn_out, window_mask)
     kv, rest, other = call(
         functools.partial(pack_kernel, tok),

time: 23.9 us -> 23.9 us (level)
  no operation moved by 1% of the time
where the time goes in v8:
time: 23.9 us; the launch traced here: 23.7 us
  starting transfers between devices  13.9 us (58%)
  Pallas kernels  6.74 us (28%)
  waiting for transfers between devices  2.28 us (10%)
  between operations  0.77 us (3%)
    ppermute x11, starting transfers between devices, exchange(): return lax.ppermute(block, ('tm', 'height'), pairs)  12.5 us
    ppermute x11, waiting for transfers between devices, exchange(): return lax.ppermute(block, ('tm', 'height'), pairs)  1.73 us
    ppermute x2, starting transfers between devices, swap_cores(): return lax.ppermute(block, 'tm', [(t, t ^ 1) for t in range(times)])  1.38 us
    pallas_call x1, Pallas kernels, body(): call(functools.partial(middle_kernel, tok, sides, scale), [square(2, bf16...  1.24 us
    pallas_call x1, Pallas kernels, body(): call(functools.partial(pack_kernel, tok), [((2 * tok + extra, width), bf1...  1.13 us
    pallas_call x1, Pallas kernels, body(): call(final_kernel, [(queries.shape, bf16)] * 3, [VMEM] * 3)  0.74 us
    ppermute x2, waiting for transfers between devices, swap_cores(): return lax.ppermute(block, 'tm', [(t, t ^ 1) for t in range(times)])  0.56 us
    pallas_call x1, Pallas kernels, body(): call(functools.partial(score_kernel, tok, chips, heights, sides, scale),...  0.53 us
  transfers between devices with their start and end apart: 13, of which 5 were waited for; matrix products, arithmetic and copies ran while one was open for 0% of the time, Pallas kernels for 20%

profile of v8, /device:TPU:0, one launch (start us, length us, event | category | flops | bytes accessed | tf_op | source)
XLA Modules:
  0.0 23.7 jit_solution(14204923573530408188)
XLA Ops:
  0.6 1.1 %shard_map.85 = (bf16[440,128]{1,0:T(8,128)(2,1)S(1)}, bf16[592,128]{1,0:T(8,128)(2,1)S(1)}, bf16[976,128]{1,0:T(8,128)(2,1)S(1)}) custom-call(bf16[1,1,2,1,192,128]{5,4,3,2,1,0:T(8,128)(2,1)} %k_ref.1, bf16[1,1,2,1,192,128]{5,4,3,2,1,0:T(8,128)(2,1)} %v_ref.1, bf16[1,1,2,1,192,128]{5,4,3,2,1,0:T(8,128)(2,1)} %q_ref.1, ...), custom_call_target="tpu_custom_call" | custom-call | tf_op jit(solution)/shard_map/pallas_call | solution.py:556
  1.8 0.5 %collective-permute-start = (bf16[976,128]{1,0:T(8,128)(2,1)S(1)}, bf16[976,128]{1,0:T(8,128)(2,1)S(1)}, u32[]{:S(2)}, u32[]{:S(2)}) collective-permute-start(bf16[976,128]{1,0:T(8,128)(2,1)S(1)} %get-tuple-element.41), channel_id=1, source_target_pairs={{0,8},{8,0},{16,24},{24,16},{1,9},{9,1},{17,25},{25,17},{2,10},{10... | collective-permute-start | bytes 749576 | tf_op jit(solution)/shard_map/ppermute | solution.py:551
  2.4 3.9 %collective-permute-start.2 = (bf16[440,128]{1,0:T(8,128)(2,1)S(1)}, bf16[440,128]{1,0:T(8,128)(2,1)S(1)}, u32[]{:S(2)}, u32[]{:S(2)}) collective-permute-start(bf16[440,128]{1,0:T(8,128)(2,1)S(1)} %get-tuple-element.39.kv_ref.refs_1_.refs_0_), channel_id=1, source_target_pairs={{0,10},{2,8},{4,14},{6,12},{8,2},{10,0},{12,6},{14,4},{16,26},{18,... | collective-permute-start | bytes 337928 | tf_op jit(solution)/shard_map/ppermute | solution.py:548
  6.2 0.2 shard_map.86
  6.4 1.6 %collective-permute-start.3 = (bf16[432,128]{1,0:T(8,128)(2,1)S(1)}, bf16[432,128]{1,0:T(8,128)(2,1)S(1)}, u32[]{:S(2)}, u32[]{:S(2)}) collective-permute-start(bf16[432,128]{1,0:T(8,128)(2,1)S(1)} %get-tuple-element.51), channel_id=1, source_target_pairs={{0,24},{2,26},{4,28},{6,30},{8,16},{10,18},{12,20},{14,22},{16,8},... | collective-permute-start | bytes 331784 | tf_op jit(solution)/shard_map/ppermute | solution.py:548
  8.1 1.6 %collective-permute-start.5 = (bf16[416,128]{1,0:T(8,128)(2,1)S(1)}, bf16[416,128]{1,0:T(8,128)(2,1)S(1)}, u32[]{:S(2)}, u32[]{:S(2)}) collective-permute-start(bf16[416,128]{1,0:T(8,128)(2,1)S(1)} %get-tuple-element.42.par_kv_ref.refs_2_.refs_1_), channel_id=1, source_target_pairs={{0,10},{2,8},{4,14},{6,12},{8,2},{10,0},{12,6},{14,4},{16,26},{18,... | collective-permute-start | bytes 319496 | tf_op jit(solution)/shard_map/ppermute | solution.py:548
  9.7 0.4 %shard_map.87 = (bf16[384,128]{1,0:T(8,128)(2,1)S(1)}, bf16[384,128]{1,0:T(8,128)(2,1)S(1)}, f32[8,384]{1,0:T(8,128)S(1)}, f32[384,384]{1,0:T(8,128)S(1)}, f32[384,384]{1,0:T(8,128)S(1)}) custom-call(bf16[440,128]{1,0:T(8,128)(2,1)S(1)} %get-tuple-element.39.kv_ref.refs_1_.refs_0_, bf16[416,128]{1,0:T(8,128)(2,1)S(1)} %get-tuple-element.42.par_kv_ref.refs_2_.refs_1_, ...), custom_call_target="tpu_custom_call" | custom-call | tf_op jit(solution)/shard_map/pallas_call | solution.py:579
  10.1 0.5 %shard_map.88 = (f32[384,384]{1,0:T(8,128)S(1)}, f32[384,384]{1,0:T(8,128)S(1)}, f32[8,384]{1,0:T(8,128)S(1)}) custom-call(bf16[384,128]{1,0:T(8,128)(2,1)S(1)} %get-tuple-element.43.q_all, bf16[384,128]{1,0:T(8,128)(2,1)S(1)} %get-tuple-element.44.g_all, f32[8,384]{1,0:T(8,128)S(1)} %get-tuple-element.45.table, f32[384,384]{1,0:T(8,128)S(1)} %get-tuple-element.46.s_own, ...), custom_call_target="tpu_custom_call" | custom-call | tf_op jit(solution)/shard_map/pallas_call | solution.py:591
  10.6 0.6 %collective-permute-done.3.refs_0_.refs_6_.refs_1_ = bf16[432,128]{1,0:T(8,128)(2,1)S(1)} collective-permute-done((bf16[432,128]{1,0:T(8,128)(2,1)S(1)}, bf16[432,128]{1,0:T(8,128)(2,1)S(1)}, u32[]{:S(2)}, u32[]{:S(2)}) %collective-permute-start.3) | collective-permute-done | bytes 110624 | tf_op jit(solution)/shard_map/ppermute | solution.py:548
  11.3 1.0 %collective-permute-start.7 = (bf16[1168,128]{1,0:T(8,128)(2,1)S(1)}, bf16[1168,128]{1,0:T(8,128)(2,1)S(1)}, u32[]{:S(2)}, u32[]{:S(2)}) collective-permute-start(bf16[1168,128]{1,0:T(8,128)(2,1)S(1)} %shard_map.93), channel_id=1, source_target_pairs={{0,10},{2,8},{4,14},{6,12},{8,2},{10,0},{12,6},{14,4},{16,26},{18,... | collective-permute-start | bytes 897032 | tf_op jit(solution)/shard_map/ppermute | solution.py:548
  12.4 0.4 %collective-permute-done.5.refs_5_.refs_4_.extras = bf16[416,128]{1,0:T(8,128)(2,1)S(1)} collective-permute-done((bf16[416,128]{1,0:T(8,128)(2,1)S(1)}, bf16[416,128]{1,0:T(8,128)(2,1)S(1)}, u32[]{:S(2)}, u32[]{:S(2)}) %collective-permute-start.5) | collective-permute-done | bytes 106528 | tf_op jit(solution)/shard_map/ppermute | solution.py:548
  12.8 0.5 %shard_map.89 = (f32[384,384]{1,0:T(8,128)S(1)}, f32[576,256]{1,0:T(8,128)S(1)}, f32[8,384]{1,0:T(8,128)S(1)}) custom-call(bf16[384,128]{1,0:T(8,128)(2,1)S(1)} %get-tuple-element.43.q_all, bf16[384,128]{1,0:T(8,128)(2,1)S(1)} %get-tuple-element.44.g_all, f32[8,384]{1,0:T(8,128)S(1)} %get-tuple-element.45.table, f32[8,384]{1,0:T(8,128)S(1)} %get-tuple-element.50.part, ...), custom_call_target="tpu_custom_call" | custom-call | tf_op jit(solution)/shard_map/pallas_call | solution.py:594
  13.4 1.4 %collective-permute-start.6 = (f32[8,384]{1,0:T(8,128)S(1)}, f32[8,384]{1,0:T(8,128)S(1)}, u32[]{:S(2)}, u32[]{:S(2)}) collective-permute-start(f32[8,384]{1,0:T(8,128)S(1)} %get-tuple-element.54.refs_7_.refs_0_), channel_id=1, source_target_pairs={{0,24},{2,26},{4,28},{6,30},{8,16},{10,18},{12,20},{14,22},{16,8},... | collective-permute-start | bytes 36872 | tf_op jit(solution)/shard_map/ppermute | solution.py:548
  14.8 1.2 %shard_map.90 = (bf16[384,384]{1,0:T(8,128)(2,1)S(1)}, bf16[384,384]{1,0:T(8,128)(2,1)S(1)}, bf16[192,256]{1,0:T(8,128)(2,1)S(1)}, bf16[192,256]{1,0:T(8,128)(2,...) custom-call(bf16[384,128]{1,0:T(8,128)(2,1)S(1)} %get-tuple-element.43.q_all, ...), custom_call_target="tpu_custom_call" | custom-call | flops 20000000000 | tf_op jit(solution)/shard_map/pallas_call | solution.py:601
  16.0 0.5 %collective-permute-start.11 = (bf16[192,128]{1,0:T(8,128)(2,1)S(1)}, bf16[192,128]{1,0:T(8,128)(2,1)S(1)}, u32[]{:S(2)}, u32[]{:S(2)}) collective-permute-start(bf16[192,128]{1,0:T(8,128)(2,1)S(1)} %get-tuple-element.72), channel_id=1, source_target_pairs={{0,24},{2,26},{4,28},{6,30},{8,16},{10,18},{12,20},{14,22},{16,8},... | collective-permute-start | bytes 147464 | tf_op jit(solution)/shard_map/ppermute | solution.py:548
  16.6 2.2 %collective-permute-start.8 = (f32[8,384]{1,0:T(8,128)S(1)}, f32[8,384]{1,0:T(8,128)S(1)}, u32[]{:S(2)}, u32[]{:S(2)}) collective-permute-start(f32[8,384]{1,0:T(8,128)S(1)} %shard_map.91.note), channel_id=1, source_target_pairs={{0,10},{2,8},{4,14},{6,12},{8,2},{10,0},{12,6},{14,4},{16,26},{18,... | collective-permute-start | bytes 36872 | tf_op jit(solution)/shard_map/ppermute | solution.py:548
  18.8 0.5 %shard_map.92 = (f32[2,384,128]{2,1,0:T(8,128)S(1)}, f32[384,128]{1,0:T(8,128)S(1)}) custom-call(bf16[384,128]{1,0:T(8,128)(2,1)S(1)} %get-tuple-element.43.q_all, bf16[384,128]{1,0:T(8,128)(2,1)S(1)} %get-tuple-element.44.g_all, bf16[384,384]{1,0:T(8,128)(2,1)S(1)} %get-tuple-element.55.e_ref, bf16[384,384]{1,0:T(8,128)(2,1)S(1)} %get-tuple-element.56.ds_ref, ...), custom_call_target="tpu_custom_call" | custom-call | tf_op jit(solution)/shard_map/pallas_call | solution.py:620
  19.3 0.6 %collective-permute-done.7.message.refs_0_ = bf16[1168,128]{1,0:T(8,128)(2,1)S(1)} collective-permute-done((bf16[1168,128]{1,0:T(8,128)(2,1)S(1)}, bf16[1168,128]{1,0:T(8,128)(2,1)S(1)}, u32[]{:S(2)}, u32[]{:S(2)}) %collective-permute-start.7) | collective-permute-done | bytes 299040 | tf_op jit(solution)/shard_map/ppermute | solution.py:548
  19.9 0.5 %shard_map.94 = (bf16[384,384]{1,0:T(8,128)(2,1)S(1)}, bf16[384,384]{1,0:T(8,128)(2,1)S(1)}, bf16[192,256]{1,0:T(8,128)(2,1)S(1)}, bf16[192,256]{1,0:T(8,128)(2,1)S(1)}, f32[8,384]{1,0:T(8,128)S(1)}) custom-call(bf16[440,128]{1,0:T(8,128)(2,1)S(1)} %get-tuple-element.39.kv_ref.refs_1_.refs_0_, ...), custom_call_target="tpu_custom_call" | custom-call | flops 20000000000 | tf_op jit(solution)/shard_map/pallas_call | solution.py:613
  20.4 0.4 %shard_map.95.outs_0_.own_ref = f32[2,192,128]{2,1,0:T(8,128)S(1)} custom-call(f32[2,384,128]{2,1,0:T(8,128)S(1)} %get-tuple-element.60.own_ref, bf16[1168,128]{1,0:T(8,128)(2,1)S(1)} %collective-permute-done.7.message.refs_0_, f32[8,384]{1,0:T(8,128)S(1)} %collective-permute-done.8.note.refs_1_, bf16[384,384]{1,0:T(8,128)(2,1)S(1)} %get-tuple-element.61.refs_0_.refs_2_, ...), custom_call_target="tpu_custom_call" | custom-call | tf_op jit(solution)/shard_map/pallas_call | solution.py:627
  21.1 0.9 %collective-permute-start.12 = (bf16[3,192,128]{2,1,0:T(8,128)(2,1)S(1)}, bf16[3,192,128]{2,1,0:T(8,128)(2,1)S(1)}, u32[]{:S(2)}, u32[]{:S(2)}) collective-permute-start(bf16[3,192,128]{2,1,0:T(8,128)(2,1)S(1)} %get-tuple-element.73), channel_id=1, source_target_pairs={{0,8},{8,0},{16,24},{24,16},{1,9},{9,1},{17,25},{25,17},{2,10},{10... | collective-permute-start | bytes 442376 | tf_op jit(solution)/shard_map/ppermute | solution.py:551
  21.9 0.4 %shard_map.97.mine_ref = bf16[2,192,128]{2,1,0:T(8,128)(2,1)S(1)} custom-call(f32[2,384,128]{2,1,0:T(8,128)S(1)} %get-tuple-element.60.own_ref, bf16[1168,128]{1,0:T(8,128)(2,1)S(1)} %collective-permute-done.7.message.refs_0_, f32[8,384]{1,0:T(8,128)S(1)} %collective-permute-done.8.note.refs_1_, bf16[384,384]{1,0:T(8,128)(2,1)S(1)} %get-tuple-element.61.refs_0_.refs_2_, ...), custom_call_target="tpu_custom_call" | custom-call | flops 20000000000 | tf_op jit(solution)/shard_map/pallas_call | solution.py:637
  22.4 0.6 %collective-permute-done.12.swap_ref = bf16[3,192,128]{2,1,0:T(8,128)(2,1)S(1)} collective-permute-done((bf16[3,192,128]{2,1,0:T(8,128)(2,1)S(1)}, bf16[3,192,128]{2,1,0:T(8,128)(2,1)S(1)}, u32[]{:S(2)}, u32[]{:S(2)}) %collective-permute-start.12) | collective-permute-done | bytes 147488 | tf_op jit(solution)/shard_map/ppermute | solution.py:551
  23.0 0.7 %shard_map.99 = (bf16[1,1,2,1,192,128]{5,4,3,2,1,0:T(8,128)(2,1)}, bf16[1,1,2,1,192,128]{5,4,3,2,1,0:T(8,128)(2,1)}, bf16[1,1,2,1,192,128]{5,4,3,2,1,0:T(8,128)(2,1)}) custom-call(bf16[2,192,128]{2,1,0:T(8,128)(2,1)S(1)} %shard_map.97.mine_ref, bf16[3,192,128]{2,1,0:T(8,128)(2,1)S(1)} %collective-permute-done.12.swap_ref, ...), custom_call_target="tpu_custom_call" | custom-call | tf_op jit(solution)/shard_map/pallas_call | solution.py:644
  (17 shorter events, 0.6 us)
Async XLA Ops:
  1.8 4.5 %collective-permute-start = (bf16[976,128]{1,0:T(8,128)(2,1)S(1)}, bf16[976,128]{1,0:T(8,128)(2,1)S(1)}, u32[]{:S(2)}, u32[]{:S(2)}) collective-permute-start(bf16[976,128]{1,0:T(8,128)(2,1)S(1)} %get-tuple-element.41), channel_id=1, source_target_pairs={{0,8},{8,0},{16,24},{24,16},{1,9},{9,1},{17,25},{25,17},{2,10},{10... | collective-permute-start | bytes 749576 | tf_op jit(solution)/shard_map/ppermute | solution.py:551
  2.3 7.8 %collective-permute-start.1 = (bf16[440,128]{1,0:T(8,128)(2,1)S(1)}, bf16[440,128]{1,0:T(8,128)(2,1)S(1)}, u32[]{:S(2)}, u32[]{:S(2)}) collective-permute-start(bf16[440,128]{1,0:T(8,128)(2,1)S(1)} %get-tuple-element.39.kv_ref.refs_1_.refs_0_), channel_id=1, source_target_pairs={{0,8},{2,12},{4,10},{6,14},{8,0},{10,4},{12,2},{14,6},{16,24},{18,... | collective-permute-start | bytes 337928 | tf_op jit(solution)/shard_map/ppermute | solution.py:548
  2.4 7.8 %collective-permute-start.2 = (bf16[440,128]{1,0:T(8,128)(2,1)S(1)}, bf16[440,128]{1,0:T(8,128)(2,1)S(1)}, u32[]{:S(2)}, u32[]{:S(2)}) collective-permute-start(bf16[440,128]{1,0:T(8,128)(2,1)S(1)} %get-tuple-element.39.kv_ref.refs_1_.refs_0_), channel_id=1, source_target_pairs={{0,10},{2,8},{4,14},{6,12},{8,2},{10,0},{12,6},{14,4},{16,26},{18,... | collective-permute-start | bytes 337928 | tf_op jit(solution)/shard_map/ppermute | solution.py:548
  6.4 4.9 %collective-permute-start.3 = (bf16[432,128]{1,0:T(8,128)(2,1)S(1)}, bf16[432,128]{1,0:T(8,128)(2,1)S(1)}, u32[]{:S(2)}, u32[]{:S(2)}) collective-permute-start(bf16[432,128]{1,0:T(8,128)(2,1)S(1)} %get-tuple-element.51), channel_id=1, source_target_pairs={{0,24},{2,26},{4,28},{6,30},{8,16},{10,18},{12,20},{14,22},{16,8},... | collective-permute-start | bytes 331784 | tf_op jit(solution)/shard_map/ppermute | solution.py:548
  8.1 4.4 %collective-permute-start.4 = (bf16[416,128]{1,0:T(8,128)(2,1)S(1)}, bf16[416,128]{1,0:T(8,128)(2,1)S(1)}, u32[]{:S(2)}, u32[]{:S(2)}) collective-permute-start(bf16[416,128]{1,0:T(8,128)(2,1)S(1)} %get-tuple-element.42.par_kv_ref.refs_2_.refs_1_), channel_id=1, source_target_pairs={{0,8},{2,12},{4,10},{6,14},{8,0},{10,4},{12,2},{14,6},{16,24},{18,... | collective-permute-start | bytes 319496 | tf_op jit(solution)/shard_map/ppermute | solution.py:548
  8.1 4.7 %collective-permute-start.5 = (bf16[416,128]{1,0:T(8,128)(2,1)S(1)}, bf16[416,128]{1,0:T(8,128)(2,1)S(1)}, u32[]{:S(2)}, u32[]{:S(2)}) collective-permute-start(bf16[416,128]{1,0:T(8,128)(2,1)S(1)} %get-tuple-element.42.par_kv_ref.refs_2_.refs_1_), channel_id=1, source_target_pairs={{0,10},{2,8},{4,14},{6,12},{8,2},{10,0},{12,6},{14,4},{16,26},{18,... | collective-permute-start | bytes 319496 | tf_op jit(solution)/shard_map/ppermute | solution.py:548
  11.3 8.6 %collective-permute-start.7 = (bf16[1168,128]{1,0:T(8,128)(2,1)S(1)}, bf16[1168,128]{1,0:T(8,128)(2,1)S(1)}, u32[]{:S(2)}, u32[]{:S(2)}) collective-permute-start(bf16[1168,128]{1,0:T(8,128)(2,1)S(1)} %shard_map.93), channel_id=1, source_target_pairs={{0,10},{2,8},{4,14},{6,12},{8,2},{10,0},{12,6},{14,4},{16,26},{18,... | collective-permute-start | bytes 897032 | tf_op jit(solution)/shard_map/ppermute | solution.py:548
  12.3 8.6 %collective-permute-start.9 = (bf16[1168,128]{1,0:T(8,128)(2,1)S(1)}, bf16[1168,128]{1,0:T(8,128)(2,1)S(1)}, u32[]{:S(2)}, u32[]{:S(2)}) collective-permute-start(bf16[1168,128]{1,0:T(8,128)(2,1)S(1)} %shard_map.93), channel_id=1, source_target_pairs={{0,8},{2,12},{4,10},{6,14},{8,0},{10,4},{12,2},{14,6},{16,24},{18,... | collective-permute-start | bytes 897032 | tf_op jit(solution)/shard_map/ppermute | solution.py:548
  13.4 3.2 %collective-permute-start.6 = (f32[8,384]{1,0:T(8,128)S(1)}, f32[8,384]{1,0:T(8,128)S(1)}, u32[]{:S(2)}, u32[]{:S(2)}) collective-permute-start(f32[8,384]{1,0:T(8,128)S(1)} %get-tuple-element.54.refs_7_.refs_0_), channel_id=1, source_target_pairs={{0,24},{2,26},{4,28},{6,30},{8,16},{10,18},{12,20},{14,22},{16,8},... | collective-permute-start | bytes 36872 | tf_op jit(solution)/shard_map/ppermute | solution.py:548
  16.0 4.9 %collective-permute-start.11 = (bf16[192,128]{1,0:T(8,128)(2,1)S(1)}, bf16[192,128]{1,0:T(8,128)(2,1)S(1)}, u32[]{:S(2)}, u32[]{:S(2)}) collective-permute-start(bf16[192,128]{1,0:T(8,128)(2,1)S(1)} %get-tuple-element.72), channel_id=1, source_target_pairs={{0,24},{2,26},{4,28},{6,30},{8,16},{10,18},{12,20},{14,22},{16,8},... | collective-permute-start | bytes 147464 | tf_op jit(solution)/shard_map/ppermute | solution.py:548
  16.6 3.8 %collective-permute-start.8 = (f32[8,384]{1,0:T(8,128)S(1)}, f32[8,384]{1,0:T(8,128)S(1)}, u32[]{:S(2)}, u32[]{:S(2)}) collective-permute-start(f32[8,384]{1,0:T(8,128)S(1)} %shard_map.91.note), channel_id=1, source_target_pairs={{0,10},{2,8},{4,14},{6,12},{8,2},{10,0},{12,6},{14,4},{16,26},{18,... | collective-permute-start | bytes 36872 | tf_op jit(solution)/shard_map/ppermute | solution.py:548
  18.8 2.1 %collective-permute-start.10 = (f32[8,384]{1,0:T(8,128)S(1)}, f32[8,384]{1,0:T(8,128)S(1)}, u32[]{:S(2)}, u32[]{:S(2)}) collective-permute-start(f32[8,384]{1,0:T(8,128)S(1)} %shard_map.91.note), channel_id=1, source_target_pairs={{0,8},{2,12},{4,10},{6,14},{8,0},{10,4},{12,2},{14,6},{16,24},{18,... | collective-permute-start | bytes 36872 | tf_op jit(solution)/shard_map/ppermute | solution.py:548
  21.1 1.9 %collective-permute-start.12 = (bf16[3,192,128]{2,1,0:T(8,128)(2,1)S(1)}, bf16[3,192,128]{2,1,0:T(8,128)(2,1)S(1)}, u32[]{:S(2)}, u32[]{:S(2)}) collective-permute-start(bf16[3,192,128]{2,1,0:T(8,128)(2,1)S(1)} %get-tuple-element.73), channel_id=1, source_target_pairs={{0,8},{8,0},{16,24},{24,16},{1,9},{9,1},{17,25},{25,17},{2,10},{10... | collective-permute-start | bytes 442376 | tf_op jit(solution)/shard_map/ppermute | solution.py:551
